TPU v7x, 32 devices: a whole 2x2x4 slice. The times are simulated.
32 devices in a mesh: dp: 8 (over z, y), mp: 4 (over x, core).
Axes of the slice: x: 2, y: 2, z: 4, core: 2. Of those that a mesh axis runs over, the one named last changes fastest.
Arguments:
- tokens: bfloat16 [8192, 2048], P(('dp', 'mp')), may hold values from -6 to 6
- cotangent: bfloat16 [8192, 2048], P(('dp', 'mp')), may hold values from -6 to 6
- qkv_weight: float32 [3, 2048, 2048], P(None, 'dp', 'mp'), may hold values from -0.1875 to 0.1875
- qkv_first: float32 [3, 2048, 2048], P(None, 'dp', 'mp'), may hold values from -64 to 64
- qkv_second: float32 [3, 2048, 2048], P(None, 'dp', 'mp'), may hold values from 4.096 to 65.536
- dense_weight: float32 [2048, 2048], P('mp', 'dp'), may hold values from -0.5 to 0.5
- dense_first: float32 [2048, 2048], P('mp', 'dp'), may hold values from -16 to 16
- dense_second: float32 [2048, 2048], P('mp', 'dp'), may hold values from 0.36864 to 5.89824
- up_weight: float32 [2048, 8192], P('dp', 'mp'), may hold values from -0.125 to 0.125
- up_first: float32 [2048, 8192], P('dp', 'mp'), may hold values from -16 to 16
- up_second: float32 [2048, 8192], P('dp', 'mp'), may hold values from 0.24576 to 4.096
- down_weight: float32 [8192, 2048], P('mp', 'dp'), may hold values from -0.0625 to 0.0625
- down_first: float32 [8192, 2048], P('mp', 'dp'), may hold values from -32 to 32
- down_second: float32 [8192, 2048], P('mp', 'dp'), may hold values from 1.47456 to 23.7568
- head_bias: float32 [3, 2048], P(None, 'mp'), may hold values from -0.625 to 0.625
- head_first: float32 [3, 2048], P(None, 'mp'), may hold values from -48 to 48
- head_second: float32 [3, 2048], P(None, 'mp'), may hold values from 2.62144 to 41.7792
- hidden_bias: float32 [8192], P('mp'), may hold values from -0.625 to 0.625
- hidden_first: float32 [8192], P('mp'), may hold values from -16 to 16
- hidden_second: float32 [8192], P('mp'), may hold values from 0.24576 to 4.096
- outer_params: float32 [4, 2048], replicated, may hold values from -0.4 to 1.5, as said below
- outer_first: float32 [4, 2048], replicated, may hold values from -96 to 96
- outer_second: float32 [4, 2048], replicated, may hold values from 9.0112 to 147.456
Outputs:
- layer_out: bfloat16 [8192, 2048], P(('dp', 'mp'))
- input_grad: float32 [8192, 2048], P(('dp', 'mp'))
- new_qkv: float32 [3, 2048, 2048], P(None, 'dp', 'mp')
- new_qkv_first: float32 [3, 2048, 2048], P(None, 'dp', 'mp')
- new_qkv_second: float32 [3, 2048, 2048], P(None, 'dp', 'mp')
- new_dense: float32 [2048, 2048], P('mp', 'dp')
- new_dense_first: float32 [2048, 2048], P('mp', 'dp')
- new_dense_second: float32 [2048, 2048], P('mp', 'dp')
- new_up: float32 [2048, 8192], P('dp', 'mp')
- new_up_first: float32 [2048, 8192], P('dp', 'mp')
- new_up_second: float32 [2048, 8192], P('dp', 'mp')
- new_down: float32 [8192, 2048], P('mp', 'dp')
- new_down_first: float32 [8192, 2048], P('mp', 'dp')
- new_down_second: float32 [8192, 2048], P('mp', 'dp')
- new_head_bias: float32 [3, 2048], P(None, 'mp')
- new_head_first: float32 [3, 2048], P(None, 'mp')
- new_head_second: float32 [3, 2048], P(None, 'mp')
- new_hidden_bias: float32 [8192], P('mp')
- new_hidden_first: float32 [8192], P('mp')
- new_hidden_second: float32 [8192], P('mp')
- new_outer: float32 [4, 2048], replicated
- new_outer_first: float32 [4, 2048], replicated
- new_outer_second: float32 [4, 2048], replicated
Inputs may be any that keep to these rules, and one draw needn't show every extreme that they name: `outer_params`: row 0, the norm's gain, lies between 0.5 and 1.5; rows 1 to 3 lie between -0.4 and 0.4.
All inputs are finite; a program needn't handle non-finite values.
Results may differ from a plain program's by a relative error of at most 0.0045.
The roundings to bfloat16 on the way count: a program that leaves them out, or rounds other values in their place, can miss the bound.
Values may be sent and summed in bfloat16 or wider, within the bound.
A program may use at most 136 MiB of HBM per device.

v0:
```python
from functools import partial
import math

import jax
import jax.numpy as jnp
from jax import lax
from jax.sharding import PartitionSpec as P

D = 2048
FF = 8192
HEAD = 64
ROT = 32
STEP = 10


BETA_ONE = 0.9
BETA_TWO = 0.999
ADAM_EPS = 1e-08
MATRIX_DECAY = 0.1
VECTOR_RATE = 0.1


def normalize(inputs, scales, offsets):
    average = jnp.mean(inputs, axis=-1, keepdims=True)
    centred = inputs - average
    variance = jnp.mean(centred * centred, axis=-1, keepdims=True)
    return centred * lax.rsqrt(variance + 1e-05) * scales + offsets


def rotation(positions):
    exponent = jnp.arange(ROT // 2, dtype=jnp.float32) * (2.0 / ROT)
    inverse = jnp.exp(-math.log(10000.0) * exponent)
    angles = positions[:, None] * inverse[None, :]
    return (jnp.cos(angles)[:, None, :], jnp.sin(angles)[:, None, :])


def rotate(pieces, cos_table, sin_table):
    first_half = pieces[..., : ROT // 2]
    second_half = pieces[..., ROT // 2 : ROT]
    return jnp.concatenate(
        [
            first_half * cos_table - second_half * sin_table,
            second_half * cos_table + first_half * sin_table,
            pieces[..., ROT:],
        ],
        axis=-1,
    )


def gelu_tanh(values):
    return jax.nn.gelu(values, approximate=True)


def masked_scores(query_rows, first_row, key_rows):
    scores = jnp.einsum(
        "qhd,khd->hqk", query_rows, key_rows, preferred_element_type=jnp.float32
    ) * HEAD ** (-0.5)
    query_index = first_row + lax.iota(jnp.int32, query_rows.shape[0])
    key_index = lax.iota(jnp.int32, key_rows.shape[0])
    allowed = key_index[None, :] <= query_index[:, None]
    return jnp.where(allowed[None], scores, -1e30)


def attend_block(query_rows, first_row, key_rows, value_rows):
    scores = masked_scores(query_rows, first_row, key_rows)
    row_max = jnp.max(scores, axis=-1, keepdims=True)
    shifted_exp = jnp.exp(scores - row_max)
    row_total = jnp.sum(shifted_exp, axis=-1, keepdims=True)
    weights_low = (shifted_exp / row_total).astype(jnp.bfloat16)
    mixed_rows = jnp.einsum(
        "hqk,khd->qhd", weights_low, value_rows, preferred_element_type=jnp.float32
    )
    return (mixed_rows.astype(jnp.bfloat16), (row_max + jnp.log(row_total))[..., 0])


def adam_update(weight, moment_one, moment_two, gradient, step_rate, decay_rate):
    first_new = BETA_ONE * moment_one + (1.0 - BETA_ONE) * gradient
    second_new = BETA_TWO * moment_two + (1.0 - BETA_TWO) * gradient * gradient
    normalized = (
        first_new
        / (1.0 - BETA_ONE**STEP)
        / (jnp.sqrt(second_new / (1.0 - BETA_TWO**STEP)) + ADAM_EPS)
    )
    return (weight - step_rate * (normalized + decay_rate * weight), first_new, second_new)


def local(
    tokens,
    cotangent,
    qkv_weight,
    qkv_first,
    qkv_second,
    dense_weight,
    dense_first,
    dense_second,
    up_weight,
    up_first,
    up_second,
    down_weight,
    down_first,
    down_second,
    head_bias,
    head_first,
    head_second,
    hidden_bias,
    hidden_first,
    hidden_second,
    outer_params,
    outer_first,
    outer_second,
):
    tok_rows = tokens.shape[0]
    seq_rows = tok_rows * lax.axis_size("mp")
    local_width = qkv_weight.shape[2]
    local_heads = local_width // HEAD
    block_rows = min(512, seq_rows)
    block_count = seq_rows // block_rows
    score_scale = HEAD ** (-0.5)
    tokens_wide = tokens.astype(jnp.float32)
    normed, norm_back = jax.vjp(normalize, tokens_wide, outer_params[0], outer_params[1])
    whole = lax.all_gather(normed.astype(jnp.bfloat16), "mp", axis=0, tiled=True)
    lowered = (
        qkv_weight.astype(jnp.bfloat16),
        dense_weight.astype(jnp.bfloat16),
        up_weight.astype(jnp.bfloat16),
        down_weight.astype(jnp.bfloat16),
    )
    qkv_full, dense_full, up_full, down_full = (
        lax.all_gather(lowered[0], "dp", axis=1, tiled=True),
        lax.all_gather(lowered[1], "dp", axis=1, tiled=True),
        lax.all_gather(lowered[2], "dp", axis=0, tiled=True),
        lax.all_gather(lowered[3], "dp", axis=1, tiled=True),
    )
    projected = (
        jnp.einsum("sd,tde->tse", whole, qkv_full, preferred_element_type=jnp.float32)
        + head_bias[:, None, :]
    )
    separated = projected.reshape(3, seq_rows, local_heads, HEAD)
    cos_table, sin_table = rotation(jnp.arange(seq_rows, dtype=jnp.float32))
    turned_pair, turn_back = jax.vjp(
        partial(rotate, cos_table=cos_table, sin_table=sin_table), separated[:2]
    )
    turned = jnp.concatenate([turned_pair, separated[2:]], axis=0).astype(jnp.bfloat16)
    queries = turned[0]
    key_rows = turned[1]
    values = turned[2]
    block_starts = jnp.arange(block_count, dtype=jnp.int32) * block_rows
    query_blocks = queries.reshape(block_count, block_rows, local_heads, HEAD)

    def forward_block(element):
        return attend_block(element[0], element[1], key_rows, values)

    mixed_blocks, log_totals = lax.map(forward_block, (query_blocks, block_starts))
    mixed = mixed_blocks.reshape(seq_rows, local_width)
    hidden = jnp.dot(whole, up_full, preferred_element_type=jnp.float32) + hidden_bias
    activated, gelu_back = jax.vjp(gelu_tanh, hidden)
    act_low = activated.astype(jnp.bfloat16)
    branch = lax.psum_scatter(
        jnp.dot(mixed, dense_full, preferred_element_type=jnp.float32)
        + jnp.dot(act_low, down_full, preferred_element_type=jnp.float32),
        "mp",
        scatter_dimension=0,
        tiled=True,
    )
    layer_out = (tokens_wide + branch + outer_params[2] + outer_params[3]).astype(jnp.bfloat16)
    back_all = lax.all_gather(cotangent, "mp", axis=0, tiled=True)
    qkv_back, dense_back, up_back, down_back = (
        lax.all_gather(lowered[0], "dp", axis=1, tiled=True),
        lax.all_gather(lowered[1], "dp", axis=1, tiled=True),
        lax.all_gather(lowered[2], "dp", axis=0, tiled=True),
        lax.all_gather(lowered[3], "dp", axis=1, tiled=True),
    )
    grad_dense = jnp.einsum("sk,sd->kd", mixed, back_all, preferred_element_type=jnp.float32)
    grad_down = jnp.einsum("sf,sd->fd", act_low, back_all, preferred_element_type=jnp.float32)
    grad_mixed = jnp.einsum(
        "sd,kd->sk", back_all, dense_back, preferred_element_type=jnp.float32
    ).astype(jnp.bfloat16)
    grad_act = jnp.einsum("sd,fd->sf", back_all, down_back, preferred_element_type=jnp.float32)
    grad_hidden = gelu_back(grad_act)[0].astype(jnp.bfloat16)
    grad_up = jnp.einsum("sd,sf->df", whole, grad_hidden, preferred_element_type=jnp.float32)
    hidden_grad = jnp.sum(grad_hidden.astype(jnp.float32), axis=0)

    def backward_block(carry, element):
        key_total, value_total = carry
        query_rows, first_row, log_block, grad_out = element
        scores = masked_scores(query_rows, first_row, key_rows)
        probs = jnp.exp(scores - log_block[..., None])
        probs_low = probs.astype(jnp.bfloat16)
        value_total = value_total + jnp.einsum(
            "hqk,qhd->khd", probs_low, grad_out, preferred_element_type=jnp.float32
        )
        grad_probs = jnp.einsum(
            "qhd,khd->hqk", grad_out, values, preferred_element_type=jnp.float32
        )
        row_inner = jnp.sum(probs * grad_probs, axis=-1, keepdims=True)
        grad_scores = (probs * (grad_probs - row_inner)).astype(jnp.bfloat16)
        grad_query = (
            jnp.einsum("hqk,khd->qhd", grad_scores, key_rows, preferred_element_type=jnp.float32)
            * score_scale
        )
        key_total = (
            key_total
            + jnp.einsum(
                "hqk,qhd->khd", grad_scores, query_rows, preferred_element_type=jnp.float32
            )
            * score_scale
        )
        return ((key_total, value_total), grad_query)

    zero_keys = jnp.zeros((seq_rows, local_heads, HEAD), jnp.float32)
    grad_blocks = grad_mixed.reshape(block_count, block_rows, local_heads, HEAD)
    (key_grad, value_grad), query_grad = lax.scan(
        backward_block,
        (zero_keys, zero_keys),
        (query_blocks, block_starts, log_totals, grad_blocks),
    )
    pair_grad = turn_back(jnp.stack([query_grad.reshape(seq_rows, local_heads, HEAD), key_grad]))[0]
    grad_projected = (
        jnp.concatenate([pair_grad, value_grad[None]], axis=0)
        .reshape(3, seq_rows, local_width)
        .astype(jnp.bfloat16)
    )
    grad_qkv = jnp.einsum("sd,tse->tde", whole, grad_projected, preferred_element_type=jnp.float32)
    head_grad = jnp.sum(grad_projected.astype(jnp.float32), axis=1)
    qkv_sum, dense_sum, up_sum, down_sum = (
        lax.psum_scatter(grad_qkv, "dp", scatter_dimension=1, tiled=True),
        lax.psum_scatter(grad_dense, "dp", scatter_dimension=1, tiled=True),
        lax.psum_scatter(grad_up, "dp", scatter_dimension=0, tiled=True),
        lax.psum_scatter(grad_down, "dp", scatter_dimension=1, tiled=True),
    )
    grad_normed = lax.psum_scatter(
        jnp.einsum("tse,tde->sd", grad_projected, qkv_back, preferred_element_type=jnp.float32)
        + jnp.einsum("sf,df->sd", grad_hidden, up_back, preferred_element_type=jnp.float32),
        "mp",
        scatter_dimension=0,
        tiled=True,
    )
    input_part, gain_grad, shift_grad = norm_back(grad_normed)
    back_wide = cotangent.astype(jnp.float32)
    input_grad = back_wide + input_part
    out_bias_grad = jnp.sum(back_wide, axis=0)
    outer_sum = lax.psum(
        jnp.stack([gain_grad, shift_grad, out_bias_grad, out_bias_grad]), ("dp", "mp")
    )
    head_sum, hidden_sum = lax.psum((head_grad, hidden_grad), "dp")
    new_qkv, new_qkv_first, new_qkv_second = adam_update(
        qkv_weight, qkv_first, qkv_second, qkv_sum, (D // 2) ** (-0.5), MATRIX_DECAY
    )
    new_dense, new_dense_first, new_dense_second = adam_update(
        dense_weight, dense_first, dense_second, dense_sum, (D // 16) ** (-0.5), MATRIX_DECAY
    )
    new_up, new_up_first, new_up_second = adam_update(
        up_weight, up_first, up_second, up_sum, D ** (-0.5), MATRIX_DECAY
    )
    new_down, new_down_first, new_down_second = adam_update(
        down_weight, down_first, down_second, down_sum, FF ** (-0.5), MATRIX_DECAY
    )
    new_head_bias, new_head_first, new_head_second = adam_update(
        head_bias, head_first, head_second, head_sum, VECTOR_RATE, 0.0
    )
    new_hidden_bias, new_hidden_first, new_hidden_second = adam_update(
        hidden_bias, hidden_first, hidden_second, hidden_sum, VECTOR_RATE, 0.0
    )
    new_outer, new_outer_first, new_outer_second = adam_update(
        outer_params, outer_first, outer_second, outer_sum, VECTOR_RATE, 0.0
    )
    return (
        layer_out,
        input_grad,
        new_qkv,
        new_qkv_first,
        new_qkv_second,
        new_dense,
        new_dense_first,
        new_dense_second,
        new_up,
        new_up_first,
        new_up_second,
        new_down,
        new_down_first,
        new_down_second,
        new_head_bias,
        new_head_first,
        new_head_second,
        new_hidden_bias,
        new_hidden_first,
        new_hidden_second,
        new_outer,
        new_outer_first,
        new_outer_second,
    )


def solution(mesh):
    in_specs = (
        P(("dp", "mp"), None),
        P(("dp", "mp"), None),
        P(None, "dp", "mp"),
        P(None, "dp", "mp"),
        P(None, "dp", "mp"),
        P("mp", "dp"),
        P("mp", "dp"),
        P("mp", "dp"),
        P("dp", "mp"),
        P("dp", "mp"),
        P("dp", "mp"),
        P("mp", "dp"),
        P("mp", "dp"),
        P("mp", "dp"),
        P(None, "mp"),
        P(None, "mp"),
        P(None, "mp"),
        P("mp"),
        P("mp"),
        P("mp"),
        P(),
        P(),
        P(),
    )
    out_specs = (
        P(("dp", "mp"), None),
        P(("dp", "mp"), None),
        P(None, "dp", "mp"),
        P(None, "dp", "mp"),
        P(None, "dp", "mp"),
        P("mp", "dp"),
        P("mp", "dp"),
        P("mp", "dp"),
        P("dp", "mp"),
        P("dp", "mp"),
        P("dp", "mp"),
        P("mp", "dp"),
        P("mp", "dp"),
        P("mp", "dp"),
        P(None, "mp"),
        P(None, "mp"),
        P(None, "mp"),
        P("mp"),
        P("mp"),
        P("mp"),
        P(),
        P(),
        P(),
    )
    return jax.shard_map(local, mesh=mesh, in_specs=in_specs, out_specs=out_specs, check_vma=False)
```

profile of v0, /device:TPU:0, one launch (start us, length us, event | category | flops | bytes accessed | tf_op | source)
XLA Modules:
  0.0 1585.9 jit_solution(12064014862108651117)
XLA Ops:
  13.2 2.7 fusion.49
  18.6 34.5 %all-gather.7.cloned.1.call-done = bf16[1024,2048]{1,0:T(8,128)(2,1)} async-done(((bf16[256,2048]{1,0:T(8,128)(2,1)}), bf16[1024,2048]{1,0:T(8,128)(2,1)}) %all-gather.7.cloned.1.call-update) | async-done | bytes 4194320 | tf_op jit(solution)/shard_map/all_gather | solution.py:121
  53.2 102.6 %all-gather.9.cloned.1.call-done = bf16[3,2048,512]{1,2,0:T(8,128)(2,1)} async-done(((bf16[3,256,512]{1,2,0:T(8,128)(2,1)}), bf16[3,2048,512]{1,2,0:T(8,128)(2,1)}) %all-gather.9.cloned.1.call-update) | async-done | bytes 6291472 | tf_op jit(solution)/shard_map/all_gather | solution.py:129
  155.8 10.1 add_bitcast_fusion
  170.6 34.0 %while.27 = (s32[]{:T(128)}, bf16[2,512,8,64]{1,3,2,0:T(8,128)(2,1)}, f32[2,8,512]{2,1,0:T(8,128)S(1)}, s32[2]{0:T(128)S(1)}, bf16[2,512,8,64]{1,3,2,0:T(8,128)(...) while((s32[]{:T(128)}, bf16[2,512,8,64]{1,3,2,0:T(8,128)(2,1)}, ...), condition=%wide.region_5.6_spmd, body=%wide.region_2.5_spmd.sunk | while | flops 1124856320 | bytes 64098480 | solution.py:153
  172.2 4.2 fusion.129
  176.4 4.2 fusion.130
  180.6 5.9 fusion.131
  189.1 4.1 fusion.129
  193.3 4.2 fusion.130
  197.5 5.9 fusion.131
  204.6 2.3 copy.63
  208.1 6.6 fusion.84
  217.5 84.1 %reduce-scatter.13.cloned.1.call-done = f32[512,256]{1,0:T(8,128)} async-done(((f32[512,2048]{1,0:T(8,128)}), f32[512,256]{1,0:T(8,128)}) %reduce-scatter.13.cloned.1.call-update) | async-done | bytes 524304 | tf_op jit(solution)/shard_map/reduce_scatter | solution.py:227
  301.5 3.1 multiply_subtract_fusion.3
  304.8 124.3 %all-gather.13.cloned.1.call-done = bf16[2048,2048]{1,0:T(8,128)(2,1)} async-done(((bf16[256,2048]{1,0:T(8,128)(2,1)}), bf16[2048,2048]{1,0:T(8,128)(2,1)}) %all-gather.13.cloned.1.call-update) | async-done | bytes 8388624 | tf_op jit(solution)/shard_map/all_gather | solution.py:131
  429.0 12.6 fusion.82
  441.6 3.2 copy-done.49
  444.9 12.8 fusion.71
  457.8 23.2 %all-gather.11.cloned.1.call-done = bf16[512,2048]{1,0:T(8,128)(2,1)} async-done(((bf16[512,256]{1,0:T(8,128)(2,1)}), bf16[512,2048]{1,0:T(8,128)(2,1)}) %all-gather.11.cloned.1.call-update) | async-done | bytes 2097168 | tf_op jit(solution)/shard_map/all_gather | solution.py:130
  481.0 6.2 convolution_convert_fusion
  487.2 2.8 reshape.222
  490.0 2.2 copy.66
  492.2 274.0 %reduce-scatter.17.cloned.1.call-done = f32[2048,256]{1,0:T(8,128)} async-done(((f32[2048,2048]{1,0:T(8,128)}), f32[2048,256]{1,0:T(8,128)}) %reduce-scatter.17.cloned.1.call-update) | async-done | bytes 2097168 | tf_op jit(solution)/shard_map/reduce_scatter | solution.py:229
  766.2 8.1 multiply_subtract_fusion
  774.4 128.9 %while.28 = (s32[]{:T(128)}, f32[1024,8,64]{0,2,1:T(8,128)}, f32[1024,8,64]{0,2,1:T(8,128)}, f32[2,512,8,64]{1,0,3,2:T(2,128)}, bf16[2,512,8,64]{1,3,2,0:T(8,128...) while((s32[]{:T(128)}, f32[1024,8,64]{0,2,1:T(8,128)}, ...), condition=%wide.region_9.10_spmd.clone, body=%wide.region_7.9_spmd.clone.sunk | while | flops 2725507584 | bytes 200626512 | solution.py:212
  777.9 3.8 fusion.141
  781.6 11.5 multiply_reduce_fusion.2
  793.2 9.5 multiply_convert_fusion.5
  802.7 8.9 bitcast_add_fusion.6
  811.6 2.7 fusion.142
  814.3 2.9 bitcast_add_fusion.5
  819.2 19.7 %dynamic_update_slice.20 = f32[2,512,8,64]{1,0,3,2:T(2,128)} dynamic-update-slice(f32[2,512,8,64]{1,0,3,2:T(2,128)} %get-tuple-element.467, f32[1,512,8,64]{1,0,3,2:T(1,128)} %copy.99, s32[]{:T(128)S(6)} %copy.116, s32[]{:T(128)} %constant.51.clone.1..sunk, s32[]{:T(128)} %constant.51.clone.1..sunk, s32[]{:T(128)} %constant.51.clone.1..sunk) | dynamic-update-slice | bytes 2097156 | tf_op jit(solution)/shard_map/while/body/jit(dynamic_update_index_in_dim)/dynamic_update_slice | solution.py:212
  841.9 3.8 fusion.141
  845.7 11.5 multiply_reduce_fusion.2
  857.2 9.4 multiply_convert_fusion.5
  866.6 9.4 bitcast_add_fusion.6
  876.1 2.7 fusion.142
  878.7 2.9 bitcast_add_fusion.5
  883.7 19.6 %dynamic_update_slice.20 = f32[2,512,8,64]{1,0,3,2:T(2,128)} dynamic-update-slice(f32[2,512,8,64]{1,0,3,2:T(2,128)} %get-tuple-element.467, f32[1,512,8,64]{1,0,3,2:T(1,128)} %copy.99, s32[]{:T(128)S(6)} %copy.116, s32[]{:T(128)} %constant.51.clone.1..sunk, s32[]{:T(128)} %constant.51.clone.1..sunk, s32[]{:T(128)} %constant.51.clone.1..sunk) | dynamic-update-slice | bytes 2097156 | tf_op jit(solution)/shard_map/while/body/jit(dynamic_update_index_in_dim)/dynamic_update_slice | solution.py:212
  903.3 4.2 stack_reshape.3
  907.5 2.9 convert.29
  915.0 2.6 copy.68
  917.6 12.1 convolution_bitcast_fusion
  930.4 18.6 %convert_reduce_fusion = (f32[2048]{0:T(1024)S(1)}, bf16[1024,2048]{1,0:T(8,128)(2,1)S(1)}) fusion(f32[1024,2048]{1,0:T(8,128)} %copy-done.49, f32[2048]{0:T(1024)S(1)} %copy-done.45, bf16[1024,2048]{1,0:T(8,128)(2,1)} %all-gather.17.cloned.1.call-done, bf16[2048,2048]{1,0:T(8,128)(2,1)} %all-gather.15.cloned.1.call-done), kind=kOutput, calls=%fused_computation.53 | convolution fusion | flops 8638167040 | bytes 25182208 | tf_op jit(solution)/shard_map/sd,fd->sf/dot_general | solution.py:178
  949.0 12.8 fusion.83
  961.9 10.7 bitcast_add_fusion.2
  973.1 15.8 fusion.72
  988.9 5.7 convolution_add_fusion
  994.8 15.3 fusion.85
  1012.0 3.2 copy.73
  1015.2 2.4 convert_reduce_fusion.1
  1017.6 119.0 %reduce-scatter.11.cloned.1.call-done = f32[3,256,512]{1,2,0:T(8,128)} async-done(((f32[3,2048,512]{1,2,0:T(8,128)}), f32[3,256,512]{1,2,0:T(8,128)}) %reduce-scatter.11.cloned.1.call-update) | async-done | bytes 1572880 | tf_op jit(solution)/shard_map/reduce_scatter | solution.py:226
  1136.6 4.8 multiply_subtract_fusion.2
  1141.4 3.1 copy.76
  1144.6 3.2 copy.77
  1149.4 35.3 %all-reduce.3 = (f32[3,512]{1,0:T(4,128)S(1)}, f32[2048]{0:T(1024)S(1)}) all-reduce(f32[3,512]{1,0:T(4,128)S(1)} %convert_reduce_fusion.1, f32[2048]{0:T(1024)S(1)} %get-tuple-element.281), channel_id=1, replica_groups=mesh['dp'=8,'mp'=4] {'dp'}, use_global_device_ids=true, to_apply=%region_18.19 | all-reduce | flops 3584 | bytes 28672 | tf_op jit(solution)/shard_map/psum | solution.py:245
  1186.1 23.8 %reduce-scatter.9.cloned.1.call-done = f32[256,2048]{1,0:T(8,128)} async-done(((f32[1024,2048]{1,0:T(8,128)}), f32[256,2048]{1,0:T(8,128)}) %reduce-scatter.9.cloned.1.call-update) | async-done | bytes 2097168 | tf_op jit(solution)/shard_map/reduce_scatter | solution.py:231
  1209.9 2.2 fusion.52
  1213.2 71.2 %reduce-scatter.7.cloned.1.call-done = f32[256,2048]{1,0:T(8,128)} async-done(((f32[1024,2048]{1,0:T(8,128)}), f32[256,2048]{1,0:T(8,128)}) %reduce-scatter.7.cloned.1.call-update) | async-done | bytes 2097168 | tf_op jit(solution)/shard_map/reduce_scatter | solution.py:158
  1284.4 5.1 convert_reduce_fusion.3
  1289.6 43.0 %psum.23 = f32[4,2048]{1,0:T(4,128)S(1)} all-reduce(f32[4,2048]{1,0:T(4,128)S(1)} %pad_maximum_fusion.5), channel_id=1, replica_groups=mesh['dp'=8,'mp'=4] {'dp','mp'}, use_global_device_ids=true, to_apply=%region_24.25 | all-reduce | flops 8192 | bytes 65536 | tf_op jit(solution)/shard_map/psum | solution.py:242
  1333.3 238.0 %reduce-scatter.15.cloned.1.call-done = f32[256,2048]{1,0:T(8,128)} async-done(((f32[2048,2048]{1,0:T(8,128)}), f32[256,2048]{1,0:T(8,128)}) %reduce-scatter.15.cloned.1.call-update) | async-done | bytes 2097168 | tf_op jit(solution)/shard_map/reduce_scatter | solution.py:228
  1571.3 7.5 multiply_subtract_fusion.1
  (200 shorter events, 45.2 us)
Async XLA Ops:
  7.2 8.7 copy-start.17
  7.2 46.0 %all-gather.7.cloned.1.call-start = ((), (), s32[]{:S(2)}) async-start(), calls=%async_computation.6 | async-start | bytes 5242880 | tf_op jit(solution)/shard_map/all_gather | solution.py:121
  8.8 3.8 copy-start.30
  11.0 1.6 copy-start.36
  15.8 139.9 %copy-start.40 = (f32[3,512]{1,0:T(4,128)S(1)}, f32[3,512]{1,0:T(4,128)}, u32[]{:S(2)}) copy-start(f32[3,512]{1,0:T(4,128)} %param.41) | copy-start | bytes 18436
  15.8 139.9 %all-gather.9.cloned.1.call-start = ((), (), s32[]{:S(2)}) async-start(), calls=%async_computation.7 | async-start | bytes 7077888 | tf_op jit(solution)/shard_map/all_gather | solution.py:129
  16.4 149.5 %copy-start.8 = (f32[3,256,512]{1,2,0:T(8,128)}, f32[3,256,512]{1,2,0:T(8,128)S(1)}, u32[]{:S(2)}) copy-start(f32[3,256,512]{1,2,0:T(8,128)S(1)} %copy.61) | copy-start | bytes 4718596
  17.5 189.7 %all-gather.17.cloned.1.call-start = ((), (), s32[]{:S(2)}) async-start(), calls=%async_computation.12 | async-start | bytes 5242880 | tf_op jit(solution)/shard_map/all_gather | solution.py:166
  18.2 283.3 %reduce-scatter.13.cloned.1.call-start = ((), (), s32[]{:S(2)}) async-start(), calls=%async_computation.15 | async-start | bytes 4718592 | tf_op jit(solution)/shard_map/reduce_scatter | solution.py:227
  18.6 149.1 %copy-start.19 = (f32[1024,16]{0,1:T(8,128)}, f32[1024,16]{0,1:T(8,128)S(1)}, u32[]{:S(2)}) copy-start(f32[1024,16]{0,1:T(8,128)S(1)} %get-tuple-element.314) | copy-start | bytes 196612
  18.6 149.1 %copy-start.21 = (f32[1024,16]{0,1:T(8,128)}, f32[1024,16]{0,1:T(8,128)S(1)}, u32[]{:S(2)}) copy-start(f32[1024,16]{0,1:T(8,128)S(1)} %get-tuple-element.315) | copy-start | bytes 196612
  176.3 4.3 copy-start.23
  193.3 4.3 copy-start.23
  214.7 1.6 copy-start.10
  214.7 214.3 %all-gather.13.cloned.1.call-start = ((), (), s32[]{:S(2)}) async-start(), calls=%async_computation.9 | async-start | bytes 9437184 | tf_op jit(solution)/shard_map/all_gather | solution.py:131
  217.4 263.5 %all-gather.11.cloned.1.call-start = ((), (), s32[]{:S(2)}) async-start(), calls=%async_computation.8 | async-start | bytes 2359296 | tf_op jit(solution)/shard_map/all_gather | solution.py:130
  304.7 140.2 %copy-start.44 = (f32[2048]{0:T(1024)S(1)}, f32[2048]{0:T(1024)}, u32[]{:S(2)}) copy-start(f32[2048]{0:T(1024)} %param.44) | copy-start | bytes 24580
  304.7 461.5 %reduce-scatter.17.cloned.1.call-start = ((), (), s32[]{:S(2)}) async-start(), calls=%async_computation.17 | async-start | bytes 18874368 | tf_op jit(solution)/shard_map/reduce_scatter | solution.py:229
  429.0 15.9 copy-start.48
  441.6 3.2 copy-start.49
  457.7 472.0 %all-gather.15.cloned.1.call-start = ((), (), s32[]{:S(2)}) async-start(), calls=%async_computation.10 | async-start | bytes 9437184 | tf_op jit(solution)/shard_map/all_gather | solution.py:132
  774.4 362.2 %reduce-scatter.11.cloned.1.call-start = ((), (), s32[]{:S(2)}) async-start(), calls=%async_computation.14 | async-start | bytes 14155776 | tf_op jit(solution)/shard_map/reduce_scatter | solution.py:226
  774.8 1.9 copy-start.25
  793.2 9.5 copy-start.4
  802.7 8.9 copy-start
  811.6 2.7 copy-start.1
  817.1 21.8 %copy-start.2 = (f32[1024,8,64]{0,2,1:T(8,128)}, f32[1024,8,64]{0,2,1:T(8,128)S(1)}, u32[]{:S(2)}) copy-start(f32[1024,8,64]{0,2,1:T(8,128)S(1)} %bitcast_add_fusion.5) | copy-start | bytes 6291460 | tf_op jit(solution)/shard_map/while
  817.2 21.8 %copy-start.26 = (f32[2,8,512]{2,1,0:T(8,128)S(1)}, f32[2,8,512]{2,1,0:T(8,128)}, u32[]{:S(2)}) copy-start(f32[2,8,512]{2,1,0:T(8,128)} %copy-done.25) | copy-start | bytes 98308 | tf_op jit(solution)/shard_map/while
  838.9 1.9 copy-start.25
  857.2 9.4 copy-start.4
  866.6 9.4 copy-start
  876.1 2.7 copy-start.1
  881.6 21.7 %copy-start.2 = (f32[1024,8,64]{0,2,1:T(8,128)}, f32[1024,8,64]{0,2,1:T(8,128)S(1)}, u32[]{:S(2)}) copy-start(f32[1024,8,64]{0,2,1:T(8,128)S(1)} %bitcast_add_fusion.5) | copy-start | bytes 6291460 | tf_op jit(solution)/shard_map/while
  881.6 21.7 %copy-start.26 = (f32[2,8,512]{2,1,0:T(8,128)S(1)}, f32[2,8,512]{2,1,0:T(8,128)}, u32[]{:S(2)}) copy-start(f32[2,8,512]{2,1,0:T(8,128)} %copy-done.25) | copy-start | bytes 98308 | tf_op jit(solution)/shard_map/while
  907.5 4.4 copy-start.3
  911.9 49.9 %copy-start.15 = (bf16[1,1024,512]{2,1,0:T(8,128)(2,1)}, bf16[1,1024,512]{2,1,0:T(8,128)(2,1)S(1)}, u32[]{:S(2)}) copy-start(bf16[1,1024,512]{2,1,0:T(8,128)(2,1)S(1)} %copy.69) | copy-start | bytes 3145732
  911.9 2.3 copy-start.6
  911.9 2.3 copy-start.20
  912.0 2.3 copy-start.22
  929.7 280.2 %reduce-scatter.9.cloned.1.call-start = ((), (), s32[]{:S(2)}) async-start(), calls=%async_computation.13 | async-start | bytes 10485760 | tf_op jit(solution)/shard_map/reduce_scatter | solution.py:231
  949.0 12.9 copy-start.50
  949.0 12.9 copy-start.11
  972.6 16.2 %copy-start.13 = (bf16[64,8,2,512]{3,1,2,0:T(8,128)(2,1)S(1)}, bf16[64,8,2,512]{3,1,2,0:T(8,128)(2,1)}, u32[]{:S(2)}) copy-start(bf16[64,8,2,512]{3,1,2,0:T(8,128)(2,1)} %copy-done.12) | copy-start | bytes 3145732
  972.6 16.2 %copy-start.16 = (bf16[512,2048]{1,0:T(8,128)(2,1)S(1)}, bf16[512,2048]{1,0:T(8,128)(2,1)}, u32[]{:S(2)}) copy-start(bf16[512,2048]{1,0:T(8,128)(2,1)} %all-gather.11.cloned.1.call-done) | copy-start | bytes 6291460
  972.6 311.8 %reduce-scatter.7.cloned.1.call-start = ((), (), s32[]{:S(2)}) async-start(), calls=%async_computation.11 | async-start | bytes 10485760 | tf_op jit(solution)/shard_map/reduce_scatter | solution.py:158
  994.6 576.7 %reduce-scatter.15.cloned.1.call-start = ((), (), s32[]{:S(2)}) async-start(), calls=%async_computation.16 | async-start | bytes 18874368 | tf_op jit(solution)/shard_map/reduce_scatter | solution.py:228
  1012.0 124.6 %copy-start.9 = (f32[3,256,512]{1,2,0:T(8,128)S(1)}, f32[3,256,512]{1,2,0:T(8,128)}, u32[]{:S(2)}) copy-start(f32[3,256,512]{1,2,0:T(8,128)} %copy-done.8) | copy-start | bytes 4718596
  1141.4 6.4 copy-start.14
  1144.6 40.2 %copy-start.41 = (f32[3,512]{1,0:T(4,128)S(1)}, f32[3,512]{1,0:T(4,128)}, u32[]{:S(2)}) copy-start(f32[3,512]{1,0:T(4,128)} %param.41) | copy-start | bytes 18436
  1144.6 40.2 %copy-start.42 = (f32[3,512]{1,0:T(4,128)S(1)}, f32[3,512]{1,0:T(4,128)}, u32[]{:S(2)}) copy-start(f32[3,512]{1,0:T(4,128)} %param.42) | copy-start | bytes 18436
  1144.6 40.2 %copy-start.43 = (f32[3,512]{1,0:T(4,128)S(1)}, f32[3,512]{1,0:T(4,128)}, u32[]{:S(2)}) copy-start(f32[3,512]{1,0:T(4,128)} %param.43) | copy-start | bytes 18436
  1144.6 40.9 %copy-start.46 = (f32[2048]{0:T(1024)S(1)}, f32[2048]{0:T(1024)}, u32[]{:S(2)}) copy-start(f32[2048]{0:T(1024)} %param.45) | copy-start | bytes 24580
  1144.6 40.9 %copy-start.47 = (f32[2048]{0:T(1024)S(1)}, f32[2048]{0:T(1024)}, u32[]{:S(2)}) copy-start(f32[2048]{0:T(1024)} %param.46) | copy-start | bytes 24580
  1144.6 65.3 %copy-start.5 = (bf16[256,2048]{1,0:T(8,128)(2,1)S(1)}, bf16[256,2048]{1,0:T(8,128)(2,1)}, u32[]{:S(2)}) copy-start(bf16[256,2048]{1,0:T(8,128)(2,1)} %param.27) | copy-start | bytes 3145732
  1144.6 65.3 %copy-start.28 = (f32[1,2048]{1,0:T(1,128)S(1)}, f32[1,2048]{1,0:T(1,128)}, u32[]{:S(2)}) copy-start(f32[1,2048]{1,0:T(1,128)} %copy-done.27) | copy-start | bytes 24580
  1144.6 65.3 %copy-start.31 = (f32[256]{0:T(256)S(1)}, f32[256]{0:T(256)}, u32[]{:S(2)}) copy-start(f32[256]{0:T(256)} %copy-done.30) | copy-start | bytes 3076
  1147.8 64.3 %copy-start.39 = (f32[256]{0:T(256)S(1)}, f32[256]{0:T(256)}, u32[]{:S(2)}) copy-start(f32[256]{0:T(256)} %copy-done.38) | copy-start | bytes 3076
  1147.8 64.3 %copy-start.37 = (f32[256]{0:T(256)S(1)}, f32[256]{0:T(256)}, u32[]{:S(2)}) copy-start(f32[256]{0:T(256)} %copy-done.36) | copy-start | bytes 3076
  1186.1 98.3 %copy-start.34 = (f32[1,2048]{1,0:T(1,128)S(1)}, f32[1,2048]{1,0:T(1,128)}, u32[]{:S(2)}) copy-start(f32[1,2048]{1,0:T(1,128)} %get-tuple-element.310) | copy-start | bytes 24580
  1186.1 98.3 %copy-start.35 = (f32[1,2048]{1,0:T(1,128)S(1)}, f32[1,2048]{1,0:T(1,128)}, u32[]{:S(2)}) copy-start(f32[1,2048]{1,0:T(1,128)} %get-tuple-element.313) | copy-start | bytes 24580
  1209.9 2.3 copy-start.7
  1284.4 48.1 %copy-start.29 = (f32[4,2048]{1,0:T(4,128)S(1)}, f32[4,2048]{1,0:T(4,128)}, u32[]{:S(2)}) copy-start(f32[4,2048]{1,0:T(4,128)} %param.47) | copy-start | bytes 98308
  1284.4 48.2 %copy-start.32 = (f32[4,2048]{1,0:T(4,128)S(1)}, f32[4,2048]{1,0:T(4,128)}, u32[]{:S(2)}) copy-start(f32[4,2048]{1,0:T(4,128)} %param.48) | copy-start | bytes 98308
  1284.4 48.2 %copy-start.33 = (f32[4,2048]{1,0:T(4,128)S(1)}, f32[4,2048]{1,0:T(4,128)}, u32[]{:S(2)}) copy-start(f32[4,2048]{1,0:T(4,128)} %param.49) | copy-start | bytes 98308
  (7 other events, 6.2 us)
Sparse Core Ops, SparseCore 0:
  16.0 37.1 all-gather.6
  55.8 99.9 all-gather.8
  157.3 32.6 all-gather.16
  214.8 86.6 reduce-scatter.12
  304.3 124.6 all-gather.12
  431.7 49.2 all-gather.10
  485.2 280.9 reduce-scatter.16
  774.5 124.3 all-gather.14
  929.8 206.7 reduce-scatter.10
  1139.0 70.7 reduce-scatter.8
  1212.6 71.7 reduce-scatter.6
  1288.0 283.2 reduce-scatter.14
where the time goes:
time: 1600 us; the launch traced here: 1590 us
  waiting for transfers between devices  1100 us (69%)
  matrix products  219 us (14%)
  local copies, waits for them, and re-layouts  92 us (6%)
  other arithmetic  83.7 us (5%)
  blocking collectives  78.3 us (5%)
    reduce_scatter x1, waiting for transfers between devices, local(): lax.psum_scatter(grad_down, 'dp', scatter_dimension=1, tiled=True)  274 us
    reduce_scatter x1, waiting for transfers between devices, local(): lax.psum_scatter(grad_up, 'dp', scatter_dimension=0, tiled=True)  238 us
    all_gather x1, waiting for transfers between devices, local(): lax.all_gather(lowered[2], 'dp', axis=0, tiled=True)  124 us
    reduce_scatter x1, waiting for transfers between devices, local(): lax.psum_scatter(grad_qkv, 'dp', scatter_dimension=1, tiled=True)  119 us
    all_gather x1, waiting for transfers between devices, local(): lax.all_gather(lowered[0], 'dp', axis=1, tiled=True)  103 us
    reduce_scatter x1, waiting for transfers between devices, local(): lax.psum_scatter(grad_dense, 'dp', scatter_dimension=1, tiled=True)  84.1 us
    reduce_scatter x1, waiting for transfers between devices, local(): lax.psum_scatter(jnp.dot(mixed, dense_full, preferred_element_type=jnp.fl...  71.2 us
    dynamic_update_slice x4, local copies, waits for them, and re-layouts, local(): lax.scan(backward_block, (zero_keys, zero_keys), (query_blocks, block_sta...  43.5 us
  transfers between devices with their start and end apart: 12, of which 10 were waited for; matrix products, arithmetic and copies ran while one was open for 22% of the time, Pallas kernels for 0%

commit v1 on v0

v1 whole, which is shorter than its diff:
```python
import functools
import math

import jax
import jax.numpy as jnp
import numpy as np
from jax import lax
from jax.experimental import pallas as pl
from jax.experimental.pallas import tpu as pltpu
from jax.sharding import Mesh
from jax.sharding import PartitionSpec as P

HEAD = 64
ROT = 32
STEP = 10

BETA_ONE = 0.9
BETA_TWO = 0.999
ADAM_EPS = 1e-08
MATRIX_DECAY = 0.1
VECTOR_RATE = 0.1

F32 = jnp.float32
BF16 = jnp.bfloat16
MESH = pl.DeviceIdType.MESH
ANY = pl.BlockSpec(memory_space=pl.ANY)
VMEM_LIMIT = 52 * 1024 * 1024


def gather_kernel(n_zh, n_ref, c_ref, *refs):
    halves = refs[:8]
    n_all, c_all = refs[8:10]
    full = refs[10:14]
    w_send, w_recv, y_send, y_recv, a_send, a_recv, local_sem = refs[14:]
    zh, zp, y = lax.axis_index("zh"), lax.axis_index("zp"), lax.axis_index("y")
    x, c = lax.axis_index("x"), lax.axis_index("c")
    mp = x * 2 + c
    steps = [(s, f) for s in range(n_zh) for f in (0, 1)]

    def block_of(s, f):
        return lax.rem(zh - s + n_zh, n_zh) * 4 + (zp ^ f) * 2 + y

    def target(s, f):
        return {"zh": lax.rem(zh + s, n_zh), "zp": zp ^ f}

    barrier = pltpu.get_barrier_semaphore()
    partners = [target(s, f) for s, f in steps[1:]] + [{"y": 1 - y}, {"x": 1 - x}, {"c": 1 - c}]
    for partner in partners:
        pl.semaphore_signal(barrier, inc=1, device_id=partner, device_id_type=MESH)
    pl.semaphore_wait(barrier, len(partners))

    def remote(src, dst, send, recv, to):
        return pltpu.make_async_remote_copy(
            src_ref=src, dst_ref=dst, send_sem=send, recv_sem=recv, device_id=to, device_id_type=MESH
        )

    me = block_of(0, 0)
    locals_ = [
        pltpu.make_async_copy(n_ref, n_all.at[zp, mp], local_sem.at[0]),
        pltpu.make_async_copy(c_ref, c_all.at[zp, mp], local_sem.at[1]),
    ]
    for w in range(4):
        locals_.append(pltpu.make_async_copy(halves[2 * w], full[w].at[me], local_sem.at[2 + w]))
    started = []

    def go(copy):
        copy.start()
        started.append(copy)
        return copy

    def z_copy(w, i):
        s, f = steps[i]
        return remote(halves[2 * w + f], full[w].at[me], w_send.at[w, i], w_recv.at[w, i], target(s, f))

    def y_copy(w, i):
        s, f = steps[i]
        src = halves[2 * w] if i == 0 else full[w].at[block_of(s, f)]
        return remote(src, full[w].at[block_of(s, f)], y_send.at[w, i], y_recv.at[w, i], {"y": 1 - y})

    def act_copy(k, stage, part):
        own, every = ((n_ref, n_all), (c_ref, c_all))[k]
        if stage == 0:
            return remote(own, every.at[zp, mp], a_send.at[k, 0], a_recv.at[k, 0], {"zp": 1 - zp})
        row = zp ^ (part % 2)
        column = mp if part < 2 else (1 - x) * 2 + c
        src = own if part == 0 else every.at[row, column]
        slot = 1 + part if stage == 1 else 3 + part
        to = {"x": 1 - x} if stage == 1 else {"c": 1 - c}
        return remote(src, every.at[row, column], a_send.at[k, slot], a_recv.at[k, slot], to)

    for k in (0, 1):
        go(act_copy(k, 0, 0))
        go(act_copy(k, 1, 0))
    for w in (0, 1):
        for i in range(1, len(steps)):
            go(z_copy(w, i))
        go(y_copy(w, 0))
    for copy in locals_:
        copy.start()
    for k in (0, 1):
        go(act_copy(k, 2, 0))

    for k in (0, 1):
        act_copy(k, 0, 0).wait_recv()
        go(act_copy(k, 1, 1))
        go(act_copy(k, 2, 1))
    for w in range(4):
        for i in range(1, len(steps)):
            z_copy(w, i).wait_recv()
            go(y_copy(w, i))
        if w + 2 < 4:
            for i in range(1, len(steps)):
                go(z_copy(w + 2, i))
            go(y_copy(w + 2, 0))
        if w < 2:
            for part in (0, 1):
                act_copy(w, 1, part).wait_recv()
                go(act_copy(w, 2, 2 + part))
    for k in (0, 1):
        for part in range(4):
            act_copy(k, 2, part).wait_recv()
    for w in range(4):
        for i in range(len(steps)):
            y_copy(w, i).wait_recv()
    for copy in started:
        copy.wait_send()
    for copy in locals_:
        copy.wait()


def gather(n_zh, normed, cotangent, halves):
    rows, width = normed.shape
    dp = 4 * n_zh
    outs = [jax.ShapeDtypeStruct((2, 4, rows, width), BF16)] * 2
    outs += [jax.ShapeDtypeStruct((dp,) + halves[2 * w].shape, BF16) for w in range(4)]
    count = 2 * n_zh
    dma = pltpu.SemaphoreType.DMA
    return pl.pallas_call(
        functools.partial(gather_kernel, n_zh),
        out_shape=outs,
        in_specs=[ANY] * 10,
        out_specs=[ANY] * 6,
        scratch_shapes=[
            dma((4, count)),
            dma((4, count)),
            dma((4, count)),
            dma((4, count)),
            dma((2, 7)),
            dma((2, 7)),
            dma((6,)),
        ],
        compiler_params=pltpu.CompilerParams(collective_id=0, has_side_effects=True),
    )(normed, cotangent, *halves)


def mlp_kernel(n_ref, c_ref, up_ref, down_ref, bias_ref, act_ref, grad_ref, sum_ref):
    chunk = 256
    rows = n_ref[...]
    back = c_ref[...]

    @pl.when(pl.program_id(0) == 0)
    def _():
        sum_ref[...] = jnp.zeros_like(sum_ref)

    for j in range(up_ref.shape[1] // chunk):
        cols = pl.ds(j * chunk, chunk)
        hidden = jnp.dot(rows, up_ref[:, cols], preferred_element_type=F32) + bias_ref[:, cols]
        grad = jnp.dot(back, down_ref[:, cols], preferred_element_type=F32)
        k0 = math.sqrt(2.0 / math.pi)
        square = hidden * hidden
        tanh = jnp.tanh(k0 * (hidden * (1.0 + 0.044715 * square)))
        act_ref[:, cols] = (0.5 * hidden * (1.0 + tanh)).astype(BF16)
        slope = 0.5 * (1.0 + tanh) + 0.5 * hidden * (1.0 - tanh * tanh) * (
            k0 * (1.0 + 3.0 * 0.044715 * square)
        )
        low = (grad * slope).astype(BF16)
        grad_ref[:, cols] = low
        sum_ref[:, cols] += jnp.sum(low.astype(F32), axis=0, keepdims=True)


def mlp(normed, back, up, down_t, bias):
    tokens, width = normed.shape
    units = up.shape[1]
    tile = 512
    rows = pl.BlockSpec((tile, width), lambda i: (i, 0))
    whole = pl.BlockSpec((width, units), lambda i: (0, 0))
    one = pl.BlockSpec((1, units), lambda i: (0, 0))
    out = pl.BlockSpec((tile, units), lambda i: (i, 0))
    return pl.pallas_call(
        mlp_kernel,
        grid=(tokens // tile,),
        out_shape=[
            jax.ShapeDtypeStruct((tokens, units), BF16),
            jax.ShapeDtypeStruct((tokens, units), BF16),
            jax.ShapeDtypeStruct((1, units), F32),
        ],
        in_specs=[rows, rows, whole, whole, one],
        out_specs=[out, out, one],
        compiler_params=pltpu.CompilerParams(vmem_limit_bytes=VMEM_LIMIT),
        cost_estimate=pl.CostEstimate(
            flops=4 * tokens * width * units,
            bytes_accessed=4 * width * (tokens + units) + 4 * tokens * units,
            transcendentals=tokens * units,
        ),
    )(normed, back, up, down_t, bias)


def turn(values, cos, sin_up, sin_down):
    lanes = values.shape[-1]
    after = pltpu.roll(values, lanes - ROT // 2, 1)
    before = pltpu.roll(values, ROT // 2, 1)
    return values * cos + after * sin_up + before * sin_down


def attention_kernel(
    proj_ref, bias_ref, grad_ref, cos_ref, up_ref, down_ref,
    mixed_ref, out_ref, sum_ref,
    q_s, k_s, v_s, dq_s, dk_s, dv_s, s_s, p_s,
):
    seq = proj_ref.shape[1]
    width = proj_ref.shape[2] // 3
    lanes = 2 * HEAD
    block = 256
    count = seq // block
    scale = HEAD ** (-0.5)
    cos, sin_up, sin_down = cos_ref[...], up_ref[...], down_ref[...]
    first = lax.broadcasted_iota(jnp.int32, (1, lanes), 1) < HEAD
    diagonal = lax.broadcasted_iota(jnp.int32, (block, block), 0) <= lax.broadcasted_iota(
        jnp.int32, (block, block), 1
    )
    tn = (((0,), (0,)), ((), ()))
    nt = (((1,), (1,)), ((), ()))

    def pair(hp, carry):
        def cols(t):
            return pl.ds(pl.multiple_of(t * width + hp * lanes, lanes), lanes)

        here = pl.ds(pl.multiple_of(hp * lanes, lanes), lanes)

        def load(t):
            return proj_ref[0, :, cols(t)] + bias_ref[:, cols(t)]

        q_s[...] = turn(load(0), cos, sin_up, sin_down).astype(BF16)
        k_s[...] = turn(load(1), cos, sin_up, sin_down).astype(BF16)
        v_s[...] = load(2).astype(BF16)
        dk_s[...] = jnp.zeros_like(dk_s)
        dv_s[...] = jnp.zeros_like(dv_s)
        for qb in range(count):
            rows = pl.ds(qb * block, block)
            q_rows = q_s[rows, :] * jnp.asarray(scale, BF16)
            g_rows = grad_ref[0, rows, here]
            mixed_halves, dq_halves = [], []
            for h in (0, 1):
                mine = first if h == 0 else jnp.logical_not(first)
                q_one = jnp.where(mine, q_rows, jnp.zeros_like(q_rows))
                g_one = jnp.where(mine, g_rows, jnp.zeros_like(g_rows))
                top = None
                for j in range(qb + 1):
                    scores = lax.dot_general(
                        k_s[pl.ds(j * block, block), :], q_one, nt, preferred_element_type=F32
                    )
                    if j == qb:
                        scores = jnp.where(diagonal, scores, -1e30)
                    s_s[h, j] = scores
                    peak = jnp.max(scores, axis=0, keepdims=True)
                    top = peak if top is None else jnp.maximum(top, peak)
                total = None
                for j in range(qb + 1):
                    e = jnp.exp(s_s[h, j] - top)
                    s_s[h, j] = e
                    part = jnp.sum(e, axis=0, keepdims=True)
                    total = part if total is None else total + part
                inverse = 1.0 / total
                mixed, inner = None, None
                for j in range(qb + 1):
                    keys = pl.ds(j * block, block)
                    probs = s_s[h, j] * inverse
                    low = probs.astype(BF16)
                    part = lax.dot_general(low, v_s[keys, :], tn, preferred_element_type=F32)
                    mixed = part if mixed is None else mixed + part
                    dv_s[h, keys, :] += jnp.dot(low, g_rows, preferred_element_type=F32)
                    grad_probs = lax.dot_general(v_s[keys, :], g_one, nt, preferred_element_type=F32)
                    s_s[h, j] = probs
                    p_s[h, j] = grad_probs
                    part = jnp.sum(probs * grad_probs, axis=0, keepdims=True)
                    inner = part if inner is None else inner + part
                dq = None
                for j in range(qb + 1):
                    keys = pl.ds(j * block, block)
                    grad_scores = (s_s[h, j] * (p_s[h, j] - inner)).astype(BF16)
                    part = lax.dot_general(grad_scores, k_s[keys, :], tn, preferred_element_type=F32)
                    dq = part if dq is None else dq + part
                    dk_s[h, keys, :] += jnp.dot(grad_scores, q_rows, preferred_element_type=F32)
                mixed_halves.append(mixed)
                dq_halves.append(dq)
            mixed_ref[0, rows, here] = jnp.where(first, *mixed_halves).astype(BF16)
            dq_s[rows, :] = jnp.where(first, *dq_halves) * scale
        gq = turn(dq_s[...], cos, -sin_up, -sin_down).astype(BF16)
        gk = turn(jnp.where(first, dk_s[0], dk_s[1]), cos, -sin_up, -sin_down).astype(BF16)
        gv = jnp.where(first, dv_s[0], dv_s[1]).astype(BF16)
        for t, g in enumerate((gq, gk, gv)):
            out_ref[0, :, cols(t)] = g
            sum_ref[0, :, cols(t)] = jnp.sum(g.astype(F32), axis=0, keepdims=True)
        return carry

    lax.fori_loop(0, width // lanes, pair, 0)


def attention(proj, bias, grad_mixed, tables):
    seqs, seq, triple = proj.shape
    width = triple // 3
    lanes = 2 * HEAD
    block = 256
    table = pl.BlockSpec((seq, lanes), lambda i: (0, 0))
    return pl.pallas_call(
        attention_kernel,
        grid=(seqs,),
        out_shape=[
            jax.ShapeDtypeStruct((seqs, seq, width), BF16),
            jax.ShapeDtypeStruct((seqs, seq, triple), BF16),
            jax.ShapeDtypeStruct((seqs, 1, triple), F32),
        ],
        in_specs=[
            pl.BlockSpec((1, seq, triple), lambda i: (i, 0, 0)),
            pl.BlockSpec((1, triple), lambda i: (0, 0)),
            pl.BlockSpec((1, seq, width), lambda i: (i, 0, 0)),
            table,
            table,
            table,
        ],
        out_specs=[
            pl.BlockSpec((1, seq, width), lambda i: (i, 0, 0)),
            pl.BlockSpec((1, seq, triple), lambda i: (i, 0, 0)),
            pl.BlockSpec((1, 1, triple), lambda i: (i, 0, 0)),
        ],
        scratch_shapes=[
            pltpu.VMEM((seq, lanes), BF16),
            pltpu.VMEM((seq, lanes), BF16),
            pltpu.VMEM((seq, lanes), BF16),
            pltpu.VMEM((seq, lanes), F32),
            pltpu.VMEM((2, seq, lanes), F32),
            pltpu.VMEM((2, seq, lanes), F32),
            pltpu.VMEM((2, seq // block, block, block), F32),
            pltpu.VMEM((2, seq // block, block, block), F32),
        ],
        compiler_params=pltpu.CompilerParams(vmem_limit_bytes=VMEM_LIMIT),
        cost_estimate=pl.CostEstimate(
            flops=40 * seqs * seq * seq * width, bytes_accessed=20 * seqs * seq * width, transcendentals=0
        ),
    )(proj, bias, grad_mixed, *tables)


def rotation_tables(seq):
    lane = np.arange(2 * HEAD) % HEAD
    exponent = (lane % (ROT // 2)).astype(np.float32) * np.float32(2.0 / ROT)
    inverse = jnp.exp(-math.log(10000.0) * jnp.asarray(exponent))
    angles = jnp.arange(seq, dtype=F32)[:, None] * inverse[None, :]
    cos, sin = jnp.cos(angles), jnp.sin(angles)
    turned = jnp.asarray(lane < ROT)[None, :]
    low = jnp.asarray(lane < ROT // 2)[None, :]
    zero = jnp.zeros_like(sin)
    return (
        jnp.where(turned, cos, 1.0),
        jnp.where(low, -sin, zero),
        jnp.where(turned & ~low, sin, zero),
    )


def normalize(inputs, scales, offsets):
    average = jnp.mean(inputs, axis=-1, keepdims=True)
    centred = inputs - average
    variance = jnp.mean(centred * centred, axis=-1, keepdims=True)
    return centred * lax.rsqrt(variance + 1e-05) * scales + offsets


def adam_update(weight, moment_one, moment_two, gradient, step_rate, decay_rate):
    first_new = BETA_ONE * moment_one + (1.0 - BETA_ONE) * gradient
    second_new = BETA_TWO * moment_two + (1.0 - BETA_TWO) * gradient * gradient
    normalized = (
        first_new
        / (1.0 - BETA_ONE**STEP)
        / (jnp.sqrt(second_new / (1.0 - BETA_TWO**STEP)) + ADAM_EPS)
    )
    return (weight - step_rate * (normalized + decay_rate * weight), first_new, second_new)


def flip(value, name):
    return lax.ppermute(value, name, [(0, 1), (1, 0)])


def pick(value, index, axis):
    return lax.dynamic_index_in_dim(value, index, axis, keepdims=False)


def z_send(value, n_zh, s, f):
    pairs = [
        (h * 2 + p, (h + s) % n_zh * 2 + (p ^ f)) for h in range(n_zh) for p in range(2)
    ]
    return lax.ppermute(value, ("zh", "zp"), pairs)


def reduce_weight(partial, n_zh):
    zh, zp, y = lax.axis_index("zh"), lax.axis_index("zp"), lax.axis_index("y")
    blocks = partial.reshape(n_zh, 2, 2, -1, partial.shape[1])
    got = flip(pick(blocks, 1 - y, 2), "y")
    summed = (pick(blocks, y, 2).astype(F32) + got.astype(F32)).astype(BF16)

    def block(s, f):
        return pick(pick(summed, lax.rem(zh + s, n_zh), 0), zp ^ f, 0)

    mine = block(0, 0).astype(F32)
    theirs = z_send(block(0, 1), n_zh, 0, 1).astype(F32)
    for s in range(1, n_zh):
        mine = mine + z_send(block(s, 0), n_zh, s, 0).astype(F32)
        theirs = theirs + z_send(block(s, 1), n_zh, s, 1).astype(F32)
    low = jnp.where(zp == 0, mine, theirs)
    high = jnp.where(zp == 0, theirs, mine)
    return jnp.stack([low, high], axis=1)


def reduce_rows(partial, tok_rows):
    zp, x, c = lax.axis_index("zp"), lax.axis_index("x"), lax.axis_index("c")
    value = partial.reshape(2, 2, 2, tok_rows, partial.shape[1])
    value = pick(value, c, 2) + flip(pick(value, 1 - c, 2).astype(BF16), "c").astype(F32)
    value = pick(value, x, 1) + flip(pick(value, 1 - x, 1).astype(BF16), "x").astype(F32)
    return pick(value, zp, 0) + flip(pick(value, 1 - zp, 0).astype(BF16), "zp").astype(F32)


def sum_over(value, n_zh, names):
    for name in names:
        if name == "zh":
            step = 1
            while step < n_zh:
                value = value + lax.ppermute(value, "zh", [(i, i ^ step) for i in range(n_zh)])
                step *= 2
        else:
            value = value + flip(value, name)
    return value


def local(
    n_zh,
    tokens, cotangent,
    qkv_weight, qkv_first, qkv_second,
    dense_weight, dense_first, dense_second,
    up_weight, up_first, up_second,
    down_weight, down_first, down_second,
    head_bias, head_first, head_second,
    hidden_bias, hidden_first, hidden_second,
    outer_params, outer_first, outer_second,
):
    zp = lax.axis_index("zp")
    tok_rows, width = tokens.shape
    seq_rows = tok_rows * 4
    bw = qkv_weight.shape[1]
    local_width = qkv_weight.shape[2]
    half_width = local_width // 2
    half_units = up_weight.shape[1] // 2

    tokens_wide = tokens.astype(F32)
    normed, norm_back = jax.vjp(normalize, tokens_wide, outer_params[0], outer_params[1])

    qkv_rows = jnp.moveaxis(qkv_weight, 0, 1).reshape(bw, 3, 2, half_width)
    qkv_rows = jnp.moveaxis(qkv_rows, 2, 1).reshape(bw, 2, 3 * half_width).astype(BF16)
    dense_rows = dense_weight.T.reshape(bw, 2, half_width).astype(BF16)
    up_rows = up_weight.reshape(bw, 2, half_units).astype(BF16)
    down_rows = down_weight.T.reshape(bw, 2, half_units).astype(BF16)
    halves = []
    for rows in (up_rows, down_rows, qkv_rows, dense_rows):
        halves += [pick(rows, zp, 1), pick(rows, 1 - zp, 1)]
    n_all, c_all, up, down_t, qkv, dense_t = gather(
        n_zh, normed.astype(BF16), cotangent, halves
    )
    n_all = n_all.reshape(2 * seq_rows, width)
    c_all = c_all.reshape(2 * seq_rows, width)
    up, down_t, qkv, dense_t = (w.reshape(width, w.shape[2]) for w in (up, down_t, qkv, dense_t))

    bias_half = pick(hidden_bias.reshape(2, 1, half_units), zp, 0)
    act, grad_hidden, hidden_part = mlp(n_all, c_all, up, down_t, bias_half)
    tn = (((0,), (0,)), ((), ()))
    nt = (((1,), (1,)), ((), ()))

    def weight_grad(left, right):
        return lax.dot_general(left, right, tn, preferred_element_type=F32).astype(BF16)

    down_sum = reduce_weight(weight_grad(c_all, act), n_zh)
    up_sum = reduce_weight(weight_grad(n_all, grad_hidden), n_zh)

    proj = jnp.dot(n_all, qkv, preferred_element_type=F32).reshape(2, seq_rows, 3 * half_width)
    grad_mixed = (
        jnp.dot(c_all, dense_t, preferred_element_type=F32)
        .astype(BF16)
        .reshape(2, seq_rows, half_width)
    )
    head_half = pick(head_bias.reshape(3, 2, half_width), zp, 1).reshape(1, 3 * half_width)
    mixed, grad_proj, head_part = attention(
        proj, head_half, grad_mixed, rotation_tables(seq_rows)
    )
    mixed = mixed.reshape(2 * seq_rows, half_width)
    grad_proj = grad_proj.reshape(2 * seq_rows, 3 * half_width)
    dense_sum = reduce_weight(weight_grad(c_all, mixed), n_zh)
    qkv_sum = reduce_weight(weight_grad(n_all, grad_proj), n_zh)

    grad_normed = reduce_rows(
        lax.dot_general(grad_hidden, up, nt, preferred_element_type=F32)
        + lax.dot_general(grad_proj, qkv, nt, preferred_element_type=F32),
        tok_rows,
    )
    branch = reduce_rows(
        lax.dot_general(act, down_t, nt, preferred_element_type=F32)
        + lax.dot_general(mixed, dense_t, nt, preferred_element_type=F32),
        tok_rows,
    )
    layer_out = (tokens_wide + branch + outer_params[2] + outer_params[3]).astype(BF16)

    input_part, gain_grad, shift_grad = norm_back(grad_normed)
    back_wide = cotangent.astype(F32)
    input_grad = back_wide + input_part
    out_bias_grad = jnp.sum(back_wide, axis=0)

    vectors = jnp.concatenate(
        [hidden_part.reshape(half_units), jnp.sum(head_part, axis=0).reshape(3 * half_width)]
    )
    both = jnp.where(
        jnp.arange(2)[:, None] == zp, vectors[None, :], jnp.zeros_like(vectors)[None, :]
    )
    both = sum_over(both, n_zh, ("zp", "y", "zh"))
    hidden_sum = both[:, :half_units].reshape(2 * half_units)
    head_sum = jnp.moveaxis(both[:, half_units:].reshape(2, 3, half_width), 0, 1).reshape(
        3, local_width
    )
    outer_sum = sum_over(
        jnp.stack([gain_grad, shift_grad, out_bias_grad]), n_zh, ("c", "x", "y", "zp", "zh")
    )
    outer_sum = jnp.concatenate([outer_sum, outer_sum[2:]], axis=0)

    model = width
    qkv_sum = qkv_sum.reshape(bw, 2, 3, half_width)
    qkv_sum = jnp.moveaxis(qkv_sum, 2, 0).reshape(3, bw, local_width)
    dense_sum = dense_sum.reshape(bw, local_width).T
    up_sum = up_sum.reshape(bw, 2 * half_units)
    down_sum = down_sum.reshape(bw, 2 * half_units).T
    new_qkv = adam_update(
        qkv_weight, qkv_first, qkv_second, qkv_sum, (model // 2) ** (-0.5), MATRIX_DECAY
    )
    new_dense = adam_update(
        dense_weight, dense_first, dense_second, dense_sum, (model // 16) ** (-0.5), MATRIX_DECAY
    )
    new_up = adam_update(up_weight, up_first, up_second, up_sum, model ** (-0.5), MATRIX_DECAY)
    new_down = adam_update(
        down_weight, down_first, down_second, down_sum, (4 * model) ** (-0.5), MATRIX_DECAY
    )
    new_head = adam_update(head_bias, head_first, head_second, head_sum, VECTOR_RATE, 0.0)
    new_hidden = adam_update(
        hidden_bias, hidden_first, hidden_second, hidden_sum, VECTOR_RATE, 0.0
    )
    new_outer = adam_update(outer_params, outer_first, outer_second, outer_sum, VECTOR_RATE, 0.0)
    return (
        layer_out,
        input_grad,
        *new_qkv,
        *new_dense,
        *new_up,
        *new_down,
        *new_head,
        *new_hidden,
        *new_outer,
    )


def solution(mesh):
    n_zh = mesh.shape["dp"] // 4
    split = Mesh(mesh.devices.reshape(n_zh, 2, 2, 2, 2), ("zh", "zp", "y", "x", "c"))
    dp, mp = ("zh", "zp", "y"), ("x", "c")
    rows = P(dp + mp, None)
    qkv, dense, up, down = P(None, dp, mp), P(mp, dp), P(dp, mp), P(mp, dp)
    rest = (qkv,) * 3 + (dense,) * 3 + (up,) * 3 + (down,) * 3
    rest += (P(None, mp),) * 3 + (P(mp),) * 3 + (P(),) * 3
    return jax.shard_map(
        functools.partial(local, n_zh),
        mesh=split,
        in_specs=(rows, rows) + rest,
        out_specs=(rows, rows) + rest,
        check_vma=False,
    )
```

time: 1600 us -> 699 us (0.44)
  waiting for transfers between devices: 1100 us -> 123 us
  Pallas kernels: 0 us -> 288 us
  matrix products: 219 us -> 113 us
  blocking collectives: 78.3 us -> 0 us
  starting transfers between devices: 1.07 us -> 37 us
  local copies, waits for them, and re-layouts: 92 us -> 62.2 us
  other arithmetic: 83.7 us -> 65.5 us
    reduce_scatter x6 -> x0, waiting for transfers between devices: 810 us -> none  [the longest x1 274 us: local(): lax.psum_scatter(grad_down, 'dp', scatter_dimension=1, tiled=True)]
    pallas_call x0 -> x3, Pallas kernels: none -> 288 us  [the longest x1 221 us: gather(): pl.pallas_call(functools.partial(gather_kernel, n_zh), out_shape=outs, in...]
    all_gather x6 -> x0, waiting for transfers between devices: 285 us -> none  [the longest x1 124 us: local(): lax.all_gather(lowered[2], 'dp', axis=0, tiled=True)]
    ppermute x0 -> x30, waiting for transfers between devices: none -> 123 us  [the longest x16 105 us: flip(): return lax.ppermute(value, name, [(0, 1), (1, 0)])]
    dot_general x26 -> x10, matrix products: 219 us -> 113 us  [the longest x4 46.2 us: weight_grad(): lax.dot_general(left, right, tn, preferred_element_type=F32).astype(BF16)]
    psum x2 -> x0, blocking collectives: 78.3 us -> none  [the longest x1 43 us: local(): lax.psum(jnp.stack([gain_grad, shift_grad, out_bias_grad, out_bias_grad])...]
    dynamic_update_slice x4 -> x0, local copies, waits for them, and re-layouts: 43.5 us -> none  [local(): lax.scan(backward_block, (zero_keys, zero_keys), (query_blocks, block_sta...]
    ppermute x0 -> x30, starting transfers between devices: none -> 37 us  [the longest x12 21.8 us: z_send(): return lax.ppermute(value, ('zh', 'zp'), pairs)]
  transfers between devices with their start and end apart: 12 -> 30, of which waited for: 10 -> 10; matrix products, arithmetic and copies ran while one was open for 22% -> 27% of each run, Pallas kernels for 0% -> 4%
where the time goes in v1:
time: 699 us; the launch traced here: 691 us
  Pallas kernels  288 us (41%)
  waiting for transfers between devices  123 us (18%)
  matrix products  113 us (16%)
  other arithmetic  65.5 us (9%)
  local copies, waits for them, and re-layouts  62.2 us (9%)
  starting transfers between devices  37 us (5%)
    pallas_call x1, Pallas kernels, gather(): pl.pallas_call(functools.partial(gather_kernel, n_zh), out_shape=outs, in...  221 us
    ppermute x16, waiting for transfers between devices, flip(): return lax.ppermute(value, name, [(0, 1), (1, 0)])  105 us
    dot_general x4, matrix products, weight_grad(): lax.dot_general(left, right, tn, preferred_element_type=F32).astype(BF16)  46.2 us
    pallas_call x1, Pallas kernels, attention(): pl.pallas_call(attention_kernel, grid=(seqs,), out_shape=[jax.ShapeDtypeS...  38 us
    pallas_call x1, Pallas kernels, mlp(): pl.pallas_call(mlp_kernel, grid=(tokens // tile,), out_shape=[jax.ShapeDt...  29.6 us
    unnamed x127, local copies, waits for them, and re-layouts  24.4 us
    ppermute x12, starting transfers between devices, z_send(): return lax.ppermute(value, ('zh', 'zp'), pairs)  21.8 us
    sub x7, other arithmetic, adam_update(): weight - step_rate * (normalized + decay_rate * weight)  18.3 us
  transfers between devices with their start and end apart: 30, of which 10 were waited for; matrix products, arithmetic and copies ran while one was open for 27% of the time, Pallas kernels for 4%

profile of v1, /device:TPU:0, one launch (start us, length us, event | category | flops | bytes accessed | tf_op | source)
XLA Modules:
  0.0 690.6 jit_solution(2718220681722948008)
XLA Ops:
  2.2 1.6 fusion.14
  6.7 2.9 convert_element_type.230
  9.6 1.8 convert_element_type.231
  13.6 3.1 constant_dynamic-slice_fusion.14
  16.7 1.9 copy.86
  21.6 2.6 copy_bitcast_fusion
  25.6 220.6 %shard_map.425 = (bf16[2,4,256,2048]{3,2,1,0:T(8,128)(2,1)}, bf16[2,4,256,2048]{3,2,1,0:T(8,128)(2,1)}, bf16[8,256,1024]{2,1,0:T(8,128)(2,1)}, bf16[8,256,1024]{...) custom-call(bf16[256,2048]{1,0:T(8,128)(2,1)} %fusion.12.n_ref, bf16[256,2048]{1,0:T(8,128)(2,1)} %c_ref.1, ...), custom_call_target="tpu_custom_call" | custom-call | tf_op jit(solution)/shard_map/pallas_call | solution.py:138
  246.3 7.1 %convolution_convert_fusion.4 = bf16[2048,256]{1,0:T(8,128)(2,1)} fusion(bf16[2048,2048]{1,0:T(8,128)(2,1)} %bitcast.281, bf16[2048,256]{1,0:T(8,128)(2,1)} %bitcast.255), kind=kOutput, calls=%fused_computation.34 | convolution fusion | flops 2148007936 | bytes 10485760 | tf_op jit(solution)/shard_map/dot_general | solution.py:491
  253.4 8.6 %fusion.59.proj_ref = f32[2,1024,768]{2,1,0:T(8,128)} fusion(bf16[2,1024,2048]{2,1,0:T(8,128)(2,1)S(1)} %bitcast.288, bf16[2048,768,1]{1,0,2:T(8,128)(2,1)S(1)} %bitcast.294), kind=kOutput, calls=%fused_computation.162 | convolution fusion | flops 6442450944 | bytes 17825792 | tf_op jit(solution)/shard_map/dot_general | solution.py:489
  262.1 2.0 fusion.34
  264.1 38.0 %shard_map.427 = (bf16[2,1024,256]{2,1,0:T(8,128)(2,1)}, bf16[2,1024,768]{2,1,0:T(8,128)(2,1)}, f32[2,1,768]{2,1,0:T(1,128)S(1)}) custom-call(f32[2,1024,768]{2,1,0:T(8,128)} %fusion.59.proj_ref, f32[1,768]{1,0:T(1,128)S(1)} %bitcast.231, bf16[2,1024,256]{2,1,0:T(8,128)(2,1)} %bitcast.297, f32[1024,128]{1,0:T(8,128)S(1)} %get-tuple-element.135.cos_ref, ...), custom_call_target="tpu_custom_call" | custom-call | flops 21474836480 | bytes 10485760 | tf_op jit(solution)/shard_map/pallas_call | solution.py:315
  302.1 6.1 convolution_convert_fusion.3
  309.7 10.2 %convolution_convert_fusion.2 = bf16[2048,768]{1,0:T(8,128)(2,1)S(1)} fusion(bf16[2048,2048]{1,0:T(8,128)(2,1)} %bitcast.285, bf16[2048,768]{1,0:T(8,128)(2,1)} %bitcast.295), kind=kOutput, calls=%fused_computation.18 | convolution fusion | flops 6444023808 | bytes 14680064 | tf_op jit(solution)/shard_map/dot_general | solution.py:484
  321.3 1.6 copy.99
  324.4 29.6 %shard_map.426 = (bf16[2048,1024]{1,0:T(8,128)(2,1)}, bf16[2048,1024]{1,0:T(8,128)(2,1)}, f32[1,1024]{1,0:T(1,128)S(1)}) custom-call(bf16[2048,2048]{1,0:T(8,128)(2,1)} %bitcast.286, bf16[2048,2048]{1,0:T(8,128)(2,1)} %bitcast.283, bf16[2048,1024]{1,0:T(8,128)(2,1)} %bitcast.291, bf16[2048,1024]{1,0:T(8,128)(2,1)} %bitcast.289, f32[1,1024]{1,0:T(1,128)S(1)} %fusion.39.bias_ref), custom_call_target="tpu_custom_call" | custom-call | flops 17179869184 | bytes 33554432 | tf_op jit(solution)/shard_map/pallas_call | solution.py:189
  354.1 12.9 %fusion.60 = f32[2048,2048]{1,0:T(8,128)} fusion(bf16[2048,768]{1,0:T(8,128)(2,1)} %bitcast.296, bf16[2048,768]{1,0:T(8,128)(2,1)} %bitcast.293), kind=kOutput, calls=%fused_computation.163 | convolution fusion | flops 6442450944 | bytes 23068672 | tf_op jit(solution)/shard_map/dot_general | solution.py:506
  367.1 17.5 %convolution_add_fusion.1 = f32[2048,2048]{1,0:T(8,128)} fusion(f32[2048,2048]{1,0:T(8,128)} %fusion.60, bf16[2048,1024]{1,0:T(8,128)(2,1)} %get-tuple-element.43, bf16[2048,1024]{1,0:T(8,128)(2,1)} %bitcast.292), kind=kOutput, calls=%fused_computation.5 | convolution fusion | flops 8594128896 | bytes 41943040 | tf_op jit(solution)/shard_map/dot_general | solution.py:505
  384.6 6.3 fusion.1
  392.0 11.9 %fusion.58 = f32[2048,2048]{1,0:T(8,128)} fusion(bf16[2048,1024]{1,0:T(8,128)(2,1)S(1)} %copy-done.52, bf16[2048,1024]{1,0:T(8,128)(2,1)S(1)} %bitcast.290), kind=kOutput, calls=%fused_computation.161 | convolution fusion | flops 8589934592 | bytes 25165824 | tf_op jit(solution)/shard_map/dot_general | solution.py:510
  403.9 8.6 %convolution_add_fusion = f32[2048,2048]{1,0:T(8,128)S(1)} fusion(f32[2048,2048]{1,0:T(8,128)} %fusion.58, bf16[2048,256]{1,0:T(8,128)(2,1)S(1)} %bitcast.245, bf16[2048,256]{1,0:T(8,128)(2,1)S(1)} %bitcast.256), kind=kOutput, calls=%fused_computation | convolution fusion | flops 2151677952 | bytes 35651584 | tf_op jit(solution)/shard_map/dot_general | solution.py:511
  412.5 3.0 fusion
  415.5 16.8 %convolution_convert_fusion.1 = bf16[2048,1024]{1,0:T(8,128)(2,1)S(1)} fusion(bf16[2048,2048]{1,0:T(8,128)(2,1)} %bitcast.287, bf16[2048,1024]{1,0:T(8,128)(2,1)} %get-tuple-element.43), kind=kOutput, calls=%fused_computation.17 | convolution fusion | flops 8592031744 | bytes 16777216 | tf_op jit(solution)/shard_map/dot_general | solution.py:484
  432.4 13.0 %convolution_convert_fusion = bf16[2048,1024]{1,0:T(8,128)(2,1)S(1)} fusion(bf16[2048,2048]{1,0:T(8,128)(2,1)} %bitcast.284, bf16[2048,1024]{1,0:T(8,128)(2,1)S(1)} %copy-done.53), kind=kOutput, calls=%fused_computation.16 | convolution fusion | flops 8592031744 | bytes 16777216 | tf_op jit(solution)/shard_map/dot_general | solution.py:484
  446.0 1.9 dynamic-slice_bitcast_fusion
  453.0 3.0 copy.101
  456.1 2.0 copy.119
  460.1 1.9 collective-permute-start.11
  463.6 8.5 %collective-permute-done.11 = bf16[256,256]{1,0:T(8,128)(2,1)S(1)} collective-permute-done((bf16[256,256]{1,0:T(8,128)(2,1)S(1)}, bf16[256,256]{1,0:T(8,128)(2,1)S(1)}, u32[]{:S(2)}, u32[]{:S(2)}) %collective-permute-start.11) | collective-permute-done | bytes 131104 | tf_op jit(solution)/shard_map/ppermute | solution.py:399
  473.3 3.7 collective-permute-done.12
  477.9 2.0 copy.104
  479.9 2.9 multiply_subtract_fusion.3
  482.8 1.8 fusion.4
  488.3 5.9 bitcast_add_fusion
  494.2 1.9 fusion.22
  496.2 2.0 copy-done.4
  499.7 5.9 bitcast_add_fusion.1
  505.6 1.8 fusion.21
  507.5 5.1 collective-permute-done.7
  517.0 2.8 multiply_subtract_fusion.2
  519.9 3.1 copy.108
  523.0 1.6 copy.109
  524.6 1.6 copy.110
  526.2 3.2 fusion.2
  529.6 9.4 %collective-permute-start.19 = (bf16[256,1024]{1,0:T(8,128)(2,1)S(1)}, bf16[256,1024]{1,0:T(8,128)(2,1)S(1)}, u32[]{:S(2)}, u32[]{:S(2)}) collective-permute-start(bf16[256,1024]{1,0:T(8,128)(2,1)S(1)} %get-tuple-element.104), channel_id=1, source_target_pairs={{0,16},{8,24},{16,0},{24,8},{1,17},{9,25},{17,1},{25,9},{2,18},{10... | collective-permute-start | bytes 1572872 | tf_op jit(solution)/shard_map/ppermute | solution.py:399
  539.4 7.7 %collective-permute-done.4 = bf16[2,256,2048]{2,1,0:T(8,128)(2,1)} collective-permute-done((bf16[2,256,2048]{2,1,0:T(8,128)(2,1)}, bf16[2,256,2048]{2,1,0:T(8,128)(2,1)}, u32[]{:S(2)}, u32[]{:S(2)}) %collective-permute-start.4) | collective-permute-done | bytes 2097184 | tf_op jit(solution)/shard_map/ppermute | solution.py:388
  548.1 3.7 bitcast_add_fusion.2
  551.9 37.0 %collective-permute-done.1 = bf16[2,256,2048]{2,1,0:T(8,128)(2,1)} collective-permute-done((bf16[2,256,2048]{2,1,0:T(8,128)(2,1)}, bf16[2,256,2048]{2,1,0:T(8,128)(2,1)}, u32[]{:S(2)}, u32[]{:S(2)}) %collective-permute-start.1) | collective-permute-done | bytes 2097184 | tf_op jit(solution)/shard_map/ppermute | solution.py:388
  589.0 1.5 collective-permute-start.5
  590.5 2.6 bitcast_add_fusion.3
  593.9 2.8 fusion.3
  598.0 2.7 collective-permute-start.15
  602.4 23.8 %collective-permute-done.5 = bf16[256,2048]{1,0:T(8,128)(2,1)S(1)} collective-permute-done((bf16[256,2048]{1,0:T(8,128)(2,1)S(1)}, bf16[256,2048]{1,0:T(8,128)(2,1)S(1)}, u32[]{:S(2)}, u32[]{:S(2)}) %collective-permute-start.5) | collective-permute-done | bytes 1048608 | tf_op jit(solution)/shard_map/ppermute | solution.py:388
  627.3 30.6 %collective-permute-done.2 = bf16[256,2048]{1,0:T(8,128)(2,1)S(1)} collective-permute-done((bf16[256,2048]{1,0:T(8,128)(2,1)S(1)}, bf16[256,2048]{1,0:T(8,128)(2,1)S(1)}, u32[]{:S(2)}, u32[]{:S(2)}) %collective-permute-start.2) | collective-permute-done | bytes 1048608 | tf_op jit(solution)/shard_map/ppermute | solution.py:388
  657.9 2.1 fusion.56
  660.0 1.7 convert_reduce_fusion.1
  661.9 1.6 pad_maximum_fusion
  663.4 3.0 copy.107
  666.5 1.6 collective-permute-start.26
  668.1 6.5 multiply_subtract_fusion
  675.4 1.6 select_bitcast_fusion.3
  677.0 1.6 collective-permute-done.27
  679.1 3.5 collective-permute-done.28
  682.6 2.7 collective-permute-start.29
  685.3 4.0 multiply_subtract_fusion.1
  (220 shorter events, 45.9 us)
Async XLA Ops:
  2.2 22.0 %copy-start.32 = (f32[256]{0:T(256)}, f32[256]{0:T(256)S(1)}, u32[]{:S(2)}) copy-start(f32[256]{0:T(256)S(1)} %broadcast_multiply_fusion) | copy-start | bytes 3076
  3.9 20.3 %copy-start.37 = (f32[256]{0:T(256)}, f32[256]{0:T(256)S(1)}, u32[]{:S(2)}) copy-start(f32[256]{0:T(256)S(1)} %fusion.41) | copy-start | bytes 3076
  5.1 19.1 %copy-start.26 = (f32[1,2048]{1,0:T(1,128)}, f32[1,2048]{1,0:T(1,128)S(1)}, u32[]{:S(2)}) copy-start(f32[1,2048]{1,0:T(1,128)S(1)} %get-tuple-element.131) | copy-start | bytes 24580
  6.7 4.7 copy-start.7
  246.3 7.1 %copy-start.49 = (bf16[2,4,256,2048]{3,2,1,0:T(8,128)(2,1)S(1)}, bf16[2,4,256,2048]{3,2,1,0:T(8,128)(2,1)}, u32[]{:S(2)}) copy-start(bf16[2,4,256,2048]{3,2,1,0:T(8,128)(2,1)} %get-tuple-element.35) | copy-start | bytes 25165828
  246.3 7.1 %copy-start.51 = (bf16[8,256,768]{2,1,0:T(8,128)(2,1)S(1)}, bf16[8,256,768]{2,1,0:T(8,128)(2,1)}, u32[]{:S(2)}) copy-start(bf16[8,256,768]{2,1,0:T(8,128)(2,1)} %get-tuple-element.40) | copy-start | bytes 9437188
  253.4 8.7 %copy-start.45 = (pred[128]{0:T(512)(128)(4,1)S(1)}, pred[128]{0:T(512)(128)(4,1)}, u32[]{:S(2)}) copy-start(pred[128]{0:T(512)(128)(4,1)} %constant.622) | copy-start | bytes 388
  253.4 8.7 %copy-start.46 = (f32[128]{0:T(128)S(1)}, f32[128]{0:T(128)}, u32[]{:S(2)}) copy-start(f32[128]{0:T(128)} %constant.620) | copy-start | bytes 1540
  253.4 8.7 %copy-start.47 = (pred[128]{0:T(512)(128)(4,1)S(1)}, pred[128]{0:T(512)(128)(4,1)}, u32[]{:S(2)}) copy-start(pred[128]{0:T(512)(128)(4,1)} %constant.618.clone) | copy-start | bytes 388
  253.4 8.7 %copy-start.48 = (pred[128]{0:T(512)(128)(4,1)S(1)}, pred[128]{0:T(512)(128)(4,1)}, u32[]{:S(2)}) copy-start(pred[128]{0:T(512)(128)(4,1)} %constant.617.clone) | copy-start | bytes 388
  308.3 11.7 %copy-start.23 = (bf16[2048,256]{1,0:T(8,128)(2,1)}, bf16[2048,256]{1,0:T(8,128)(2,1)S(1)}, u32[]{:S(2)}) copy-start(bf16[2048,256]{1,0:T(8,128)(2,1)S(1)} %convolution_convert_fusion.3) | copy-start | bytes 3145732
  309.2 149.6 %collective-permute-start.10 = (bf16[2,2,256,256]{3,2,1,0:T(8,128)(2,1)}, bf16[2,2,256,256]{3,2,1,0:T(8,128)(2,1)}, u32[]{:S(2)}, u32[]{:S(2)}) collective-permute-start(bf16[2,2,256,256]{3,2,1,0:T(8,128)(2,1)} %dynamic-slice_bitcast_fusion.8), channel_id=1, source_target_pairs={{0,4},{4,0},{1,5},{5,1},{2,6},{6,2},{3,7},{7,3},{8,12},{12,8},{9,1... | collective-permute-start | bytes 1572872 | tf_op jit(solution)/shard_map/ppermute | solution.py:388
  322.8 160.0 %collective-permute-start.6 = (bf16[2,2,256,768]{2,3,1,0:T(8,128)(2,1)}, bf16[2,2,256,768]{2,3,1,0:T(8,128)(2,1)}, u32[]{:S(2)}, u32[]{:S(2)}) collective-permute-start(bf16[2,2,256,768]{2,3,1,0:T(8,128)(2,1)} %bitcast.52), channel_id=1, source_target_pairs={{0,4},{4,0},{1,5},{5,1},{2,6},{6,2},{3,7},{7,3},{8,12},{12,8},{9,1... | collective-permute-start | bytes 4718600 | tf_op jit(solution)/shard_map/ppermute | solution.py:388
  354.1 91.3 %collective-permute-start.22 = (f32[2,1792]{1,0:T(2,128)S(1)}, f32[2,1792]{1,0:T(2,128)S(1)}, u32[]{:S(2)}, u32[]{:S(2)}) collective-permute-start(f32[2,1792]{1,0:T(2,128)S(1)} %broadcast_select_fusion), channel_id=1, source_target_pairs={{0,8},{8,0},{1,9},{9,1},{2,10},{10,2},{3,11},{11,3},{4,12},{12,4},... | collective-permute-start | bytes 43016 | tf_op jit(solution)/shard_map/ppermute | solution.py:388
  384.6 6.3 copy-start.50
  384.6 7.4 %copy-start.52 = (bf16[2048,1024]{1,0:T(8,128)(2,1)S(1)}, bf16[2048,1024]{1,0:T(8,128)(2,1)}, u32[]{:S(2)}) copy-start(bf16[2048,1024]{1,0:T(8,128)(2,1)} %get-tuple-element.39) | copy-start | bytes 12582916
  390.9 96.3 %collective-permute-start.3 = (bf16[2,2,256,2048]{3,2,0,1:T(8,128)(2,1)}, bf16[2,2,256,2048]{3,2,0,1:T(8,128)(2,1)}, u32[]{:S(2)}, u32[]{:S(2)}) collective-permute-start(bf16[2,2,256,2048]{3,2,0,1:T(8,128)(2,1)} %fusion.1), channel_id=1, source_target_pairs={{0,1},{1,0},{2,3},{3,2},{4,5},{5,4},{6,7},{7,6},{8,9},{9,8},{10,11... | collective-permute-start | bytes 12582920 | tf_op jit(solution)/shard_map/ppermute | solution.py:388
  392.0 11.9 %copy-start.17 = (bf16[2,1024,256]{2,1,0:T(8,128)(2,1)S(1)}, bf16[2,1024,256]{2,1,0:T(8,128)(2,1)}, u32[]{:S(2)}) copy-start(bf16[2,1024,256]{2,1,0:T(8,128)(2,1)} %get-tuple-element.42) | copy-start | bytes 3145732
  392.0 11.9 %copy-start.22 = (bf16[8,256,256]{2,1,0:T(8,128)(2,1)S(1)}, bf16[8,256,256]{2,1,0:T(8,128)(2,1)}, u32[]{:S(2)}) copy-start(bf16[8,256,256]{2,1,0:T(8,128)(2,1)} %get-tuple-element.41) | copy-start | bytes 3145732
  412.5 19.9 %copy-start = (f32[2048,2048]{1,0:T(8,128)}, f32[2048,2048]{1,0:T(8,128)S(1)}, u32[]{:S(2)}) copy-start(f32[2048,2048]{1,0:T(8,128)S(1)} %convolution_add_fusion) | copy-start | bytes 50331652
  415.5 16.8 %copy-start.53 = (bf16[2048,1024]{1,0:T(8,128)(2,1)S(1)}, bf16[2048,1024]{1,0:T(8,128)(2,1)}, u32[]{:S(2)}) copy-start(bf16[2048,1024]{1,0:T(8,128)(2,1)} %get-tuple-element.39) | copy-start | bytes 12582916
  415.5 80.7 %collective-permute-start = (bf16[2,2,256,2048]{3,2,0,1:T(8,128)(2,1)}, bf16[2,2,256,2048]{3,2,0,1:T(8,128)(2,1)}, u32[]{:S(2)}, u32[]{:S(2)}) collective-permute-start(bf16[2,2,256,2048]{3,2,0,1:T(8,128)(2,1)} %fusion), channel_id=1, source_target_pairs={{0,1},{1,0},{2,3},{3,2},{4,5},{5,4},{6,7},{7,6},{8,9},{9,8},{10,11... | collective-permute-start | bytes 12582920 | tf_op jit(solution)/shard_map/ppermute | solution.py:388
  432.4 18.1 %copy-start.13 = (bf16[2048,1024]{1,0:T(8,128)(2,1)}, bf16[2048,1024]{1,0:T(8,128)(2,1)S(1)}, u32[]{:S(2)}) copy-start(bf16[2048,1024]{1,0:T(8,128)(2,1)S(1)} %convolution_convert_fusion.1) | copy-start | bytes 12582916
  445.5 3.7 collective-permute-start.23
  449.3 8.7 %collective-permute-start.24 = (f32[2,1792]{1,0:T(2,128)S(1)}, f32[2,1792]{1,0:T(2,128)S(1)}, u32[]{:S(2)}, u32[]{:S(2)}) collective-permute-start(f32[2,1792]{1,0:T(2,128)S(1)} %fusion.82), channel_id=1, source_target_pairs={{0,16},{16,0},{1,17},{17,1},{2,18},{18,2},{3,19},{19,3},{4,20},{20... | collective-permute-start | bytes 43016 | tf_op jit(solution)/shard_map/ppermute | solution.py:434
  456.0 16.0 %copy-start.43 = (f32[2048]{0:T(1024)S(1)}, f32[2048]{0:T(1024)}, u32[]{:S(2)}) copy-start(f32[2048]{0:T(1024)} %param.44) | copy-start | bytes 24580
  456.0 16.0 %copy-start.44 = (f32[2048]{0:T(1024)S(1)}, f32[2048]{0:T(1024)}, u32[]{:S(2)}) copy-start(f32[2048]{0:T(1024)} %param.45) | copy-start | bytes 24580
  460.1 11.9 %collective-permute-start.11 = (bf16[256,256]{1,0:T(8,128)(2,1)S(1)}, bf16[256,256]{1,0:T(8,128)(2,1)S(1)}, u32[]{:S(2)}, u32[]{:S(2)}) collective-permute-start(bf16[256,256]{1,0:T(8,128)(2,1)S(1)} %get-tuple-element.124), channel_id=1, source_target_pairs={{0,16},{8,24},{16,0},{24,8},{1,17},{9,25},{17,1},{25,9},{2,18},{10... | collective-permute-start | bytes 393224 | tf_op jit(solution)/shard_map/ppermute | solution.py:399
  462.0 10.6 %collective-permute-start.13 = (bf16[256,256]{1,0:T(8,128)(2,1)S(1)}, bf16[256,256]{1,0:T(8,128)(2,1)S(1)}, u32[]{:S(2)}, u32[]{:S(2)}) collective-permute-start(bf16[256,256]{1,0:T(8,128)(2,1)S(1)} %get-tuple-element.125), channel_id=1, source_target_pairs={{0,24},{8,16},{16,8},{24,0},{1,25},{9,17},{17,9},{25,1},{2,26},{10... | collective-permute-start | bytes 393224 | tf_op jit(solution)/shard_map/ppermute | solution.py:399
  472.0 5.0 collective-permute-start.12
  472.7 53.6 %collective-permute-start.18 = (bf16[2,2,256,1024]{3,2,1,0:T(8,128)(2,1)}, bf16[2,2,256,1024]{3,2,1,0:T(8,128)(2,1)}, u32[]{:S(2)}, u32[]{:S(2)}) collective-permute-start(bf16[2,2,256,1024]{3,2,1,0:T(8,128)(2,1)} %dynamic-slice_bitcast_fusion), channel_id=1, source_target_pairs={{0,4},{4,0},{1,5},{5,1},{2,6},{6,2},{3,7},{7,3},{8,12},{12,8},{9,1... | collective-permute-start | bytes 6291464 | tf_op jit(solution)/shard_map/ppermute | solution.py:388
  484.7 27.9 %collective-permute-start.7 = (bf16[256,768]{0,1:T(8,128)(2,1)S(1)}, bf16[256,768]{0,1:T(8,128)(2,1)S(1)}, u32[]{:S(2)}, u32[]{:S(2)}) collective-permute-start(bf16[256,768]{0,1:T(8,128)(2,1)S(1)} %get-tuple-element.110), channel_id=1, source_target_pairs={{0,16},{8,24},{16,0},{24,8},{1,17},{9,25},{17,1},{25,9},{2,18},{10... | collective-permute-start | bytes 1179656 | tf_op jit(solution)/shard_map/ppermute | solution.py:399
  486.0 27.2 %collective-permute-start.9 = (bf16[256,768]{0,1:T(8,128)(2,1)S(1)}, bf16[256,768]{0,1:T(8,128)(2,1)S(1)}, u32[]{:S(2)}, u32[]{:S(2)}) collective-permute-start(bf16[256,768]{0,1:T(8,128)(2,1)S(1)} %get-tuple-element.111), channel_id=1, source_target_pairs={{0,24},{8,16},{16,8},{24,0},{1,25},{9,17},{17,9},{25,1},{2,26},{10... | collective-permute-start | bytes 1179656 | tf_op jit(solution)/shard_map/ppermute | solution.py:399
  487.3 27.5 %collective-permute-start.8 = (bf16[256,768]{0,1:T(8,128)(2,1)S(1)}, bf16[256,768]{0,1:T(8,128)(2,1)S(1)}, u32[]{:S(2)}, u32[]{:S(2)}) collective-permute-start(bf16[256,768]{0,1:T(8,128)(2,1)S(1)} %get-tuple-element.112), channel_id=1, source_target_pairs={{0,8},{8,0},{16,24},{24,16},{1,9},{9,1},{17,25},{25,17},{2,10},{10... | collective-permute-start | bytes 1179656 | tf_op jit(solution)/shard_map/ppermute | solution.py:399
  498.2 48.9 %collective-permute-start.4 = (bf16[2,256,2048]{2,1,0:T(8,128)(2,1)}, bf16[2,256,2048]{2,1,0:T(8,128)(2,1)}, u32[]{:S(2)}, u32[]{:S(2)}) collective-permute-start(bf16[2,256,2048]{2,1,0:T(8,128)(2,1)} %fusion.22), channel_id=1, source_target_pairs={{0,2},{2,0},{1,3},{3,1},{4,6},{6,4},{5,7},{7,5},{8,10},{10,8},{9,1... | collective-permute-start | bytes 6291464 | tf_op jit(solution)/shard_map/ppermute | solution.py:388
  505.6 9.7 %copy-start.3 = (f32[2,2,256,2048]{3,2,0,1:T(8,128)}, f32[2,2,256,2048]{3,2,0,1:T(8,128)S(1)}, u32[]{:S(2)}) copy-start(f32[2,2,256,2048]{3,2,0,1:T(8,128)S(1)} %bitcast_add_fusion.1) | copy-start | bytes 25165828
  512.6 80.7 %collective-permute-start.14 = (bf16[2,2,256,1024]{3,2,1,0:T(8,128)(2,1)}, bf16[2,2,256,1024]{3,2,1,0:T(8,128)(2,1)}, u32[]{:S(2)}, u32[]{:S(2)}) collective-permute-start(bf16[2,2,256,1024]{3,2,1,0:T(8,128)(2,1)} %dynamic-slice_bitcast_fusion.1), channel_id=1, source_target_pairs={{0,4},{4,0},{1,5},{5,1},{2,6},{6,2},{3,7},{7,3},{8,12},{12,8},{9,1... | collective-permute-start | bytes 6291464 | tf_op jit(solution)/shard_map/ppermute | solution.py:388
  513.2 75.7 %collective-permute-start.1 = (bf16[2,256,2048]{2,1,0:T(8,128)(2,1)}, bf16[2,256,2048]{2,1,0:T(8,128)(2,1)}, u32[]{:S(2)}, u32[]{:S(2)}) collective-permute-start(bf16[2,256,2048]{2,1,0:T(8,128)(2,1)} %fusion.21), channel_id=1, source_target_pairs={{0,2},{2,0},{1,3},{3,1},{4,6},{6,4},{5,7},{7,5},{8,10},{10,8},{9,1... | collective-permute-start | bytes 6291464 | tf_op jit(solution)/shard_map/ppermute | solution.py:388
  529.4 61.1 %slice-start = ((s8[8388608]{0:T(1024)(128)(4,1)}), s8[4194304]{0:T(1024)(128)(4,1)S(1)}, s32[]{:S(2)}) async-start(s8[8388608]{0:T(1024)(128)(4,1)} %bitcast.234), calls=%async_computation | async-start | bytes 8388608
  529.6 68.4 %collective-permute-start.19 = (bf16[256,1024]{1,0:T(8,128)(2,1)S(1)}, bf16[256,1024]{1,0:T(8,128)(2,1)S(1)}, u32[]{:S(2)}, u32[]{:S(2)}) collective-permute-start(bf16[256,1024]{1,0:T(8,128)(2,1)S(1)} %get-tuple-element.104), channel_id=1, source_target_pairs={{0,16},{8,24},{16,0},{24,8},{1,17},{9,25},{17,1},{25,9},{2,18},{10... | collective-permute-start | bytes 1572872 | tf_op jit(solution)/shard_map/ppermute | solution.py:399
  539.0 61.7 %collective-permute-start.21 = (bf16[256,1024]{1,0:T(8,128)(2,1)S(1)}, bf16[256,1024]{1,0:T(8,128)(2,1)S(1)}, u32[]{:S(2)}, u32[]{:S(2)}) collective-permute-start(bf16[256,1024]{1,0:T(8,128)(2,1)S(1)} %get-tuple-element.105), channel_id=1, source_target_pairs={{0,24},{8,16},{16,8},{24,0},{1,25},{9,17},{17,9},{25,1},{2,26},{10... | collective-permute-start | bytes 1572872 | tf_op jit(solution)/shard_map/ppermute | solution.py:399
  547.1 43.4 %slice-start.1 = ((s8[8388608]{0:T(1024)(128)(4,1)}), s8[4194304]{0:T(1024)(128)(4,1)S(1)}, s32[]{:S(2)}) async-start(s8[8388608]{0:T(1024)(128)(4,1)} %bitcast.234), calls=%async_computation.1 | async-start | bytes 8388608
  547.1 54.8 %collective-permute-start.20 = (bf16[256,1024]{1,0:T(8,128)(2,1)S(1)}, bf16[256,1024]{1,0:T(8,128)(2,1)S(1)}, u32[]{:S(2)}, u32[]{:S(2)}) collective-permute-start(bf16[256,1024]{1,0:T(8,128)(2,1)S(1)} %get-tuple-element.106), channel_id=1, source_target_pairs={{0,8},{8,0},{16,24},{24,16},{1,9},{9,1},{17,25},{25,17},{2,10},{10... | collective-permute-start | bytes 1572872 | tf_op jit(solution)/shard_map/ppermute | solution.py:399
  589.0 37.3 %collective-permute-start.5 = (bf16[256,2048]{1,0:T(8,128)(2,1)S(1)}, bf16[256,2048]{1,0:T(8,128)(2,1)S(1)}, u32[]{:S(2)}, u32[]{:S(2)}) collective-permute-start(bf16[256,2048]{1,0:T(8,128)(2,1)S(1)} %fusion.27), channel_id=1, source_target_pairs={{0,8},{8,0},{1,9},{9,1},{2,10},{10,2},{3,11},{11,3},{4,12},{12,4},... | collective-permute-start | bytes 3145736 | tf_op jit(solution)/shard_map/ppermute | solution.py:388
  593.3 64.6 %collective-permute-start.2 = (bf16[256,2048]{1,0:T(8,128)(2,1)S(1)}, bf16[256,2048]{1,0:T(8,128)(2,1)S(1)}, u32[]{:S(2)}, u32[]{:S(2)}) collective-permute-start(bf16[256,2048]{1,0:T(8,128)(2,1)S(1)} %fusion.26), channel_id=1, source_target_pairs={{0,8},{8,0},{1,9},{9,1},{2,10},{10,2},{3,11},{11,3},{4,12},{12,4},... | collective-permute-start | bytes 3145736 | tf_op jit(solution)/shard_map/ppermute | solution.py:388
  596.7 5.7 copy-start.10
  598.0 77.4 %collective-permute-start.15 = (bf16[256,1024]{1,0:T(8,128)(2,1)}, bf16[256,1024]{1,0:T(8,128)(2,1)S(1)}, u32[]{:S(2)}, u32[]{:S(2)}) collective-permute-start(bf16[256,1024]{1,0:T(8,128)(2,1)} %get-tuple-element.107), channel_id=1, source_target_pairs={{0,16},{8,24},{16,0},{24,8},{1,17},{9,25},{17,1},{25,9},{2,18},{10... | collective-permute-start | bytes 1572872 | tf_op jit(solution)/shard_map/ppermute | solution.py:399
  600.6 74.7 %collective-permute-start.17 = (bf16[256,1024]{1,0:T(8,128)(2,1)}, bf16[256,1024]{1,0:T(8,128)(2,1)S(1)}, u32[]{:S(2)}, u32[]{:S(2)}) collective-permute-start(bf16[256,1024]{1,0:T(8,128)(2,1)} %get-tuple-element.108), channel_id=1, source_target_pairs={{0,24},{8,16},{16,8},{24,0},{1,25},{9,17},{17,9},{25,1},{2,26},{10... | collective-permute-start | bytes 1572872 | tf_op jit(solution)/shard_map/ppermute | solution.py:399
  601.9 24.4 %copy-start.2 = (bf16[256,2048]{1,0:T(8,128)(2,1)S(1)}, bf16[256,2048]{1,0:T(8,128)(2,1)}, u32[]{:S(2)}) copy-start(bf16[256,2048]{1,0:T(8,128)(2,1)} %param.26) | copy-start | bytes 3145732
  601.9 24.4 %copy-start.27 = (f32[1,2048]{1,0:T(1,128)S(1)}, f32[1,2048]{1,0:T(1,128)}, u32[]{:S(2)}) copy-start(f32[1,2048]{1,0:T(1,128)} %copy-done.26) | copy-start | bytes 24580
  601.9 24.4 %copy-start.33 = (f32[256]{0:T(256)S(1)}, f32[256]{0:T(256)}, u32[]{:S(2)}) copy-start(f32[256]{0:T(256)} %copy-done.32) | copy-start | bytes 3076
  601.9 24.4 %copy-start.38 = (f32[256]{0:T(256)S(1)}, f32[256]{0:T(256)}, u32[]{:S(2)}) copy-start(f32[256]{0:T(256)} %copy-done.37) | copy-start | bytes 3076
  601.9 73.5 %collective-permute-start.16 = (bf16[256,1024]{1,0:T(8,128)(2,1)}, bf16[256,1024]{1,0:T(8,128)(2,1)}, u32[]{:S(2)}, u32[]{:S(2)}) collective-permute-start(bf16[256,1024]{1,0:T(8,128)(2,1)} %get-tuple-element.109), channel_id=1, source_target_pairs={{0,8},{8,0},{16,24},{24,16},{1,9},{9,1},{17,25},{25,17},{2,10},{10... | collective-permute-start | bytes 1572872 | tf_op jit(solution)/shard_map/ppermute | solution.py:399
  602.4 24.8 %copy-start.40 = (f32[256]{0:T(256)S(1)}, f32[256]{0:T(256)}, u32[]{:S(2)}) copy-start(f32[256]{0:T(256)} %copy-done.39) | copy-start | bytes 3076
  602.4 55.5 %copy-start.30 = (f32[1,2048]{1,0:T(1,128)S(1)}, f32[1,2048]{1,0:T(1,128)}, u32[]{:S(2)}) copy-start(f32[1,2048]{1,0:T(1,128)} %get-tuple-element.129) | copy-start | bytes 24580
  602.4 55.5 %copy-start.31 = (f32[1,2048]{1,0:T(1,128)S(1)}, f32[1,2048]{1,0:T(1,128)}, u32[]{:S(2)}) copy-start(f32[1,2048]{1,0:T(1,128)} %get-tuple-element.132) | copy-start | bytes 24580
  661.8 4.7 collective-permute-start.25
  666.5 8.1 %collective-permute-start.26 = (f32[3,2048]{1,0:T(4,128)S(1)}, f32[3,2048]{1,0:T(4,128)S(1)}, u32[]{:S(2)}, u32[]{:S(2)}) collective-permute-start(f32[3,2048]{1,0:T(4,128)S(1)} %fusion.43), channel_id=1, source_target_pairs={{0,2},{2,0},{1,3},{3,1},{4,6},{6,4},{5,7},{7,5},{8,10},{10,8},{9,1... | collective-permute-start | bytes 73736 | tf_op jit(solution)/shard_map/ppermute | solution.py:388
  674.6 4.0 collective-permute-start.27
  678.6 4.0 collective-permute-start.28
  678.7 6.6 copy-start.19
  679.0 6.3 copy-start.9
  679.0 6.3 copy-start.18
  682.6 6.8 collective-permute-start.29
  (22 other events, 64.1 us)

commit v2 on v1

v2 whole, which is shorter than its diff:
```python
import functools
import math

import jax
import jax.numpy as jnp
import numpy as np
from jax import lax
from jax.experimental import pallas as pl
from jax.experimental.pallas import tpu as pltpu
from jax.sharding import Mesh
from jax.sharding import PartitionSpec as P

HEAD = 64
ROT = 32
STEP = 10

BETA_ONE = 0.9
BETA_TWO = 0.999
ADAM_EPS = 1e-08
MATRIX_DECAY = 0.1
VECTOR_RATE = 0.1

F32 = jnp.float32
BF16 = jnp.bfloat16
MESH = pl.DeviceIdType.MESH
ANY = pl.BlockSpec(memory_space=pl.ANY)
VMEM_LIMIT = 63 * 1024 * 1024


CHUNK = 256
TILE_SLOTS = 4
NT = (((1,), (1,)), ((), ()))
TN = (((0,), (0,)), ((), ()))


def at(index, size):
    return pl.ds(pl.multiple_of(index * size, size), size)


def block_kernel(
    n_zh,
    n_in, c_in, down_own, down_other, up_own, up_other, dense_own, dense_other, qkv_own, qkv_other,
    hidden_bias, head_bias, cos_ref, sin_ref,
    z_mlp, z_dense, z_qkv, y_mlp, y_dense, y_qkv, rows_in, grad_out, branch_out, hidden_sum, head_sum,
    rows2, mlp_w, dense_w, qkv_w, units2, heads3, heads1,
    dq_s, dk_s, dv_s, s_s, p_s,
    y_stage, z_stage, qkv_stage, dense_stage, tile_stage, load_s, wide_s, turned_s,
    w_send, w_recv, fwd_send, fwd_recv, a_send, a_recv, local_sem,
    ym_send, ym_recv, zm_send, zm_recv, yd_send, yd_recv, zd_send, zd_recv,
    yq_send, yq_recv, zq_send, zq_recv, tile_send, tile_recv, load_sem, wide_sem,
):
    zh, zp, y = lax.axis_index("zh"), lax.axis_index("zp"), lax.axis_index("y")
    x, c = lax.axis_index("x"), lax.axis_index("c")
    mp = x * 2 + c
    n = 2 * n_zh
    tok_rows, width = n_in.shape
    bw = up_own.shape[0]
    units = up_own.shape[1]
    half_width = dense_own.shape[1]
    seq = 4 * tok_rows
    half = width // 2
    lanes = 2 * HEAD
    count = seq // CHUNK
    scale = HEAD ** (-0.5)

    def step(i):
        back = n - 1 - i
        if isinstance(back, int):
            return back // 2, back % 2
        return lax.div(back, 2), lax.rem(back, 2)

    def source_block(i):
        s, f = step(i)
        return lax.rem(zh - s + n_zh, n_zh) * 4 + (zp ^ f) * 2 + y

    def target(i):
        s, f = step(i)
        return {"zh": lax.rem(zh + s, n_zh), "zp": zp ^ f}

    def target_block(i):
        s, f = step(i)
        return lax.rem(zh + s, n_zh) * 4 + (zp ^ f) * 2

    to_y, to_x, to_c, to_zp = {"y": 1 - y}, {"x": 1 - x}, {"c": 1 - c}, {"zp": 1 - zp}
    barrier = pltpu.get_barrier_semaphore()
    partners = [target(i) for i in range(n - 1)] + [to_y, to_x, to_c]
    for partner in partners:
        pl.semaphore_signal(barrier, inc=1, device_id=partner, device_id_type=MESH)
    pl.semaphore_wait(barrier, len(partners))

    def remote(src, dst, send, recv, to):
        return pltpu.make_async_remote_copy(
            src_ref=src, dst_ref=dst, send_sem=send, recv_sem=recv, device_id=to, device_id_type=MESH
        )


    me = source_block(n - 1)
    halves = ((down_own, down_other), (up_own, up_other), (dense_own, dense_other), (qkv_own, qkv_other))

    def place(w, b):
        if w < 2:
            return mlp_w.at[w, at(b, bw), :]
        return (dense_w, qkv_w)[w - 2].at[at(b, bw), :]

    started = []

    def go(copy):
        copy.start()
        started.append(copy)

    def z_copy(w, i):
        return remote(halves[w][step(i)[1]], place(w, me), w_send.at[w, i], w_recv.at[w, i], target(i))

    def y_copy(w, i):
        b = source_block(i)
        src = halves[w][0] if i == n - 1 else place(w, b)
        return remote(src, place(w, b), fwd_send.at[w, i], fwd_recv.at[w, i], to_y)

    own_rows = (c_in, n_in)

    def act_copy(k, stage, part):
        if stage == 0:
            slot, to, row, column = 0, to_zp, zp, mp
        else:
            row = zp ^ (part % 2)
            column = mp if part < 2 else (1 - x) * 2 + c
            slot, to = (1 + part, to_x) if stage == 1 else (3 + part, to_c)
        spot = rows2.at[k, at(row * 4 + column, tok_rows), :]
        src = own_rows[k] if stage == 0 or part == 0 else spot
        return remote(src, spot, a_send.at[k, slot], a_recv.at[k, slot], to)

    def locals_():
        copies = [
            pltpu.make_async_copy(own_rows[k], rows2.at[k, at(zp * 4 + mp, tok_rows), :], local_sem.at[k])
            for k in (0, 1)
        ]
        return copies + [
            pltpu.make_async_copy(halves[w][0], place(w, me), local_sem.at[2 + w]) for w in range(4)
        ]

    go(act_copy(1, 0, 0))
    go(act_copy(1, 1, 0))
    for i in range(n - 1):
        go(z_copy(1, i))
    go(y_copy(1, n - 1))
    go(act_copy(0, 0, 0))
    go(act_copy(0, 1, 0))
    for i in range(n - 1):
        go(z_copy(0, i))
    go(y_copy(0, n - 1))
    go(act_copy(1, 2, 0))
    go(act_copy(0, 2, 0))
    for w in (3, 2):
        for i in range(n - 1):
            go(z_copy(w, i))
    for copy in locals_():
        copy.start()

    def pass_on(k, stage, part):
        act_copy(k, stage, part).wait_recv()
        if stage == 0:
            go(act_copy(k, 1, 1))
            go(act_copy(k, 2, 1))
        else:
            go(act_copy(k, 2, 2 + part))

    def forward(w, i):
        z_copy(w, i).wait_recv()
        go(y_copy(w, i))

    pass_on(1, 0, 0)
    for i in range(n - 1):
        forward(1, i)
    pass_on(1, 1, 0)
    pass_on(0, 0, 0)
    pass_on(1, 1, 1)
    for i in range(n - 1):
        forward(0, i)
    pass_on(0, 1, 0)
    pass_on(0, 1, 1)
    go(y_copy(3, n - 1))
    go(y_copy(2, n - 1))
    for copy in locals_():
        copy.wait()
    for k in (1, 0):
        for part in range(4):
            act_copy(k, 2, part).wait_recv()
    for w in (1, 0):
        for i in range(n):
            y_copy(w, i).wait_recv()


    hidden_sum[...] = jnp.zeros_like(hidden_sum)
    events = [(w, i) for w in (3, 2) for i in range(n - 1)]
    tiles = 2 * seq // CHUNK

    def mlp_tile(r, carry):
        rows = at(r, CHUNK)
        for j in range(units // CHUNK):
            cols = pl.ds(j * CHUNK, CHUNK)
            hidden = jnp.dot(rows2[1, rows, :], mlp_w[1, :, cols], preferred_element_type=F32)
            hidden = hidden + hidden_bias[:, cols]
            grad = jnp.dot(rows2[0, rows, :], mlp_w[0, :, cols], preferred_element_type=F32)
            k0 = math.sqrt(2.0 / math.pi)
            square = hidden * hidden
            tanh = jnp.tanh(k0 * (hidden * (1.0 + 0.044715 * square)))
            units2[0, rows, cols] = (0.5 * hidden * (1.0 + tanh)).astype(BF16)
            slope = 0.5 * (1.0 + tanh) + 0.5 * hidden * (1.0 - tanh * tanh) * (
                k0 * (1.0 + 3.0 * 0.044715 * square)
            )
            low = (grad * slope).astype(BF16)
            units2[1, rows, cols] = low
            hidden_sum[:, cols] += jnp.sum(low.astype(F32), axis=0, keepdims=True)
        for r_at in range(tiles):
            mine = [e for k, e in enumerate(events) if min(k + 1, tiles - 1) == r_at]
            if mine:
                @pl.when(r == r_at)
                def _():
                    for w, i in mine:
                        z_copy(w, i).wait_recv()
                        y_copy(w, i).start()
        return carry

    lax.fori_loop(0, tiles, mlp_tile, 0)
    started.extend(y_copy(w, i) for w, i in events)


    def weight_grad(left, right, b, put):
        wide = max(bw, 128)
        turned = turned_s.at[pl.ds(0, wide), :]
        if bw == wide:
            turned[...] = left[:, at(b, bw)].T
        else:
            turned[...] = left[:, at(lax.div(b, wide // bw), wide)].T
        for j in range(right.shape[1] // CHUNK):
            cols = pl.ds(j * CHUNK, CHUNK)
            value = jnp.dot(turned[...], right[:, cols], preferred_element_type=F32)
            if bw < wide:
                spot = lax.rem(b, wide // bw)
                value = sum(
                    jnp.where(spot == k, value[k * bw : (k + 1) * bw], 0.0) for k in range(wide // bw)
                )
            put(cols, value)

    def mlp_grad(w, b, put):
        weight_grad(rows2.at[w], units2.at[w], b, put)

    def ym_copy(k):
        w, i = lax.div(k, n), lax.rem(k, n)
        return remote(y_stage.at[k], y_mlp.at[w, i], ym_send.at[k], ym_recv.at[k], to_y)

    def ym_step(k, carry):
        w, i = lax.div(k, n), lax.rem(k, n)

        def put(cols, value):
            y_stage[k, :, cols] = value.astype(BF16)

        mlp_grad(w, target_block(i) + 1 - y, put)
        ym_copy(k).start()
        return carry

    lax.fori_loop(0, 2 * n, ym_step, 0)

    def zm_copy(k):
        w, i = lax.div(k, n), lax.rem(k, n)
        return remote(z_stage.at[i], z_mlp.at[w, i], zm_send.at[i], zm_recv.at[k], target(i))

    def zm_local(k):
        w, i = lax.div(k, n), lax.rem(k, n)
        return pltpu.make_async_copy(z_stage.at[i], z_mlp.at[w, i], zm_send.at[i])

    def zm_step(k, carry):
        w, i = lax.div(k, n), lax.rem(k, n)
        ym_copy(k).wait_recv()
        load = pltpu.make_async_copy(y_mlp.at[w, i], load_s.at[0, pl.ds(0, bw), :], load_sem.at[0])
        load.start()

        @pl.when((k >= n) & (i < n - 1))
        def _():
            zm_copy(k - n).wait_send()

        @pl.when((k >= n) & (i == n - 1))
        def _():
            zm_local(k - n).wait()

        load.wait()

        def put(cols, value):
            z_stage[i, :, cols] = (value + load_s[0, pl.ds(0, bw), cols].astype(F32)).astype(BF16)

        mlp_grad(w, target_block(i) + y, put)

        @pl.when(i < n - 1)
        def _():
            zm_copy(k).start()

        @pl.when(i == n - 1)
        def _():
            zm_local(k).start()

        return carry


    for w in (3, 2):
        for i in range(n):
            y_copy(w, i).wait_recv()
    low_lane = lax.broadcasted_iota(jnp.int32, (1, lanes), 1) % HEAD < ROT // 2

    def turn(values, rows, sign):
        after = pltpu.roll(values, lanes - ROT // 2, 1)
        before = pltpu.roll(values, ROT // 2, 1)
        return values * cos_ref[rows, :] + jnp.where(low_lane, after, before) * (sign * sin_ref[rows, :])

    def proj_tile(r, carry):
        rows = at(r, CHUNK)
        where = at(lax.rem(r, count), CHUNK)
        for t in range(3):
            cols = pl.ds(t * half_width, half_width)
            proj = jnp.dot(rows2[1, rows, :], qkv_w[:, cols], preferred_element_type=F32) + head_bias[:, cols]
            for g in range(half_width // lanes):
                part = proj[:, g * lanes : (g + 1) * lanes]
                if t < 2:
                    part = turn(part, where, 1.0)
                heads3[rows, pl.ds(t * half_width + g * lanes, lanes)] = part.astype(BF16)
        heads1[rows, :] = jnp.dot(rows2[0, rows, :], dense_w[...], preferred_element_type=F32).astype(BF16)
        return carry

    lax.fori_loop(0, tiles, proj_tile, 0)


    first = lax.broadcasted_iota(jnp.int32, (1, lanes), 1) < HEAD
    pairs = half_width // lanes

    def attend(it, carry):
        base = lax.div(it, pairs) * count
        hp = lax.rem(it, pairs)

        def cols(t):
            return at(t * pairs + hp, lanes)

        here = at(hp, lanes)
        dk_s[...] = jnp.zeros_like(dk_s)
        dv_s[...] = jnp.zeros_like(dv_s)
        diagonal = lax.broadcasted_iota(jnp.int32, (CHUNK, CHUNK), 0) <= lax.broadcasted_iota(
            jnp.int32, (CHUNK, CHUNK), 1
        )
        for qb in range(count):
            rows = at(base + qb, CHUNK)
            q_rows = heads3[rows, cols(0)] * jnp.asarray(scale, BF16)
            g_rows = heads1[rows, here]
            mixed_halves, dq_halves = [], []
            for h in (0, 1):
                mine = first if h == 0 else jnp.logical_not(first)
                q_one = jnp.where(mine, q_rows, jnp.zeros_like(q_rows))
                g_one = jnp.where(mine, g_rows, jnp.zeros_like(g_rows))
                top = None
                for j in range(qb + 1):
                    keys = heads3[at(base + j, CHUNK), cols(1)]
                    scores = lax.dot_general(keys, q_one, NT, preferred_element_type=F32)
                    if j == qb:
                        scores = jnp.where(diagonal, scores, -1e30)
                    s_s[j] = scores
                    peak = jnp.max(scores, axis=0, keepdims=True)
                    top = peak if top is None else jnp.maximum(top, peak)
                total = None
                for j in range(qb + 1):
                    e = jnp.exp(s_s[j] - top)
                    s_s[j] = e
                    part = jnp.sum(e, axis=0, keepdims=True)
                    total = part if total is None else total + part
                inverse = 1.0 / total
                mixed, inner = None, None
                for j in range(qb + 1):
                    values = heads3[at(base + j, CHUNK), cols(2)]
                    probs = s_s[j] * inverse
                    low = probs.astype(BF16)
                    part = lax.dot_general(low, values, TN, preferred_element_type=F32)
                    mixed = part if mixed is None else mixed + part
                    dv_s[h, pl.ds(j * CHUNK, CHUNK), :] += jnp.dot(low, g_rows, preferred_element_type=F32)
                    grad_probs = lax.dot_general(values, g_one, NT, preferred_element_type=F32)
                    s_s[j] = probs
                    p_s[j] = grad_probs
                    part = jnp.sum(probs * grad_probs, axis=0, keepdims=True)
                    inner = part if inner is None else inner + part
                dq = None
                for j in range(qb + 1):
                    keys = heads3[at(base + j, CHUNK), cols(1)]
                    grad_scores = (s_s[j] * (p_s[j] - inner)).astype(BF16)
                    part = lax.dot_general(grad_scores, keys, TN, preferred_element_type=F32)
                    dq = part if dq is None else dq + part
                    dk_s[h, pl.ds(j * CHUNK, CHUNK), :] += jnp.dot(
                        grad_scores, q_rows, preferred_element_type=F32
                    )
                mixed_halves.append(mixed)
                dq_halves.append(dq)
            heads1[rows, here] = jnp.where(first, *mixed_halves).astype(BF16)
            dq_s[pl.ds(qb * CHUNK, CHUNK), :] = jnp.where(first, *dq_halves) * scale
        for qb in range(count):
            rows = pl.ds(qb * CHUNK, CHUNK)
            gq = turn(dq_s[rows, :], rows, -1.0)
            gk = turn(jnp.where(first, dk_s[0, rows, :], dk_s[1, rows, :]), rows, -1.0)
            gv = jnp.where(first, dv_s[0, rows, :], dv_s[1, rows, :])
            for t, g in enumerate((gq, gk, gv)):
                low = g.astype(BF16)
                heads3[at(base + qb, CHUNK), cols(t)] = low
                head_sum[:, cols(t)] += jnp.sum(low.astype(F32), axis=0, keepdims=True)
        per = n // 4
        lax.fori_loop(it * per, (it + 1) * per, zm_step, 0)
        return carry

    head_sum[...] = jnp.zeros_like(head_sum)
    lax.fori_loop(0, 2 * pairs, attend, 0)


    def small(left, right, y_buf, z_buf, stage, ys, yr, zs, zr):
        cols = stage.shape[2]

        def y_copy_(i):
            return remote(stage.at[i], y_buf.at[i], ys.at[i], yr.at[i], to_y)

        def z_copy_(i):
            return remote(stage.at[i], z_buf.at[i], zs.at[i], zr.at[i], target(i))

        def z_local(i):
            return pltpu.make_async_copy(stage.at[i], z_buf.at[i], zs.at[i])

        def y_step(i, carry):
            def put(at_cols, value):
                stage[i, :, at_cols] = value.astype(BF16)

            weight_grad(left, right, target_block(i) + 1 - y, put)
            y_copy_(i).start()
            return carry

        def z_step(i, carry):
            y_copy_(i).wait_recv()
            spot = load_s.at[0, pl.ds(0, bw), pl.ds(0, cols)]
            load = pltpu.make_async_copy(y_buf.at[i], spot, load_sem.at[0])
            load.start()
            y_copy_(i).wait_send()
            load.wait()

            def put(at_cols, value):
                stage[i, :, at_cols] = (value + spot[:, at_cols].astype(F32)).astype(BF16)

            weight_grad(left, right, target_block(i) + y, put)

            @pl.when(i < n - 1)
            def _():
                z_copy_(i).start()

            @pl.when(i == n - 1)
            def _():
                z_local(i).start()

            return carry

        def finish(i, carry):
            @pl.when(i < n - 1)
            def _():
                z_copy_(i).wait_send()
                z_copy_(i).wait_recv()

            @pl.when(i == n - 1)
            def _():
                z_local(i).wait()

            return carry

        return y_step, z_step, finish

    dense_steps = small(
        rows2.at[0], heads1, y_dense, z_dense, dense_stage, yd_send, yd_recv, zd_send, zd_recv
    )
    qkv_steps = small(
        rows2.at[1], heads3, y_qkv, z_qkv, qkv_stage, yq_send, yq_recv, zq_send, zq_recv
    )


    def tile_copy(kind, slot, index, to):
        return remote(
            tile_stage.at[slot], rows_in.at[kind, index], tile_send.at[slot],
            tile_recv.at[kind, index], to,
        )

    def row_tiles(kind, stage, base, total):
        left, left_w = units2.at[1 - kind], mlp_w.at[1 - kind]
        right, right_w = ((heads3, qkv_w), (heads1, dense_w))[kind]

        def one(t, carry):
            h = lax.rem(t, 2)
            if stage == 0:
                zq, xq = lax.div(t, 4), lax.rem(lax.div(t, 2), 2)
                block, come, to, index = zq * 4 + xq * 2 + 1 - c, (), to_c, t
            elif stage == 1:
                zq = lax.div(t, 2)
                block, to, index = zq * 4 + (1 - x) * 2 + c, to_x, 8 + t
                come = (zq * 4 + (1 - x) * 2 + h,)
            elif stage == 2:
                block, to, index = (1 - zp) * 4 + x * 2 + c, to_zp, 12 + h
                come = ((1 - zp) * 4 + x * 2 + h, 8 + (1 - zp) * 2 + h)
            else:
                block, to, index = zp * 4 + x * 2 + c, None, None
                come = (zp * 4 + x * 2 + h, 8 + zp * 2 + h, 12 + h)
            loads = []
            for slot, (spot, back) in enumerate(zip(come, (to_c, to_x, to_zp))):
                tile_copy(kind, 0, spot, back).wait_recv()
                loads.append(
                    pltpu.make_async_copy(rows_in.at[kind, spot], load_s.at[slot], load_sem.at[slot])
                )
                loads[-1].start()
            for load in loads:
                load.wait()
            rows = at(block, tok_rows)
            if stage < 3:
                slot = lax.rem(base + t, TILE_SLOTS)

                @pl.when(base + t >= TILE_SLOTS)
                def _():
                    tile_copy(kind, slot, index, to).wait_send()

            for j in range(half // CHUNK):
                cols = pl.ds(j * CHUNK, CHUNK)
                model = at(h * (half // CHUNK) + j, CHUNK)
                value = lax.dot_general(left[rows, :], left_w[model, :], NT, preferred_element_type=F32)
                value += lax.dot_general(right[rows, :], right_w[model, :], NT, preferred_element_type=F32)
                for k in range(len(loads)):
                    value += load_s[k, :, cols].astype(F32)
                if stage < 3:
                    tile_stage[slot, :, cols] = value.astype(BF16)
                else:
                    wide_s[:, cols] = value
            if stage < 3:
                tile_copy(kind, slot, index, to).start()
            else:
                out = (grad_out, branch_out)[kind]
                copy = pltpu.make_async_copy(wide_s, out.at[:, at(h, half)], wide_sem)
                copy.start()
                copy.wait()
            return carry

        lax.fori_loop(0, total, one, 0)

    lax.fori_loop(0, n, dense_steps[0], 0)
    lax.fori_loop(0, n, qkv_steps[0], 0)
    per = n // 4
    lax.fori_loop(n, n + per, zm_step, 0)
    row_tiles(0, 0, 0, 8)
    lax.fori_loop(n + per, n + 2 * per, zm_step, 0)
    row_tiles(1, 0, 8, 8)
    lax.fori_loop(n + 2 * per, n + 3 * per, zm_step, 0)
    row_tiles(0, 1, 16, 4)
    lax.fori_loop(n + 3 * per, 2 * n, zm_step, 0)
    row_tiles(1, 1, 20, 4)
    lax.fori_loop(0, n, dense_steps[1], 0)
    row_tiles(0, 2, 24, 2)
    lax.fori_loop(0, n, qkv_steps[1], 0)
    row_tiles(1, 2, 26, 2)
    row_tiles(0, 3, 0, 2)
    row_tiles(1, 3, 0, 2)


    for copy in started:
        copy.wait_send()

    def finish_y(k, carry):
        ym_copy(k).wait_send()
        return carry

    def finish_z(k, carry):
        i = lax.rem(k, n)

        @pl.when(i < n - 1)
        def _():
            zm_copy(k).wait_recv()

        @pl.when((k >= n) & (i < n - 1))
        def _():
            zm_copy(k).wait_send()

        @pl.when((k >= n) & (i == n - 1))
        def _():
            zm_local(k).wait()

        return carry

    lax.fori_loop(0, 2 * n, finish_y, 0)
    lax.fori_loop(0, 2 * n, finish_z, 0)
    for slot in range(TILE_SLOTS):
        tile_copy(0, slot, 0, to_c).wait_send()
    lax.fori_loop(0, n, dense_steps[2], 0)
    lax.fori_loop(0, n, qkv_steps[2], 0)


def block(n_zh, normed, cotangent, halves, hidden_bias, head_bias, tables):
    tok_rows, width = normed.shape
    n = 2 * n_zh
    dp = 2 * n
    bw = width // dp
    units = halves[2].shape[1]
    half_width = halves[4].shape[1]
    triple = 3 * half_width
    seq = 4 * tok_rows
    count = seq // CHUNK
    shape = jax.ShapeDtypeStruct
    vmem = pl.BlockSpec(memory_space=pltpu.VMEM)
    dma = pltpu.SemaphoreType.DMA
    outs = [
        shape((2, n, bw, units), BF16),
        shape((n, bw, half_width), BF16),
        shape((n, bw, triple), BF16),
        shape((2, n, bw, units), BF16),
        shape((n, bw, half_width), BF16),
        shape((n, bw, triple), BF16),
        shape((2, 14, tok_rows, width // 2), BF16),
        shape((tok_rows, width), F32),
        shape((tok_rows, width), F32),
        shape((1, units), F32),
        shape((1, triple), F32),
    ]
    scratch = [
        pltpu.VMEM((2, 2 * seq, width), BF16),
        pltpu.VMEM((2, width, units), BF16),
        pltpu.VMEM((width, half_width), BF16),
        pltpu.VMEM((width, triple), BF16),
        pltpu.VMEM((2, 2 * seq, units), BF16),
        pltpu.VMEM((2 * seq, triple), BF16),
        pltpu.VMEM((2 * seq, half_width), BF16),
        pltpu.VMEM((seq, 2 * HEAD), F32),
        pltpu.VMEM((2, seq, 2 * HEAD), F32),
        pltpu.VMEM((2, seq, 2 * HEAD), F32),
        pltpu.VMEM((count, CHUNK, CHUNK), F32),
        pltpu.VMEM((count, CHUNK, CHUNK), F32),
        pltpu.VMEM((2 * n, bw, units), BF16),
        pltpu.VMEM((n, bw, units), BF16),
        pltpu.VMEM((n, bw, triple), BF16),
        pltpu.VMEM((n, bw, half_width), BF16),
        pltpu.VMEM((TILE_SLOTS, tok_rows, width // 2), BF16),
        pltpu.VMEM((3, tok_rows, width // 2), BF16),
        pltpu.VMEM((tok_rows, width // 2), F32),
        pltpu.VMEM((max(bw, 128), 2 * seq), BF16),
        dma((4, n)), dma((4, n)), dma((4, n)), dma((4, n)), dma((2, 7)), dma((2, 7)), dma((6,)),
        dma((2 * n,)), dma((2 * n,)), dma((n,)), dma((2 * n,)),
        dma((n,)), dma((n,)), dma((n,)), dma((n,)),
        dma((n,)), dma((n,)), dma((n,)), dma((n,)),
        dma((TILE_SLOTS,)), dma((2, 14)), dma((3,)), dma,
    ]
    return pl.pallas_call(
        functools.partial(block_kernel, n_zh),
        out_shape=outs,
        in_specs=[ANY] * 10 + [vmem] * 4,
        out_specs=[ANY] * 9 + [vmem] * 2,
        scratch_shapes=scratch,
        compiler_params=pltpu.CompilerParams(
            collective_id=0, has_side_effects=True, vmem_limit_bytes=VMEM_LIMIT
        ),
    )(normed, cotangent, *halves, hidden_bias, head_bias, *tables)


def rotation_tables(seq):
    lane = np.arange(2 * HEAD) % HEAD
    exponent = (lane % (ROT // 2)).astype(np.float32) * np.float32(2.0 / ROT)
    inverse = jnp.exp(-math.log(10000.0) * jnp.asarray(exponent))
    angles = jnp.arange(seq, dtype=F32)[:, None] * inverse[None, :]
    cos, sin = jnp.cos(angles), jnp.sin(angles)
    turned = jnp.asarray(lane < ROT)[None, :]
    low = jnp.asarray(lane < ROT // 2)[None, :]
    return jnp.where(turned, cos, 1.0), jnp.where(turned, jnp.where(low, -sin, sin), 0.0)


def normalize(inputs, scales, offsets):
    average = jnp.mean(inputs, axis=-1, keepdims=True)
    centred = inputs - average
    variance = jnp.mean(centred * centred, axis=-1, keepdims=True)
    return centred * lax.rsqrt(variance + 1e-05) * scales + offsets


def adam_update(weight, moment_one, moment_two, gradient, step_rate, decay_rate):
    first_new = BETA_ONE * moment_one + (1.0 - BETA_ONE) * gradient
    second_new = BETA_TWO * moment_two + (1.0 - BETA_TWO) * gradient * gradient
    normalized = (
        first_new
        / (1.0 - BETA_ONE**STEP)
        / (jnp.sqrt(second_new / (1.0 - BETA_TWO**STEP)) + ADAM_EPS)
    )
    return (weight - step_rate * (normalized + decay_rate * weight), first_new, second_new)


def flip(value, name):
    return lax.ppermute(value, name, [(0, 1), (1, 0)])


def pick(value, index, axis):
    return lax.dynamic_index_in_dim(value, index, axis, keepdims=False)


def owner_sum(parts, n_zh):
    zp = lax.axis_index("zp")
    wide = parts.astype(F32)
    mine = sum(wide[2 * n_zh - 1 - 2 * s] for s in range(n_zh))
    theirs = sum(wide[2 * n_zh - 2 - 2 * s] for s in range(n_zh))
    low = jnp.where(zp == 0, mine, theirs)
    high = jnp.where(zp == 0, theirs, mine)
    return jnp.stack([low, high], axis=1)


def sum_over(value, n_zh, names):
    for name in names:
        if name == "zh":
            step = 1
            while step < n_zh:
                value = value + lax.ppermute(value, "zh", [(i, i ^ step) for i in range(n_zh)])
                step *= 2
        else:
            value = value + flip(value, name)
    return value


def local(
    n_zh,
    tokens, cotangent,
    qkv_weight, qkv_first, qkv_second,
    dense_weight, dense_first, dense_second,
    up_weight, up_first, up_second,
    down_weight, down_first, down_second,
    head_bias, head_first, head_second,
    hidden_bias, hidden_first, hidden_second,
    outer_params, outer_first, outer_second,
):
    zp = lax.axis_index("zp")
    tok_rows, width = tokens.shape
    seq_rows = tok_rows * 4
    bw = qkv_weight.shape[1]
    local_width = qkv_weight.shape[2]
    half_width = local_width // 2
    half_units = up_weight.shape[1] // 2

    tokens_wide = tokens.astype(F32)
    normed, norm_back = jax.vjp(normalize, tokens_wide, outer_params[0], outer_params[1])

    qkv_rows = jnp.moveaxis(qkv_weight, 0, 1).reshape(bw, 3, 2, half_width)
    qkv_rows = jnp.moveaxis(qkv_rows, 2, 1).reshape(bw, 2, 3 * half_width).astype(BF16)
    dense_rows = dense_weight.T.reshape(bw, 2, half_width).astype(BF16)
    up_rows = up_weight.reshape(bw, 2, half_units).astype(BF16)
    down_rows = down_weight.T.reshape(bw, 2, half_units).astype(BF16)
    halves = []
    for rows in (down_rows, up_rows, dense_rows, qkv_rows):
        halves += [pick(rows, zp, 1), pick(rows, 1 - zp, 1)]
    bias_half = pick(hidden_bias.reshape(2, 1, half_units), zp, 0)
    head_half = pick(head_bias.reshape(3, 2, half_width), zp, 1).reshape(1, 3 * half_width)
    outs = block(
        n_zh, normed.astype(BF16), cotangent, halves, bias_half, head_half, rotation_tables(seq_rows)
    )
    z_mlp, z_dense, z_qkv = outs[:3]
    grad_normed, branch, hidden_part, head_part = outs[7:]
    down_sum = owner_sum(z_mlp[0], n_zh)
    up_sum = owner_sum(z_mlp[1], n_zh)
    dense_sum = owner_sum(z_dense, n_zh)
    qkv_sum = owner_sum(z_qkv, n_zh)
    layer_out = (tokens_wide + branch + outer_params[2] + outer_params[3]).astype(BF16)

    input_part, gain_grad, shift_grad = norm_back(grad_normed)
    back_wide = cotangent.astype(F32)
    input_grad = back_wide + input_part
    out_bias_grad = jnp.sum(back_wide, axis=0)

    vectors = jnp.concatenate(
        [hidden_part.reshape(half_units), head_part.reshape(3 * half_width)]
    )
    both = jnp.where(
        jnp.arange(2)[:, None] == zp, vectors[None, :], jnp.zeros_like(vectors)[None, :]
    )
    both = sum_over(both, n_zh, ("zp", "y", "zh"))
    hidden_sum = both[:, :half_units].reshape(2 * half_units)
    head_sum = jnp.moveaxis(both[:, half_units:].reshape(2, 3, half_width), 0, 1).reshape(
        3, local_width
    )
    outer_sum = sum_over(
        jnp.stack([gain_grad, shift_grad, out_bias_grad]), n_zh, ("c", "x", "y", "zp", "zh")
    )
    outer_sum = jnp.concatenate([outer_sum, outer_sum[2:]], axis=0)

    model = width
    qkv_sum = qkv_sum.reshape(bw, 2, 3, half_width)
    qkv_sum = jnp.moveaxis(qkv_sum, 2, 0).reshape(3, bw, local_width)
    dense_sum = dense_sum.reshape(bw, local_width).T
    up_sum = up_sum.reshape(bw, 2 * half_units)
    down_sum = down_sum.reshape(bw, 2 * half_units).T
    new_qkv = adam_update(
        qkv_weight, qkv_first, qkv_second, qkv_sum, (model // 2) ** (-0.5), MATRIX_DECAY
    )
    new_dense = adam_update(
        dense_weight, dense_first, dense_second, dense_sum, (model // 16) ** (-0.5), MATRIX_DECAY
    )
    new_up = adam_update(up_weight, up_first, up_second, up_sum, model ** (-0.5), MATRIX_DECAY)
    new_down = adam_update(
        down_weight, down_first, down_second, down_sum, (4 * model) ** (-0.5), MATRIX_DECAY
    )
    new_head = adam_update(head_bias, head_first, head_second, head_sum, VECTOR_RATE, 0.0)
    new_hidden = adam_update(
        hidden_bias, hidden_first, hidden_second, hidden_sum, VECTOR_RATE, 0.0
    )
    new_outer = adam_update(outer_params, outer_first, outer_second, outer_sum, VECTOR_RATE, 0.0)
    return (
        layer_out,
        input_grad,
        *new_qkv,
        *new_dense,
        *new_up,
        *new_down,
        *new_head,
        *new_hidden,
        *new_outer,
    )


def solution(mesh):
    n_zh = mesh.shape["dp"] // 4
    split = Mesh(mesh.devices.reshape(n_zh, 2, 2, 2, 2), ("zh", "zp", "y", "x", "c"))
    dp, mp = ("zh", "zp", "y"), ("x", "c")
    rows = P(dp + mp, None)
    qkv, dense, up, down = P(None, dp, mp), P(mp, dp), P(dp, mp), P(mp, dp)
    rest = (qkv,) * 3 + (dense,) * 3 + (up,) * 3 + (down,) * 3
    rest += (P(None, mp),) * 3 + (P(mp),) * 3 + (P(),) * 3
    return jax.shard_map(
        functools.partial(local, n_zh),
        mesh=split,
        in_specs=(rows, rows) + rest,
        out_specs=(rows, rows) + rest,
        check_vma=False,
    )
```

time: 699 us -> 542 us (0.78)
  Pallas kernels: 288 us -> 412 us
  waiting for transfers between devices: 123 us -> 9.39 us
  matrix products: 113 us -> 0 us
  starting transfers between devices: 37 us -> 11.9 us
  other arithmetic: 65.5 us -> 43 us
  local copies, waits for them, and re-layouts: 62.2 us -> 53.5 us
    pallas_call x3 -> x1, Pallas kernels: 288 us -> 412 us  [block(): pl.pallas_call(functools.partial(block_kernel, n_zh), out_shape=outs, in_...]
    dot_general x10 -> x0, matrix products: 113 us -> none  [the longest x4 46.2 us: weight_grad(): lax.dot_general(left, right, tn, preferred_element_type=F32).astype(BF16)]
    ppermute x16 -> x6, waiting for transfers between devices: 105 us -> 8.11 us  [flip(): return lax.ppermute(value, name, [(0, 1), (1, 0)])]
    ppermute x12 -> x0, starting transfers between devices: 21.8 us -> none  [z_send(): return lax.ppermute(value, ('zh', 'zp'), pairs)]
    add x4 -> x0, other arithmetic: 18.2 us -> none  [the longest x2 11.9 us: reduce_rows(): pick(value, c, 2)]
    ppermute x12 -> x0, waiting for transfers between devices: 17.2 us -> none  [z_send(): return lax.ppermute(value, ('zh', 'zp'), pairs)]
    convert_element_type x6 -> x0, local copies, waits for them, and re-layouts: 13.5 us -> none  [the longest x2 9.37 us: reduce_rows(): pick(value, 1 - c, 2).astype(BF16)]
    unnamed x127 -> x100, local copies, waits for them, and re-layouts: 24.4 us -> 36.8 us
  transfers between devices with their start and end apart: 30 -> 8, of which waited for: 10 -> 4; matrix products, arithmetic and copies ran while one was open for 27% -> 11% of each run, Pallas kernels for 4% -> 0%
where the time goes in v2:
time: 542 us; the launch traced here: 532 us
  Pallas kernels  412 us (76%)
  local copies, waits for them, and re-layouts  53.5 us (10%)
  other arithmetic  43 us (8%)
  starting transfers between devices  11.9 us (2%)
  waiting for transfers between devices  9.39 us (2%)
    pallas_call x1, Pallas kernels, block(): pl.pallas_call(functools.partial(block_kernel, n_zh), out_shape=outs, in_...  412 us
    unnamed x100, local copies, waits for them, and re-layouts  36.8 us
    sub x7, other arithmetic, adam_update(): weight - step_rate * (normalized + decay_rate * weight)  17.7 us
  transfers between devices with their start and end apart: 8, of which 4 were waited for; matrix products, arithmetic and copies ran while one was open for 11% of the time, Pallas kernels for 0%

profile of v2, /device:TPU:0, one launch (start us, length us, event | category | flops | bytes accessed | tf_op | source)
XLA Modules:
  0.0 531.8 jit_solution(599996526715484413)
XLA Ops:
  0.7 1.7 convert_element_type.70
  2.4 0.8 convert_element_type.71
  3.2 1.9 copy.85
  5.2 3.5 constant_dynamic-slice_fusion.4
  8.7 0.8 constant_dynamic-slice_fusion
  9.5 1.9 copy.87
  11.4 0.9 copy.88
  12.6 1.0 copy.110
  13.6 1.0 copy.111
  14.6 1.2 convert_element_type.72
  15.9 0.8 copy.114
  16.6 0.8 copy.115
  17.4 0.6 copy.116
  18.0 0.6 dynamic-slice_bitcast_fusion.1.hidden_bias
  18.8 0.4 fusion.9
  19.3 1.3 copy_bitcast_fusion
  20.7 1.4 fusion.7.n_in
  22.1 2.9 fusion.20
  25.0 412.3 %shard_map.425 = (bf16[2,4,256,1024]{3,2,1,0:T(8,128)(2,1)}, bf16[4,256,256]{2,1,0:T(8,128)(2,1)}, bf16[4,256,768]{2,1,0:T(8,128)(2,1)}, bf16[2,4,256,1024]{3,2,...) custom-call(bf16[256,2048]{1,0:T(8,128)(2,1)} %fusion.7.n_in, ...), custom_call_target="tpu_custom_call" | custom-call | tf_op jit(solution)/shard_map/pallas_call | solution.py:648
  437.3 2.5 fusion.10
  439.8 0.3 copy-done.2
  440.1 1.0 fusion.8
  441.2 0.6 copy-done.22
  441.8 3.3 convert_reduce_fusion.1
  445.3 5.9 %collective-permute-start = (f32[2,1792]{1,0:T(2,128)S(1)}, f32[2,1792]{1,0:T(2,128)S(1)}, u32[]{:S(2)}, u32[]{:S(2)}) collective-permute-start(f32[2,1792]{1,0:T(2,128)S(1)} %broadcast_select_fusion.2), channel_id=1, source_target_pairs={{0,8},{8,0},{1,9},{9,1},{2,10},{10,2},{3,11},{11,3},{4,12},{12,4},... | collective-permute-start | bytes 43016 | tf_op jit(solution)/shard_map/ppermute | solution.py:690
  451.2 1.8 copy.102
  453.0 5.0 slice_convert_fusion
  458.0 0.4 select_bitcast_fusion.1
  458.6 1.9 copy.103
  460.5 2.6 select_bitcast_fusion.3
  463.2 1.8 copy.99
  465.0 3.1 copy.100
  468.1 2.0 copy.98
  470.3 1.2 copy-done.24
  472.8 1.2 copy.93
  474.0 0.7 copy-done.23
  474.7 1.6 copy.90
  476.3 3.2 copy.94
  479.6 6.7 %multiply_subtract_fusion = (f32[2048,256]{1,0:T(8,128)}, f32[2048,256]{1,0:T(8,128)}, f32[2048,256]{1,0:T(8,128)}) fusion(f32[2048,256]{1,0:T(8,128)S(1)} %copy-done.6, f32[256,2,1024]{0,2,1:T(8,128)} %copy.103, f32[2048,256]{1,0:T(8,128)} %param.38, f32[2048,256]{1,0:T(8,128)} %param.39), kind=kLoop, calls=%fused_computation.31 | loop fusion | flops 7864320 | bytes 14680064 | tf_op jit(solution)/shard_map/sub | solution.py:686
  486.3 2.9 multiply_subtract_fusion.2
  489.3 0.9 copy-done.8
  490.2 0.6 copy-done.9
  490.8 0.6 copy-done.10
  491.5 3.6 multiply_subtract_fusion.1
  495.0 0.8 pad_maximum_fusion.2
  495.8 1.2 copy.97
  497.2 0.6 collective-permute-start.1
  497.8 1.6 collective-permute-start.4
  499.4 1.5 collective-permute-done.1
  501.0 2.6 multiply_subtract_fusion.3
  503.7 2.9 copy.107
  506.5 2.9 copy.108
  509.4 1.8 copy.109
  511.2 3.1 copy.104
  514.4 1.6 copy.105
  516.0 1.6 copy.106
  517.7 0.6 collective-permute-start.5
  518.4 0.6 multiply_subtract_fusion.6
  519.0 2.7 collective-permute-done.5
  521.8 3.9 collective-permute-done.6
  525.7 3.0 collective-permute-start.7
  528.7 0.6 multiply_subtract_fusion.5
  529.3 1.3 collective-permute-done.7
  530.6 0.7 multiply_subtract_fusion.4
  (118 shorter events, 3.0 us)
Async XLA Ops:
  5.1 3.6 copy-start.3
  8.7 3.6 copy-start.5
  12.6 4.8 copy-start.29
  12.6 5.4 %copy-start.30 = (f32[2048]{0:T(1024)S(1)}, f32[2048]{0:T(1024)}, u32[]{:S(2)}) copy-start(f32[2048]{0:T(1024)} %param.43) | copy-start | bytes 24580
  12.6 6.0 %copy-start = (bf16[256,2048]{1,0:T(8,128)(2,1)S(1)}, bf16[256,2048]{1,0:T(8,128)(2,1)}, u32[]{:S(2)}) copy-start(bf16[256,2048]{1,0:T(8,128)(2,1)} %param.26) | copy-start | bytes 3145732
  14.6 4.6 copy-start.26
  14.6 4.7 copy-start.17
  14.6 4.7 copy-start.18
  19.3 2.8 copy-start.37
  19.3 2.8 copy-start.38
  19.3 2.8 copy-start.39
  437.2 2.6 copy-start.1
  437.2 2.9 copy-start.2
  439.8 1.4 copy-start.19
  439.8 2.0 copy-start.22
  441.8 3.4 copy-start.36
  441.8 3.4 copy-start.35
  441.8 9.4 %copy-start.11 = (f32[256,2048]{1,0:T(8,128)S(1)}, f32[256,2048]{1,0:T(8,128)}, u32[]{:S(2)}) copy-start(f32[256,2048]{1,0:T(8,128)} %param.34) | copy-start | bytes 6291460
  445.1 52.7 %collective-permute-start.3 = (f32[3,2048]{1,0:T(4,128)S(1)}, f32[3,2048]{1,0:T(4,128)S(1)}, u32[]{:S(2)}, u32[]{:S(2)}) collective-permute-start(f32[3,2048]{1,0:T(4,128)S(1)} %pad_maximum_fusion.3), channel_id=1, source_target_pairs={{0,1},{1,0},{2,3},{3,2},{4,5},{5,4},{6,7},{7,6},{8,9},{9,8},{10,11... | collective-permute-start | bytes 73736 | tf_op jit(solution)/shard_map/ppermute | solution.py:690
  445.3 51.8 %collective-permute-start = (f32[2,1792]{1,0:T(2,128)S(1)}, f32[2,1792]{1,0:T(2,128)S(1)}, u32[]{:S(2)}, u32[]{:S(2)}) collective-permute-start(f32[2,1792]{1,0:T(2,128)S(1)} %broadcast_select_fusion.2), channel_id=1, source_target_pairs={{0,8},{8,0},{1,9},{9,1},{2,10},{10,2},{3,11},{11,3},{4,12},{12,4},... | collective-permute-start | bytes 43016 | tf_op jit(solution)/shard_map/ppermute | solution.py:690
  465.0 3.1 copy-start.21
  468.1 2.1 copy-start.25
  470.1 1.4 copy-start.24
  472.8 2.0 copy-start.23
  476.3 3.2 copy-start.6
  479.5 6.7 %copy-start.4 = (f32[3,256,512]{1,2,0:T(8,128)S(1)}, f32[3,256,512]{1,2,0:T(8,128)}, u32[]{:S(2)}) copy-start(f32[3,256,512]{1,2,0:T(8,128)} %copy-done.3) | copy-start | bytes 4718596
  479.5 6.7 %copy-start.14 = (f32[3,256,2,256]{1,3,2,0:T(8,128)S(1)}, f32[3,256,2,256]{1,3,2,0:T(8,128)}, u32[]{:S(2)}) copy-start(f32[3,256,2,256]{1,3,2,0:T(8,128)} %copy.93) | copy-start | bytes 4718596
  479.5 6.7 %copy-start.15 = (f32[3,256,512]{1,2,0:T(8,128)S(1)}, f32[3,256,512]{1,2,0:T(8,128)}, u32[]{:S(2)}) copy-start(f32[3,256,512]{1,2,0:T(8,128)} %copy.90) | copy-start | bytes 4718596
  479.6 6.7 %copy-start.16 = (f32[3,256,512]{1,2,0:T(8,128)S(1)}, f32[3,256,512]{1,2,0:T(8,128)}, u32[]{:S(2)}) copy-start(f32[3,256,512]{1,2,0:T(8,128)} %copy.94) | copy-start | bytes 4718596
  486.3 3.0 copy-start.7
  486.3 3.9 copy-start.8
  486.3 4.5 copy-start.9
  486.3 5.1 copy-start.10
  495.0 6.0 %copy-start.20 = (f32[512,256]{1,0:T(8,128)S(1)}, f32[512,256]{1,0:T(8,128)}, u32[]{:S(2)}) copy-start(f32[512,256]{1,0:T(8,128)} %param.31) | copy-start | bytes 1572868
  497.2 3.7 collective-permute-start.1
  497.8 19.9 %collective-permute-start.4 = (f32[3,2048]{1,0:T(4,128)S(1)}, f32[3,2048]{1,0:T(4,128)S(1)}, u32[]{:S(2)}, u32[]{:S(2)}) collective-permute-start(f32[3,2048]{1,0:T(4,128)S(1)} %fusion.29), channel_id=1, source_target_pairs={{0,2},{2,0},{1,3},{3,1},{4,6},{6,4},{5,7},{7,5},{8,10},{10,8},{9,1... | collective-permute-start | bytes 73736 | tf_op jit(solution)/shard_map/ppermute | solution.py:690
  501.0 16.7 %collective-permute-start.2 = (f32[2,1792]{1,0:T(2,128)S(1)}, f32[2,1792]{1,0:T(2,128)S(1)}, u32[]{:S(2)}, u32[]{:S(2)}) collective-permute-start(f32[2,1792]{1,0:T(2,128)S(1)} %fusion.45), channel_id=1, source_target_pairs={{0,16},{16,0},{1,17},{17,1},{2,18},{18,2},{3,19},{19,3},{4,20},{20... | collective-permute-start | bytes 43016 | tf_op jit(solution)/shard_map/ppermute | solution.py:712
  511.2 3.1 copy-start.13
  514.4 1.7 copy-start.12
  516.0 2.4 copy-start.31
  516.0 2.4 copy-start.32
  516.0 12.7 %copy-start.33 = (f32[2048]{0:T(1024)S(1)}, f32[2048]{0:T(1024)}, u32[]{:S(2)}) copy-start(f32[2048]{0:T(1024)} %param.44) | copy-start | bytes 24580
  516.0 12.7 %copy-start.34 = (f32[2048]{0:T(1024)S(1)}, f32[2048]{0:T(1024)}, u32[]{:S(2)}) copy-start(f32[2048]{0:T(1024)} %param.45) | copy-start | bytes 24580
  516.0 14.6 %copy-start.27 = (f32[4,2048]{1,0:T(4,128)S(1)}, f32[4,2048]{1,0:T(4,128)}, u32[]{:S(2)}) copy-start(f32[4,2048]{1,0:T(4,128)} %param.47) | copy-start | bytes 98308
  516.0 14.6 %copy-start.28 = (f32[4,2048]{1,0:T(4,128)S(1)}, f32[4,2048]{1,0:T(4,128)}, u32[]{:S(2)}) copy-start(f32[4,2048]{1,0:T(4,128)} %param.48) | copy-start | bytes 98308
  517.7 4.0 collective-permute-start.5
  521.7 4.0 collective-permute-start.6
  525.7 4.9 collective-permute-start.7

commit v3 on v2

--- a/solution.py
+++ b/solution.py
@@ -28,7 +28,7 @@
 
 
 CHUNK = 256
-TILE_SLOTS = 4
+RING = 2
 NT = (((1,), (1,)), ((), ()))
 TN = (((0,), (0,)), ((), ()))
 
@@ -39,24 +39,23 @@
 
 def block_kernel(
     n_zh,
-    n_in, c_in, down_own, down_other, up_own, up_other, dense_own, dense_other, qkv_own, qkv_other,
-    hidden_bias, head_bias, cos_ref, sin_ref,
-    z_mlp, z_dense, z_qkv, y_mlp, y_dense, y_qkv, rows_in, grad_out, branch_out, hidden_sum, head_sum,
+    tok_in, c_in, down_in, up_in, dense_in, qkv_in,
+    outer_ref, hidden_bias, head_bias, cos_ref, sin_ref,
+    z_mlp, z_dense, z_qkv, y_mlp, y_dense, y_qkv, rows_in, grad_out, branch_out, sums_ref,
     rows2, mlp_w, dense_w, qkv_w, units2, heads3, heads1,
-    dq_s, dk_s, dv_s, s_s, p_s,
-    y_stage, z_stage, qkv_stage, dense_stage, tile_stage, load_s, wide_s, turned_s,
+    dq_s, dk_s, dv_s, s_s, p_s, tok_s, stat_s, hidden_sum, head_sum, vec_s, vec_in,
+    y_stage, z_stage, qkv_stage, dense_stage, tile_stage, load_s, turned_s,
     w_send, w_recv, fwd_send, fwd_recv, a_send, a_recv, local_sem,
     ym_send, ym_recv, zm_send, zm_recv, yd_send, yd_recv, zd_send, zd_recv,
-    yq_send, yq_recv, zq_send, zq_recv, tile_send, tile_recv, load_sem, wide_sem,
+    yq_send, yq_recv, zq_send, zq_recv, tile_send, tile_recv, x_send, load_sem, wide_sem, vec_send, vec_recv,
 ):
     zh, zp, y = lax.axis_index("zh"), lax.axis_index("zp"), lax.axis_index("y")
     x, c = lax.axis_index("x"), lax.axis_index("c")
     mp = x * 2 + c
     n = 2 * n_zh
-    tok_rows, width = n_in.shape
-    bw = up_own.shape[0]
-    units = up_own.shape[1]
-    half_width = dense_own.shape[1]
+    tok_rows, width = tok_in.shape
+    _, bw, units = up_in.shape
+    half_width = dense_in.shape[2]
     seq = 4 * tok_rows
     half = width // 2
     lanes = 2 * HEAD
@@ -86,6 +85,9 @@
     partners = [target(i) for i in range(n - 1)] + [to_y, to_x, to_c]
     for partner in partners:
         pl.semaphore_signal(barrier, inc=1, device_id=partner, device_id_type=MESH)
+    own = at(zp * 4 + mp, tok_rows)
+    tok_load = pltpu.make_async_copy(tok_in, tok_s, load_sem.at[0])
+    tok_load.start()
     pl.semaphore_wait(barrier, len(partners))
 
     def remote(src, dst, send, recv, to):
@@ -95,12 +97,15 @@
 
 
     me = source_block(n - 1)
-    halves = ((down_own, down_other), (up_own, up_other), (dense_own, dense_other), (qkv_own, qkv_other))
-
-    def place(w, b):
+    halves = (down_in, up_in, dense_in, qkv_in)
+
+    pieces = (4, 4, 2, 4) if n_zh == 2 else (1, 1, 1, 1)
+
+    def place(w, b, k=0, m=1):
+        spot = at(b * m + k, bw // m)
         if w < 2:
-            return mlp_w.at[w, at(b, bw), :]
-        return (dense_w, qkv_w)[w - 2].at[at(b, bw), :]
+            return mlp_w.at[w, spot, :]
+        return (dense_w, qkv_w)[w - 2].at[spot, :]
 
     started = []
 
@@ -108,15 +113,25 @@
         copy.start()
         started.append(copy)
 
-    def z_copy(w, i):
-        return remote(halves[w][step(i)[1]], place(w, me), w_send.at[w, i], w_recv.at[w, i], target(i))
-
-    def y_copy(w, i):
+    def z_copy(w, i, k):
+        m = pieces[w]
+        src = halves[w].at[zp ^ step(i)[1], pl.ds(k * (bw // m), bw // m), :]
+        return remote(src, place(w, me, k, m), w_send.at[w, i, k], w_recv.at[w, i, k], target(i))
+
+    def y_copy(w, i, k=0):
         b = source_block(i)
-        src = halves[w][0] if i == n - 1 else place(w, b)
-        return remote(src, place(w, b), fwd_send.at[w, i], fwd_recv.at[w, i], to_y)
-
-    own_rows = (c_in, n_in)
+        if i == n - 1:
+            return remote(halves[w].at[zp], place(w, b), fwd_send.at[w, i, 0], fwd_recv.at[w, i, 0], to_y)
+        spot = place(w, b, k, pieces[w])
+        return remote(spot, spot, fwd_send.at[w, i, k], fwd_recv.at[w, i, k], to_y)
+
+    def y_arrived(w):
+        for i in range(n - 1):
+            for k in range(pieces[w]):
+                y_copy(w, i, k).wait_recv()
+        y_copy(w, n - 1).wait_recv()
+
+    own_rows = (c_in, rows2.at[1, own, :])
 
     def act_copy(k, stage, part):
         if stage == 0:
@@ -130,31 +145,9 @@
         return remote(src, spot, a_send.at[k, slot], a_recv.at[k, slot], to)
 
     def locals_():
-        copies = [
-            pltpu.make_async_copy(own_rows[k], rows2.at[k, at(zp * 4 + mp, tok_rows), :], local_sem.at[k])
-            for k in (0, 1)
+        return [pltpu.make_async_copy(c_in, rows2.at[0, own, :], local_sem.at[0])] + [
+            pltpu.make_async_copy(halves[w].at[zp], place(w, me), local_sem.at[1 + w]) for w in range(4)
         ]
-        return copies + [
-            pltpu.make_async_copy(halves[w][0], place(w, me), local_sem.at[2 + w]) for w in range(4)
-        ]
-
-    go(act_copy(1, 0, 0))
-    go(act_copy(1, 1, 0))
-    for i in range(n - 1):
-        go(z_copy(1, i))
-    go(y_copy(1, n - 1))
-    go(act_copy(0, 0, 0))
-    go(act_copy(0, 1, 0))
-    for i in range(n - 1):
-        go(z_copy(0, i))
-    go(y_copy(0, n - 1))
-    go(act_copy(1, 2, 0))
-    go(act_copy(0, 2, 0))
-    for w in (3, 2):
-        for i in range(n - 1):
-            go(z_copy(w, i))
-    for copy in locals_():
-        copy.start()
 
     def pass_on(k, stage, part):
         act_copy(k, stage, part).wait_recv()
@@ -164,34 +157,84 @@
         else:
             go(act_copy(k, 2, 2 + part))
 
-    def forward(w, i):
-        z_copy(w, i).wait_recv()
-        go(y_copy(w, i))
-
+    inner = zh != zp if n_zh == 2 else zh < 0
+    outer = jnp.logical_not(inner)
+
+    def send_step(w, i, k):
+        if i == 0:
+            pl.when(outer)(z_copy(w, i, k).start)
+        else:
+            z_copy(w, i, k).start()
+
+    def forward(w, i, k):
+        z_copy(w, i, k).wait_recv()
+        y_copy(w, i, k).start()
+
+    def forward_step(w, i, k):
+        if i == 0:
+            pl.when(outer)(lambda: forward(w, i, k))
+        else:
+            forward(w, i, k)
+
+    order = [(w, k) for w in (1, 0, 3, 2) for k in range(pieces[w])]
+    later = list(range(n - 2, -1, -1))
+    go(act_copy(0, 1, 0))
+    tok_load.wait()
+    for j in range(tok_rows // 64):
+        rows = pl.ds(j * 64, 64)
+        values = tok_s[rows, :].astype(F32)
+        mean = jnp.mean(values, axis=-1, keepdims=True)
+        centred = values - mean
+        inverse = lax.rsqrt(jnp.mean(centred * centred, axis=-1, keepdims=True) + 1e-05)
+        stat_s[0, rows, :] = mean
+        stat_s[1, rows, :] = inverse
+        normed = centred * inverse * outer_ref[0:1, :] + outer_ref[1:2, :]
+        rows2[1, at((zp * 4 + mp) * (tok_rows // 64) + j, 64), :] = normed.astype(BF16)
+    go(act_copy(1, 0, 0))
+    go(act_copy(0, 0, 0))
+    go(act_copy(1, 1, 0))
+    go(act_copy(1, 2, 0))
+    go(act_copy(0, 2, 0))
+    for w in (1, 0, 3, 2):
+        go(y_copy(w, n - 1))
+
+    @pl.when(inner)
+    def _():
+        for w, k in order:
+            z_copy(w, 0, k).start()
+
+    for copy in locals_():
+        copy.start()
     pass_on(1, 0, 0)
-    for i in range(n - 1):
-        forward(1, i)
+    pl.when(inner)(lambda: forward(1, 0, 0))
+    pass_on(0, 0, 0)
+    for w, k in order:
+        for i in later:
+            send_step(w, i, k)
+
+    @pl.when(inner)
+    def _():
+        for w, k in order[1:]:
+            forward(w, 0, k)
+
     pass_on(1, 1, 0)
-    pass_on(0, 0, 0)
-    pass_on(1, 1, 1)
-    for i in range(n - 1):
-        forward(0, i)
     pass_on(0, 1, 0)
-    pass_on(0, 1, 1)
-    go(y_copy(3, n - 1))
-    go(y_copy(2, n - 1))
+    for w, extra in ((1, 1), (0, 0)):
+        for k in range(pieces[w]):
+            for i in later:
+                forward_step(w, i, k)
+        pass_on(extra, 1, 1)
     for copy in locals_():
         copy.wait()
     for k in (1, 0):
         for part in range(4):
             act_copy(k, 2, part).wait_recv()
-    for w in (1, 0):
-        for i in range(n):
-            y_copy(w, i).wait_recv()
+    y_arrived(1)
+    y_arrived(0)
 
 
     hidden_sum[...] = jnp.zeros_like(hidden_sum)
-    events = [(w, i) for w in (3, 2) for i in range(n - 1)]
+    events = [(w, i, k) for w in (3, 2) for k in range(pieces[w]) for i in later]
     tiles = 2 * seq // CHUNK
 
     def mlp_tile(r, carry):
@@ -212,17 +255,19 @@
             units2[1, rows, cols] = low
             hidden_sum[:, cols] += jnp.sum(low.astype(F32), axis=0, keepdims=True)
         for r_at in range(tiles):
-            mine = [e for k, e in enumerate(events) if min(k + 1, tiles - 1) == r_at]
+            mine = [e for k, e in enumerate(events) if k * (tiles - 2) // len(events) == r_at]
             if mine:
                 @pl.when(r == r_at)
                 def _():
-                    for w, i in mine:
-                        z_copy(w, i).wait_recv()
-                        y_copy(w, i).start()
+                    for event in mine:
+                        forward_step(*event)
         return carry
 
     lax.fori_loop(0, tiles, mlp_tile, 0)
-    started.extend(y_copy(w, i) for w, i in events)
+    for w in range(4):
+        for i in range(n - 1):
+            for k in range(pieces[w]):
+                started.extend([z_copy(w, i, k), y_copy(w, i, k)])
 
 
     def weight_grad(left, right, b, put):
@@ -247,13 +292,13 @@
 
     def ym_copy(k):
         w, i = lax.div(k, n), lax.rem(k, n)
-        return remote(y_stage.at[k], y_mlp.at[w, i], ym_send.at[k], ym_recv.at[k], to_y)
+        return remote(y_stage.at[at(k, bw), :], y_mlp.at[w, i], ym_send.at[k], ym_recv.at[k], to_y)
 
     def ym_step(k, carry):
         w, i = lax.div(k, n), lax.rem(k, n)
 
         def put(cols, value):
-            y_stage[k, :, cols] = value.astype(BF16)
+            y_stage[at(k, bw), cols] = value.astype(BF16)
 
         mlp_grad(w, target_block(i) + 1 - y, put)
         ym_copy(k).start()
@@ -301,9 +346,8 @@
         return carry
 
 
-    for w in (3, 2):
-        for i in range(n):
-            y_copy(w, i).wait_recv()
+    y_arrived(3)
+    y_arrived(2)
     low_lane = lax.broadcasted_iota(jnp.int32, (1, lanes), 1) % HEAD < ROT // 2
 
     def turn(values, rows, sign):
@@ -477,12 +521,20 @@
     )
 
 
-    def tile_copy(kind, slot, index, to):
+    def ring_copy(kind, slot, index, to):
         return remote(
             tile_stage.at[slot], rows_in.at[kind, index], tile_send.at[slot],
             tile_recv.at[kind, index], to,
         )
 
+    def x_slot(kind, t):
+        return tile_stage.at[RING + t] if kind else y_stage.at[at(t, tok_rows), :]
+
+    def x_copy(kind, t, index):
+        return remote(
+            x_slot(kind, t), rows_in.at[kind, index], x_send.at[kind, t], tile_recv.at[kind, index], to_x
+        )
+
     def row_tiles(kind, stage, base, total):
         left, left_w = units2.at[1 - kind], mlp_w.at[1 - kind]
         right, right_w = ((heads3, qkv_w), (heads1, dense_w))[kind]
@@ -490,11 +542,11 @@
         def one(t, carry):
             h = lax.rem(t, 2)
             if stage == 0:
-                zq, xq = lax.div(t, 4), lax.rem(lax.div(t, 2), 2)
-                block, come, to, index = zq * 4 + xq * 2 + 1 - c, (), to_c, t
+                zq, xq = zp ^ (1 - lax.rem(lax.div(t, 2), 2)), x ^ (1 - lax.div(t, 4))
+                block, come, to, index = zq * 4 + xq * 2 + 1 - c, (), to_c, zq * 4 + xq * 2 + h
             elif stage == 1:
-                zq = lax.div(t, 2)
-                block, to, index = zq * 4 + (1 - x) * 2 + c, to_x, 8 + t
+                zq = zp ^ (1 - lax.div(t, 2))
+                block, to, index = zq * 4 + (1 - x) * 2 + c, to_x, 8 + zq * 2 + h
                 come = (zq * 4 + (1 - x) * 2 + h,)
             elif stage == 2:
                 block, to, index = (1 - zp) * 4 + x * 2 + c, to_zp, 12 + h
@@ -504,7 +556,7 @@
                 come = (zp * 4 + x * 2 + h, 8 + zp * 2 + h, 12 + h)
             loads = []
             for slot, (spot, back) in enumerate(zip(come, (to_c, to_x, to_zp))):
-                tile_copy(kind, 0, spot, back).wait_recv()
+                ring_copy(kind, 0, spot, back).wait_recv()
                 loads.append(
                     pltpu.make_async_copy(rows_in.at[kind, spot], load_s.at[slot], load_sem.at[slot])
                 )
@@ -512,13 +564,16 @@
             for load in loads:
                 load.wait()
             rows = at(block, tok_rows)
-            if stage < 3:
-                slot = lax.rem(base + t, TILE_SLOTS)
-
-                @pl.when(base + t >= TILE_SLOTS)
+            if stage in (0, 2):
+                slot = lax.rem(base + t, RING)
+                spot, copy = tile_stage.at[slot], ring_copy(kind, slot, index, to)
+
+                @pl.when(base + t >= RING)
                 def _():
-                    tile_copy(kind, slot, index, to).wait_send()
-
+                    copy.wait_send()
+
+            elif stage == 1:
+                spot, copy = x_slot(kind, t), x_copy(kind, t, index)
             for j in range(half // CHUNK):
                 cols = pl.ds(j * CHUNK, CHUNK)
                 model = at(h * (half // CHUNK) + j, CHUNK)
@@ -527,46 +582,96 @@
                 for k in range(len(loads)):
                     value += load_s[k, :, cols].astype(F32)
                 if stage < 3:
-                    tile_stage[slot, :, cols] = value.astype(BF16)
+                    spot[:, cols] = value.astype(BF16)
                 else:
-                    wide_s[:, cols] = value
+                    s_s[j] = value
+                    if kind == 0:
+                        xhat = (tok_s[:, model].astype(F32) - stat_s[0]) * stat_s[1]
+                        back = rows2[0, own, model].astype(F32)
+                        for row, term in enumerate((value * xhat, value, back)):
+                            vec_s[row : row + 1, model] = jnp.sum(term, axis=0, keepdims=True)
             if stage < 3:
-                tile_copy(kind, slot, index, to).start()
+                copy.start()
             else:
                 out = (grad_out, branch_out)[kind]
-                copy = pltpu.make_async_copy(wide_s, out.at[:, at(h, half)], wide_sem)
-                copy.start()
-                copy.wait()
+                copies = [
+                    pltpu.make_async_copy(
+                        s_s.at[j], out.at[:, at(h * (half // CHUNK) + j, CHUNK)], wide_sem.at[j]
+                    )
+                    for j in range(half // CHUNK)
+                ]
+                for copy in copies:
+                    copy.start()
+                for copy in copies:
+                    copy.wait()
             return carry
 
         lax.fori_loop(0, total, one, 0)
-
-    lax.fori_loop(0, n, dense_steps[0], 0)
-    lax.fori_loop(0, n, qkv_steps[0], 0)
-    per = n // 4
-    lax.fori_loop(n, n + per, zm_step, 0)
-    row_tiles(0, 0, 0, 8)
-    lax.fori_loop(n + per, n + 2 * per, zm_step, 0)
-    row_tiles(1, 0, 8, 8)
-    lax.fori_loop(n + 2 * per, n + 3 * per, zm_step, 0)
-    row_tiles(0, 1, 16, 4)
-    lax.fori_loop(n + 3 * per, 2 * n, zm_step, 0)
-    row_tiles(1, 1, 20, 4)
-    lax.fori_loop(0, n, dense_steps[1], 0)
-    row_tiles(0, 2, 24, 2)
-    lax.fori_loop(0, n, qkv_steps[1], 0)
-    row_tiles(1, 2, 26, 2)
-    row_tiles(0, 3, 0, 2)
-    row_tiles(1, 3, 0, 2)
-
-
-    for copy in started:
-        copy.wait_send()
 
     def finish_y(k, carry):
         ym_copy(k).wait_send()
         return carry
 
+
+    hops = [to_zp, to_y]
+    bit = 1
+    while bit < n_zh:
+        hops.append({"zh": zh ^ bit})
+        bit *= 2
+    dp_hops = len(hops)
+    hops += [to_c, to_x]
+
+    def vec_copy(k):
+        return remote(vec_s, vec_in.at[k], vec_send.at[k], vec_recv.at[k], hops[k])
+
+    def vec_first():
+        for row in (3, 4):
+            vec_s[row : row + 1, :] = jnp.zeros((1, width), F32)
+        vec_s[3:4, at(zp, units)] = hidden_sum[...]
+        for t in range(3):
+            vec_s[4:5, at(t * 2 + zp, half_width)] = head_sum[:, pl.ds(t * half_width, half_width)]
+        vec_copy(0).start()
+
+    def vec_next(k):
+        vec_copy(k).wait()
+        vec_s[...] += vec_in[k]
+        if k + 1 == dp_hops:
+            sums_ref[3:5, :] = vec_s[3:5, :]
+        if k + 1 < len(hops):
+            vec_copy(k + 1).start()
+        else:
+            sums_ref[0:3, :] = vec_s[0:3, :]
+
+    per = n // 4
+    row_tiles(0, 0, 0, 8)
+    lax.fori_loop(0, n, finish_y, 0)
+    row_tiles(0, 1, 0, 4)
+    lax.fori_loop(n, n + per, zm_step, 0)
+    row_tiles(1, 0, 8, 8)
+    lax.fori_loop(n + per, n + 2 * per, zm_step, 0)
+    row_tiles(1, 1, 0, 4)
+    lax.fori_loop(0, n, dense_steps[0], 0)
+    lax.fori_loop(0, n, qkv_steps[0], 0)
+    row_tiles(0, 2, 16, 2)
+    lax.fori_loop(n + 2 * per, 2 * n, zm_step, 0)
+    lax.fori_loop(0, n, dense_steps[1], 0)
+    lax.fori_loop(0, n // 2, qkv_steps[1], 0)
+    row_tiles(1, 2, 18, 2)
+    row_tiles(0, 3, 0, 2)
+    vec_first()
+    lax.fori_loop(n // 2, n // 2 + per, qkv_steps[1], 0)
+    vec_next(0)
+    vec_next(1)
+    lax.fori_loop(n // 2 + per, n, qkv_steps[1], 0)
+    for k in range(2, len(hops) - 1):
+        vec_next(k)
+    row_tiles(1, 3, 0, 2)
+    vec_next(len(hops) - 1)
+
+
+    for copy in started:
+        copy.wait_send()
+
     def finish_z(k, carry):
         i = lax.rem(k, n)
 
@@ -584,24 +689,28 @@
 
         return carry
 
-    lax.fori_loop(0, 2 * n, finish_y, 0)
+    lax.fori_loop(n, 2 * n, finish_y, 0)
     lax.fori_loop(0, 2 * n, finish_z, 0)
-    for slot in range(TILE_SLOTS):
-        tile_copy(0, slot, 0, to_c).wait_send()
+    for slot in range(RING):
+        ring_copy(0, slot, 0, to_c).wait_send()
+    for kind in (0, 1):
+        for t in range(4):
+            x_copy(kind, t, 0).wait_send()
     lax.fori_loop(0, n, dense_steps[2], 0)
     lax.fori_loop(0, n, qkv_steps[2], 0)
 
 
-def block(n_zh, normed, cotangent, halves, hidden_bias, head_bias, tables):
-    tok_rows, width = normed.shape
+def block(n_zh, tokens, cotangent, halves, outer_params, hidden_bias, head_bias, tables):
+    tok_rows, width = tokens.shape
     n = 2 * n_zh
     dp = 2 * n
     bw = width // dp
-    units = halves[2].shape[1]
-    half_width = halves[4].shape[1]
+    units = halves[1].shape[2]
+    half_width = halves[2].shape[2]
     triple = 3 * half_width
     seq = 4 * tok_rows
     count = seq // CHUNK
+    hops = 4 + (n_zh - 1).bit_length()
     shape = jax.ShapeDtypeStruct
     vmem = pl.BlockSpec(memory_space=pltpu.VMEM)
     dma = pltpu.SemaphoreType.DMA
@@ -615,8 +724,7 @@
         shape((2, 14, tok_rows, width // 2), BF16),
         shape((tok_rows, width), F32),
         shape((tok_rows, width), F32),
-        shape((1, units), F32),
-        shape((1, triple), F32),
+        shape((8, width), F32),
     ]
     scratch = [
         pltpu.VMEM((2, 2 * seq, width), BF16),
@@ -631,48 +739,47 @@
         pltpu.VMEM((2, seq, 2 * HEAD), F32),
         pltpu.VMEM((count, CHUNK, CHUNK), F32),
         pltpu.VMEM((count, CHUNK, CHUNK), F32),
-        pltpu.VMEM((2 * n, bw, units), BF16),
+        pltpu.VMEM((tok_rows, width), BF16),
+        pltpu.VMEM((2, tok_rows, 1), F32),
+        pltpu.VMEM((1, units), F32),
+        pltpu.VMEM((1, triple), F32),
+        pltpu.VMEM((8, width), F32),
+        pltpu.VMEM((hops, 8, width), F32),
+        pltpu.VMEM((2 * n * bw, units), BF16),
         pltpu.VMEM((n, bw, units), BF16),
         pltpu.VMEM((n, bw, triple), BF16),
         pltpu.VMEM((n, bw, half_width), BF16),
-        pltpu.VMEM((TILE_SLOTS, tok_rows, width // 2), BF16),
+        pltpu.VMEM((RING + 4, tok_rows, width // 2), BF16),
         pltpu.VMEM((3, tok_rows, width // 2), BF16),
-        pltpu.VMEM((tok_rows, width // 2), F32),
         pltpu.VMEM((max(bw, 128), 2 * seq), BF16),
-        dma((4, n)), dma((4, n)), dma((4, n)), dma((4, n)), dma((2, 7)), dma((2, 7)), dma((6,)),
+        dma((4, n, 4)), dma((4, n, 4)), dma((4, n, 4)), dma((4, n, 4)), dma((2, 7)), dma((2, 7)), dma((6,)),
         dma((2 * n,)), dma((2 * n,)), dma((n,)), dma((2 * n,)),
         dma((n,)), dma((n,)), dma((n,)), dma((n,)),
         dma((n,)), dma((n,)), dma((n,)), dma((n,)),
-        dma((TILE_SLOTS,)), dma((2, 14)), dma((3,)), dma,
+        dma((RING,)), dma((2, 14)), dma((2, 4)), dma((3,)), dma((width // 2 // CHUNK,)), dma((hops,)), dma((hops,)),
     ]
     return pl.pallas_call(
         functools.partial(block_kernel, n_zh),
         out_shape=outs,
-        in_specs=[ANY] * 10 + [vmem] * 4,
-        out_specs=[ANY] * 9 + [vmem] * 2,
+        in_specs=[ANY] * 6 + [vmem] * 5,
+        out_specs=[ANY] * 9 + [vmem],
         scratch_shapes=scratch,
         compiler_params=pltpu.CompilerParams(
             collective_id=0, has_side_effects=True, vmem_limit_bytes=VMEM_LIMIT
         ),
-    )(normed, cotangent, *halves, hidden_bias, head_bias, *tables)
+    )(tokens, cotangent, *halves, outer_params, hidden_bias, head_bias, *tables)
 
 
 def rotation_tables(seq):
     lane = np.arange(2 * HEAD) % HEAD
     exponent = (lane % (ROT // 2)).astype(np.float32) * np.float32(2.0 / ROT)
-    inverse = jnp.exp(-math.log(10000.0) * jnp.asarray(exponent))
-    angles = jnp.arange(seq, dtype=F32)[:, None] * inverse[None, :]
-    cos, sin = jnp.cos(angles), jnp.sin(angles)
-    turned = jnp.asarray(lane < ROT)[None, :]
-    low = jnp.asarray(lane < ROT // 2)[None, :]
-    return jnp.where(turned, cos, 1.0), jnp.where(turned, jnp.where(low, -sin, sin), 0.0)
-
-
-def normalize(inputs, scales, offsets):
-    average = jnp.mean(inputs, axis=-1, keepdims=True)
-    centred = inputs - average
-    variance = jnp.mean(centred * centred, axis=-1, keepdims=True)
-    return centred * lax.rsqrt(variance + 1e-05) * scales + offsets
+    inverse = np.exp(np.float32(-math.log(10000.0)) * exponent).astype(np.float32)
+    angles = np.arange(seq, dtype=np.float32)[:, None] * inverse[None, :]
+    cos = np.cos(angles.astype(np.float64)).astype(np.float32)
+    sin = np.sin(angles.astype(np.float64)).astype(np.float32)
+    turned, low = lane < ROT, lane < ROT // 2
+    zero = np.zeros_like(sin)
+    return np.where(turned, cos, zero + 1), np.where(turned, np.where(low, -sin, sin), zero)
 
 
 def adam_update(weight, moment_one, moment_two, gradient, step_rate, decay_rate):
@@ -686,34 +793,65 @@
     return (weight - step_rate * (normalized + decay_rate * weight), first_new, second_new)
 
 
-def flip(value, name):
-    return lax.ppermute(value, name, [(0, 1), (1, 0)])
+def adam_kernel(rate, turned, zp_ref, parts_ref, w_ref, one_ref, two_ref, *outs):
+    parts = parts_ref[...].astype(F32)
+    rows, cols = parts.shape[-2:]
+    gradient = jnp.sum(parts.reshape(-1, rows, cols), axis=0)
+    if turned:
+        gradient = gradient.T
+    shape = w_ref.shape
+    new = adam_update(
+        w_ref[...].reshape(gradient.shape), one_ref[...].reshape(gradient.shape),
+        two_ref[...].reshape(gradient.shape), gradient, rate, MATRIX_DECAY,
+    )
+    for out, value in zip(outs, new):
+        out[...] = value.reshape(shape)
+
+
+def adam(zp, parts, state, rate, turned, grid, parts_spec, state_spec):
+    shape = jax.ShapeDtypeStruct(state[0].shape, F32)
+    spec = pl.BlockSpec(*state_spec)
+    return pl.pallas_call(
+        functools.partial(adam_kernel, rate, turned),
+        out_shape=[shape] * 3,
+        grid_spec=pltpu.PrefetchScalarGridSpec(
+            num_scalar_prefetch=1,
+            grid=grid,
+            in_specs=[pl.BlockSpec(*parts_spec)] + [spec] * 3,
+            out_specs=[spec] * 3,
+        ),
+        compiler_params=pltpu.CompilerParams(vmem_limit_bytes=32 * 1024 * 1024),
+    )(zp, parts, *state)
+
+
+def finish_kernel(tok_ref, back_ref, grad_ref, branch_ref, outer_ref, out_ref, in_ref):
+    values = tok_ref[...].astype(F32)
+    out_ref[...] = (values + branch_ref[...] + outer_ref[2:3, :] + outer_ref[3:4, :]).astype(BF16)
+    mean = jnp.mean(values, axis=-1, keepdims=True)
+    centred = values - mean
+    inverse = lax.rsqrt(jnp.mean(centred * centred, axis=-1, keepdims=True) + 1e-05)
+    xhat = centred * inverse
+    g = grad_ref[...] * outer_ref[0:1, :]
+    inner = g - jnp.mean(g, axis=-1, keepdims=True) - xhat * jnp.mean(g * xhat, axis=-1, keepdims=True)
+    in_ref[...] = back_ref[...].astype(F32) + inverse * inner
+
+
+def finish(tokens, cotangent, grad_normed, branch, outer_params):
+    rows, width = tokens.shape
+    tile = 64
+    spec = pl.BlockSpec((tile, width), lambda i: (i, 0))
+    return pl.pallas_call(
+        finish_kernel,
+        grid=(rows // tile,),
+        out_shape=[jax.ShapeDtypeStruct((rows, width), BF16), jax.ShapeDtypeStruct((rows, width), F32)],
+        in_specs=[spec] * 4 + [pl.BlockSpec(outer_params.shape, lambda i: (0, 0))],
+        out_specs=[spec] * 2,
+        compiler_params=pltpu.CompilerParams(vmem_limit_bytes=32 * 1024 * 1024),
+    )(tokens, cotangent, grad_normed, branch, outer_params)
 
 
 def pick(value, index, axis):
     return lax.dynamic_index_in_dim(value, index, axis, keepdims=False)
-
-
-def owner_sum(parts, n_zh):
-    zp = lax.axis_index("zp")
-    wide = parts.astype(F32)
-    mine = sum(wide[2 * n_zh - 1 - 2 * s] for s in range(n_zh))
-    theirs = sum(wide[2 * n_zh - 2 - 2 * s] for s in range(n_zh))
-    low = jnp.where(zp == 0, mine, theirs)
-    high = jnp.where(zp == 0, theirs, mine)
-    return jnp.stack([low, high], axis=1)
-
-
-def sum_over(value, n_zh, names):
-    for name in names:
-        if name == "zh":
-            step = 1
-            while step < n_zh:
-                value = value + lax.ppermute(value, "zh", [(i, i ^ step) for i in range(n_zh)])
-                step *= 2
-        else:
-            value = value + flip(value, name)
-    return value
 
 
 def local(
@@ -735,67 +873,53 @@
     half_width = local_width // 2
     half_units = up_weight.shape[1] // 2
 
-    tokens_wide = tokens.astype(F32)
-    normed, norm_back = jax.vjp(normalize, tokens_wide, outer_params[0], outer_params[1])
-
-    qkv_rows = jnp.moveaxis(qkv_weight, 0, 1).reshape(bw, 3, 2, half_width)
-    qkv_rows = jnp.moveaxis(qkv_rows, 2, 1).reshape(bw, 2, 3 * half_width).astype(BF16)
-    dense_rows = dense_weight.T.reshape(bw, 2, half_width).astype(BF16)
-    up_rows = up_weight.reshape(bw, 2, half_units).astype(BF16)
-    down_rows = down_weight.T.reshape(bw, 2, half_units).astype(BF16)
-    halves = []
-    for rows in (down_rows, up_rows, dense_rows, qkv_rows):
-        halves += [pick(rows, zp, 1), pick(rows, 1 - zp, 1)]
+    qkv_rows = qkv_weight.reshape(3, bw, 2, half_width).transpose(2, 1, 0, 3)
+    qkv_rows = qkv_rows.reshape(2, bw, 3 * half_width).astype(BF16)
+    dense_rows = dense_weight.reshape(2, half_width, bw).swapaxes(1, 2).astype(BF16)
+    up_rows = up_weight.reshape(bw, 2, half_units).swapaxes(0, 1).astype(BF16)
+    down_rows = down_weight.reshape(2, half_units, bw).swapaxes(1, 2).astype(BF16)
     bias_half = pick(hidden_bias.reshape(2, 1, half_units), zp, 0)
     head_half = pick(head_bias.reshape(3, 2, half_width), zp, 1).reshape(1, 3 * half_width)
     outs = block(
-        n_zh, normed.astype(BF16), cotangent, halves, bias_half, head_half, rotation_tables(seq_rows)
+        n_zh, tokens, cotangent, (down_rows, up_rows, dense_rows, qkv_rows), outer_params,
+        bias_half, head_half, rotation_tables(seq_rows),
     )
     z_mlp, z_dense, z_qkv = outs[:3]
-    grad_normed, branch, hidden_part, head_part = outs[7:]
-    down_sum = owner_sum(z_mlp[0], n_zh)
-    up_sum = owner_sum(z_mlp[1], n_zh)
-    dense_sum = owner_sum(z_dense, n_zh)
-    qkv_sum = owner_sum(z_qkv, n_zh)
-    layer_out = (tokens_wide + branch + outer_params[2] + outer_params[3]).astype(BF16)
-
-    input_part, gain_grad, shift_grad = norm_back(grad_normed)
-    back_wide = cotangent.astype(F32)
-    input_grad = back_wide + input_part
-    out_bias_grad = jnp.sum(back_wide, axis=0)
-
-    vectors = jnp.concatenate(
-        [hidden_part.reshape(half_units), head_part.reshape(3 * half_width)]
-    )
-    both = jnp.where(
-        jnp.arange(2)[:, None] == zp, vectors[None, :], jnp.zeros_like(vectors)[None, :]
-    )
-    both = sum_over(both, n_zh, ("zp", "y", "zh"))
-    hidden_sum = both[:, :half_units].reshape(2 * half_units)
-    head_sum = jnp.moveaxis(both[:, half_units:].reshape(2, 3, half_width), 0, 1).reshape(
-        3, local_width
-    )
-    outer_sum = sum_over(
-        jnp.stack([gain_grad, shift_grad, out_bias_grad]), n_zh, ("c", "x", "y", "zp", "zh")
-    )
-    outer_sum = jnp.concatenate([outer_sum, outer_sum[2:]], axis=0)
-
-    model = width
-    qkv_sum = qkv_sum.reshape(bw, 2, 3, half_width)
-    qkv_sum = jnp.moveaxis(qkv_sum, 2, 0).reshape(3, bw, local_width)
-    dense_sum = dense_sum.reshape(bw, local_width).T
-    up_sum = up_sum.reshape(bw, 2 * half_units)
-    down_sum = down_sum.reshape(bw, 2 * half_units).T
-    new_qkv = adam_update(
-        qkv_weight, qkv_first, qkv_second, qkv_sum, (model // 2) ** (-0.5), MATRIX_DECAY
-    )
-    new_dense = adam_update(
-        dense_weight, dense_first, dense_second, dense_sum, (model // 16) ** (-0.5), MATRIX_DECAY
-    )
-    new_up = adam_update(up_weight, up_first, up_second, up_sum, model ** (-0.5), MATRIX_DECAY)
-    new_down = adam_update(
-        down_weight, down_first, down_second, down_sum, (4 * model) ** (-0.5), MATRIX_DECAY
-    )
+    grad_normed, branch, sums = outs[7:]
+    layer_out, input_grad = finish(tokens, cotangent, grad_normed, branch, outer_params)
+
+    zp_array = jnp.reshape(zp, (1,))
+    z_mlp = z_mlp.reshape(2, n_zh, 2, bw, half_units)
+    z_dense = z_dense.reshape(n_zh, 2, bw, half_width)
+    z_qkv = z_qkv.reshape(n_zh, 2, bw, 3 * half_width)
+    tile = min(bw, 128)
+    new_up = adam(
+        zp_array, z_mlp, (up_weight, up_first, up_second), width ** (-0.5), False,
+        (2, bw // tile),
+        ((1, n_zh, 1, tile, half_units), lambda h, r, zp_: (1, 0, 1 - (h ^ zp_[0]), r, 0)),
+        ((tile, half_units), lambda h, r, zp_: (r, h)),
+    )
+    new_down = adam(
+        zp_array, z_mlp, (down_weight, down_first, down_second), (4 * width) ** (-0.5), True,
+        (2, half_units // CHUNK),
+        ((1, n_zh, 1, bw, CHUNK), lambda h, r, zp_: (0, 0, 1 - (h ^ zp_[0]), 0, r)),
+        ((CHUNK, bw), lambda h, r, zp_: (h * (half_units // CHUNK) + r, 0)),
+    )
+    new_dense = adam(
+        zp_array, z_dense, (dense_weight, dense_first, dense_second), (width // 16) ** (-0.5), True,
+        (2,),
+        ((n_zh, 1, bw, half_width), lambda h, zp_: (0, 1 - (h ^ zp_[0]), 0, 0)),
+        ((half_width, bw), lambda h, zp_: (h, 0)),
+    )
+    new_qkv = adam(
+        zp_array, z_qkv, (qkv_weight, qkv_first, qkv_second), (width // 2) ** (-0.5), False,
+        (3, 2),
+        ((n_zh, 1, bw, half_width), lambda t, h, zp_: (0, 1 - (h ^ zp_[0]), 0, t)),
+        ((1, bw, half_width), lambda t, h, zp_: (t, 0, h)),
+    )
+    outer_sum = jnp.concatenate([sums[:3], sums[2:3]], axis=0)
+    hidden_sum = sums[3]
+    head_sum = sums[4, : 3 * local_width].reshape(3, local_width)
     new_head = adam_update(head_bias, head_first, head_second, head_sum, VECTOR_RATE, 0.0)
     new_hidden = adam_update(
         hidden_bias, hidden_first, hidden_second, hidden_sum, VECTOR_RATE, 0.0

time: 542 us -> 440 us (0.81); the launches traced: 532 us -> 438 us
  other arithmetic: 43 us -> 3.12 us
  local copies, waits for them, and re-layouts: 53.5 us -> 25.7 us
  starting transfers between devices: 11.9 us -> 0 us
  waiting for transfers between devices: 9.39 us -> 0 us
    pallas_call x1, Pallas kernels: 412 us -> 391 us  [block(): pl.pallas_call(functools.partial(block_kernel, n_zh), out_shape=outs, in_...]
    pallas_call x0 -> x5, Pallas kernels: none -> 17.4 us  [the longest x4 14.5 us: adam(): pl.pallas_call(functools.partial(adam_kernel, rate, turned), out_shape=[s...]
    unnamed x100 -> x64, local copies, waits for them, and re-layouts: 36.8 us -> 19.7 us
    sub x7 -> x3, other arithmetic: 17.7 us -> 1.95 us  [adam_update(): weight - step_rate * (normalized + decay_rate * weight)]
    ppermute x8 -> x0, starting transfers between devices: 11.9 us -> none  [the longest x6 8.85 us: flip(): return lax.ppermute(value, name, [(0, 1), (1, 0)])]
    ppermute x8 -> x0, waiting for transfers between devices: 9.39 us -> none  [the longest x6 8.11 us: flip(): return lax.ppermute(value, name, [(0, 1), (1, 0)])]
    convert_element_type x8 -> x2, other arithmetic: 9.93 us -> 1.17 us  [the longest x1 1.07 us: local(): dense_weight.reshape(2, half_width, bw).swapaxes(1, 2).astype(BF16)]
    reduce_sum x5 -> x0, other arithmetic: 7.5 us -> none  [the longest x2 3.58 us: normalize(): return centred * lax.rsqrt(variance + 1e-05) * scales + offsets]
  transfers between devices with their start and end apart: 8 -> 0, of which waited for: 4 -> 0; matrix products, arithmetic and copies ran while one was open for 11% -> 0% of each run, Pallas kernels for 0% -> 0%
where the time goes in v3:
time: 440 us; the launch traced here: 438 us
  Pallas kernels  408 us (93%)
  local copies, waits for them, and re-layouts  25.7 us (6%)
    pallas_call x1, Pallas kernels, block(): pl.pallas_call(functools.partial(block_kernel, n_zh), out_shape=outs, in_...  391 us
    unnamed x64, local copies, waits for them, and re-layouts  19.7 us
    pallas_call x4, Pallas kernels, adam(): pl.pallas_call(functools.partial(adam_kernel, rate, turned), out_shape=[s...  14.5 us

profile of v3, /device:TPU:0, one launch (start us, length us, event | category | flops | bytes accessed | tf_op | source)
XLA Modules:
  0.0 437.8 jit_solution(6892272719648045309)
XLA Ops:
  0.7 1.3 dynamic-slice_bitcast_fusion.1.hidden_bias
  1.9 0.7 dynamic-slice_bitcast_fusion
  2.6 0.6 copy.64
  3.2 1.1 convert_element_type.36
  4.3 0.8 copy.59
  5.1 1.7 copy.60
  6.8 0.1 copy.61
  6.9 1.2 copy.63.qkv_in
  8.0 0.0 copy-start.1
  8.0 1.9 copy.57
  9.9 1.3 copy.58
  11.3 0.0 copy-done.1
  11.3 0.1 convert_element_type.30
  11.4 1.3 copy.56
  12.7 0.0 copy-start.20
  12.7 390.6 %shard_map.416 = (bf16[2,4,256,1024]{3,2,1,0:T(8,128)(2,1)}, bf16[4,256,256]{2,1,0:T(8,128)(2,1)}, bf16[4,256,768]{2,1,0:T(8,128)(2,1)}, bf16[2,4,256,1024]{3,2,...) custom-call(bf16[256,2048]{1,0:T(8,128)(2,1)} %tok_ref.1, ...), custom_call_target="tpu_custom_call" | custom-call | tf_op jit(solution)/shard_map/pallas_call | solution.py:761
  403.3 0.0 copy-done.20
  403.3 0.0 copy-start.5
  403.3 1.2 copy-done.5
  404.5 0.0 copy-start.6
  404.5 1.2 copy-done.6
  405.7 1.6 copy-done.7
  407.3 1.6 copy-done.8
  408.9 0.0 copy-start.25
  408.9 0.0 copy-start.28
  408.9 0.0 copy-start.29
  409.0 0.0 copy-start.22
  409.0 0.0 copy-start.23
  409.0 0.0 copy-start.9
  409.0 0.0 copy-start.17
  409.0 0.0 copy-start.18
  409.0 2.9 shard_map.417
  412.0 0.0 copy-done.21
  412.0 0.0 copy-done.24
  412.0 0.0 copy-done.26
  412.0 0.0 copy-done.27
  412.0 0.6 multiply_subtract_fusion.2
  412.7 0.0 copy-done.25
  412.7 0.0 copy-done.28
  412.7 0.0 copy-done.29
  412.7 0.6 multiply_subtract_fusion.1
  413.4 0.0 copy-done.22
  413.4 0.0 copy-done.23
  413.4 0.7 multiply_subtract_fusion
  414.1 0.0 copy-done.9
  414.1 0.0 copy-done.17
  414.1 0.0 copy-done.18
  414.1 0.0 copy-start.19
  414.1 1.0 copy-done.19
  415.1 1.5 shard_map.419
  416.6 0.0 copy-done.4
  416.6 1.4 copy-done.14
  418.0 1.4 copy-done.15
  419.4 1.4 copy-done.16
  420.9 3.8 shard_map.418
  424.7 0.0 copy-done
  424.7 0.7 copy-done.2
  425.4 1.6 copy-done.10
  427.0 1.6 copy-done.11
  428.6 5.1 %shard_map.421 = (f32[2048,256]{1,0:T(8,128)}, f32[2048,256]{1,0:T(8,128)}, f32[2048,256]{1,0:T(8,128)}) custom-call(s32[1]{0:T(128)} %bitcast.12.zp_ref, bf16[2,2,2,256,1024]{4,3,2,1,0:T(8,128)(2,1)S(1)} %bitcast.23, f32[2048,256]{1,0:T(8,128)S(1)} %copy-done.2, f32[2048,256]{1,0:T(8,128)S(1)} %copy-done.10, f32[2048,256]{1,0:T(8,128)S(1)} %copy-done.11), custom_call_target="tpu_custom_call" | custom-call | tf_op jit(solution)/shard_map/pallas_call | solution.py:814
  433.7 0.0 copy-done.3
  433.7 0.0 copy-done.12
  433.7 0.0 copy-done.13
  433.7 4.1 shard_map.420
  (21 shorter events, 0.1 us)
Async XLA Ops:
  8.0 3.2 copy-start.1
  12.7 390.6 %copy-start.20 = (f32[4,2048]{1,0:T(4,128)S(1)}, f32[4,2048]{1,0:T(4,128)}, u32[]{:S(2)}) copy-start(f32[4,2048]{1,0:T(4,128)} %outer_ref.3) | copy-start | bytes 98308
  403.3 1.2 copy-start.5
  404.5 1.2 copy-start.6
  405.7 1.6 copy-start.7
  407.3 1.6 copy-start.8
  408.9 3.1 copy-start.21
  408.9 3.1 copy-start.24
  408.9 3.1 copy-start.26
  408.9 3.1 copy-start.27
  408.9 3.8 copy-start.25
  408.9 3.8 copy-start.28
  408.9 3.8 copy-start.29
  409.0 4.4 %copy-start.22 = (f32[4,2048]{1,0:T(4,128)S(1)}, f32[4,2048]{1,0:T(4,128)}, u32[]{:S(2)}) copy-start(f32[4,2048]{1,0:T(4,128)} %param.46) | copy-start | bytes 98308
  409.0 4.4 %copy-start.23 = (f32[4,2048]{1,0:T(4,128)S(1)}, f32[4,2048]{1,0:T(4,128)}, u32[]{:S(2)}) copy-start(f32[4,2048]{1,0:T(4,128)} %param.47) | copy-start | bytes 98308
  409.0 5.1 %copy-start.9 = (f32[512,256]{1,0:T(8,128)S(1)}, f32[512,256]{1,0:T(8,128)}, u32[]{:S(2)}) copy-start(f32[512,256]{1,0:T(8,128)} %w_ref.5) | copy-start | bytes 1572868
  409.0 5.1 %copy-start.17 = (f32[512,256]{1,0:T(8,128)S(1)}, f32[512,256]{1,0:T(8,128)}, u32[]{:S(2)}) copy-start(f32[512,256]{1,0:T(8,128)} %one_ref.5) | copy-start | bytes 1572868
  409.0 5.1 %copy-start.18 = (f32[512,256]{1,0:T(8,128)S(1)}, f32[512,256]{1,0:T(8,128)}, u32[]{:S(2)}) copy-start(f32[512,256]{1,0:T(8,128)} %two_ref.5) | copy-start | bytes 1572868
  412.0 4.7 %copy-start.4 = (f32[3,256,512]{2,1,0:T(8,128)S(1)}, f32[3,256,512]{2,1,0:T(8,128)}, u32[]{:S(2)}) copy-start(f32[3,256,512]{2,1,0:T(8,128)} %w_ref.4) | copy-start | bytes 4718596
  414.1 1.0 copy-start.19
  416.6 1.4 copy-start.14
  418.0 1.4 copy-start.15
  419.4 1.4 copy-start.16
  420.8 3.8 copy-start
  420.9 4.5 %copy-start.2 = (f32[2048,256]{1,0:T(8,128)S(1)}, f32[2048,256]{1,0:T(8,128)}, u32[]{:S(2)}) copy-start(f32[2048,256]{1,0:T(8,128)} %w_ref.7) | copy-start | bytes 6291460
  425.4 1.6 copy-start.10
  427.0 1.6 copy-start.11
  428.6 5.1 %copy-start.3 = (f32[256,2048]{1,0:T(8,128)S(1)}, f32[256,2048]{1,0:T(8,128)}, u32[]{:S(2)}) copy-start(f32[256,2048]{1,0:T(8,128)} %w_ref.6) | copy-start | bytes 6291460
  428.6 5.1 %copy-start.12 = (f32[256,2048]{1,0:T(8,128)S(1)}, f32[256,2048]{1,0:T(8,128)}, u32[]{:S(2)}) copy-start(f32[256,2048]{1,0:T(8,128)} %one_ref.6) | copy-start | bytes 6291460
  428.6 5.1 %copy-start.13 = (f32[256,2048]{1,0:T(8,128)S(1)}, f32[256,2048]{1,0:T(8,128)}, u32[]{:S(2)}) copy-start(f32[256,2048]{1,0:T(8,128)} %two_ref.6) | copy-start | bytes 6291460

commit v4 on v3

--- a/solution.py
+++ b/solution.py
@@ -27,8 +27,32 @@
 VMEM_LIMIT = 63 * 1024 * 1024
 
 
+RUNS = (
+    (
+        ("proj", 4), ("f1", 1), ("proj", 3), ("f1", 1), ("proj", 1), ("att", 1), ("f1", 1), ("att", 1),
+        ("f0", 2), ("att", 1), ("f0", 1), ("att", 1), ("a1", 1),
+    ),
+    (
+        ("act", 1), ("f0", 1), ("act", 4), ("ysET", 1), ("ysQKV", 1), ("act", 1), ("ysQKV", 1), ("a0", 1),
+        ("slope", 1), ("act", 1), ("slope", 2), ("zsQKV", 1), ("ysQKV", 1), ("act", 1), ("slope", 1),
+        ("zsQKV", 1), ("ysM", 1), ("slope", 1), ("ysET", 1), ("slope", 1), ("zsET", 1), ("zsQKV", 1),
+        ("slope", 1), ("ysM", 1), ("slope", 1), ("ysM", 1),
+    ),
+    (
+        ("zsM", 1), ("r0c", 1), ("zsET", 1), ("r0c", 3), ("zsM", 1), ("r0c", 4), ("r0x", 1), ("zsM", 1),
+        ("r0x", 1), ("ysET", 1), ("ysM", 1), ("r0x", 1), ("zsET", 1), ("r0x", 1), ("r0z", 1), ("r1c", 1),
+        ("ysM", 1), ("r1c", 2), ("r0z", 1), ("r1c", 1), ("ysM", 1), ("r1c", 1), ("zsM", 2), ("r1c", 3),
+        ("r1x", 1), ("zsM", 1), ("r1x", 2), ("ysM", 1), ("r0f", 1), ("r1x", 1), ("r1z", 1), ("ysET", 1),
+        ("ysM", 1), ("r0f", 1), ("r1z", 1), ("zsET", 1), ("vec", 1), ("zsM", 1), ("vec", 3), ("ysQKV", 1),
+        ("vec", 1), ("zsM", 1), ("r1f", 1), ("vec", 1), ("r1f", 1), ("zsQKV", 1),
+    ),
+)
+ORDER = [[name for name, times in part for _ in range(times)] for part in RUNS]
+
 CHUNK = 256
 RING = 2
+LATER = 1
+GELU = math.sqrt(2.0 / math.pi)
 NT = (((1,), (1,)), ((), ()))
 TN = (((0,), (0,)), ((), ()))
 
@@ -44,10 +68,10 @@
     z_mlp, z_dense, z_qkv, y_mlp, y_dense, y_qkv, rows_in, grad_out, branch_out, sums_ref,
     rows2, mlp_w, dense_w, qkv_w, units2, heads3, heads1,
     dq_s, dk_s, dv_s, s_s, p_s, tok_s, stat_s, hidden_sum, head_sum, vec_s, vec_in,
-    y_stage, z_stage, qkv_stage, dense_stage, tile_stage, load_s, turned_s,
+    grads_s, qkv_stage, dense_stage, tile_stage, load_s, turned_s,
     w_send, w_recv, fwd_send, fwd_recv, a_send, a_recv, local_sem,
     ym_send, ym_recv, zm_send, zm_recv, yd_send, yd_recv, zd_send, zd_recv,
-    yq_send, yq_recv, zq_send, zq_recv, tile_send, tile_recv, x_send, load_sem, wide_sem, vec_send, vec_recv,
+    yq_send, yq_recv, zq_send, zq_recv, tile_send, tile_recv, x_send, zt_send, load_sem, wide_sem, vec_send, vec_recv,
 ):
     zh, zp, y = lax.axis_index("zh"), lax.axis_index("zp"), lax.axis_index("y")
     x, c = lax.axis_index("x"), lax.axis_index("c")
@@ -115,7 +139,7 @@
 
     def z_copy(w, i, k):
         m = pieces[w]
-        src = halves[w].at[zp ^ step(i)[1], pl.ds(k * (bw // m), bw // m), :]
+        src = halves[w].at[zp ^ step(i)[1], at(k, bw // m), :]
         return remote(src, place(w, me, k, m), w_send.at[w, i, k], w_recv.at[w, i, k], target(i))
 
     def y_copy(w, i, k=0):
@@ -176,9 +200,22 @@
         else:
             forward(w, i, k)
 
-    order = [(w, k) for w in (1, 0, 3, 2) for k in range(pieces[w])]
+    queue = (3, 2, 1, 0)
+    order = [(w, k) for w in queue for k in range(pieces[w])]
     later = list(range(n - 2, -1, -1))
+    go(act_copy(0, 0, 0))
     go(act_copy(0, 1, 0))
+
+    @pl.when(inner)
+    def _():
+        for w, k in order:
+            z_copy(w, 0, k).start()
+
+    for w in queue:
+        go(y_copy(w, n - 1))
+    go(act_copy(0, 2, 0))
+    for copy in locals_():
+        copy.start()
     tok_load.wait()
     for j in range(tok_rows // 64):
         rows = pl.ds(j * 64, 64)
@@ -191,23 +228,11 @@
         normed = centred * inverse * outer_ref[0:1, :] + outer_ref[1:2, :]
         rows2[1, at((zp * 4 + mp) * (tok_rows // 64) + j, 64), :] = normed.astype(BF16)
     go(act_copy(1, 0, 0))
-    go(act_copy(0, 0, 0))
     go(act_copy(1, 1, 0))
     go(act_copy(1, 2, 0))
-    go(act_copy(0, 2, 0))
-    for w in (1, 0, 3, 2):
-        go(y_copy(w, n - 1))
-
-    @pl.when(inner)
-    def _():
-        for w, k in order:
-            z_copy(w, 0, k).start()
-
-    for copy in locals_():
-        copy.start()
+    pl.when(inner)(lambda: forward(order[0][0], 0, order[0][1]))
+    pass_on(0, 0, 0)
     pass_on(1, 0, 0)
-    pl.when(inner)(lambda: forward(1, 0, 0))
-    pass_on(0, 0, 0)
     for w, k in order:
         for i in later:
             send_step(w, i, k)
@@ -217,137 +242,72 @@
         for w, k in order[1:]:
             forward(w, 0, k)
 
+    pass_on(0, 1, 0)
     pass_on(1, 1, 0)
-    pass_on(0, 1, 0)
-    for w, extra in ((1, 1), (0, 0)):
-        for k in range(pieces[w]):
+    def forward_pieces(w, start, stop):
+        def one(piece, carry):
             for i in later:
-                forward_step(w, i, k)
-        pass_on(extra, 1, 1)
+                forward_step(w, i, piece)
+            return carry
+
+        lax.fori_loop(start, stop, one, 0)
+
+    forward_pieces(3, 0, pieces[3])
+    pass_on(0, 1, 1)
+    forward_pieces(2, 0, pieces[2])
+    pass_on(1, 1, 1)
+    forward_pieces(1, 0, pieces[1] // 4)
     for copy in locals_():
         copy.wait()
-    for k in (1, 0):
+    for k in (0, 1):
         for part in range(4):
             act_copy(k, 2, part).wait_recv()
-    y_arrived(1)
-    y_arrived(0)
-
-
-    hidden_sum[...] = jnp.zeros_like(hidden_sum)
-    events = [(w, i, k) for w in (3, 2) for k in range(pieces[w]) for i in later]
+    y_arrived(3)
+    y_arrived(2)
     tiles = 2 * seq // CHUNK
 
-    def mlp_tile(r, carry):
+
+    def low_rows(r):
+        return at(n * bw // CHUNK + r, CHUNK)
+
+    def bent(hidden):
+        square = hidden * hidden
+        return square, jnp.tanh(GELU * (hidden * (1.0 + 0.044715 * square)))
+
+    def act_tile(r, carry):
         rows = at(r, CHUNK)
         for j in range(units // CHUNK):
             cols = pl.ds(j * CHUNK, CHUNK)
             hidden = jnp.dot(rows2[1, rows, :], mlp_w[1, :, cols], preferred_element_type=F32)
             hidden = hidden + hidden_bias[:, cols]
+            high = hidden.astype(BF16)
+            units2[1, rows, cols] = high
+            grads_s[low_rows(r), cols] = (hidden - high.astype(F32)).astype(BF16)
+            _, tanh = bent(hidden)
+            units2[0, rows, cols] = (0.5 * hidden * (1.0 + tanh)).astype(BF16)
+        return carry
+
+    def slope_tile(r, carry):
+        rows = at(r, CHUNK)
+        for j in range(units // CHUNK):
+            cols = pl.ds(j * CHUNK, CHUNK)
+            hidden = units2[1, rows, cols].astype(F32) + grads_s[low_rows(r), cols].astype(F32)
+            square, tanh = bent(hidden)
             grad = jnp.dot(rows2[0, rows, :], mlp_w[0, :, cols], preferred_element_type=F32)
-            k0 = math.sqrt(2.0 / math.pi)
-            square = hidden * hidden
-            tanh = jnp.tanh(k0 * (hidden * (1.0 + 0.044715 * square)))
-            units2[0, rows, cols] = (0.5 * hidden * (1.0 + tanh)).astype(BF16)
             slope = 0.5 * (1.0 + tanh) + 0.5 * hidden * (1.0 - tanh * tanh) * (
-                k0 * (1.0 + 3.0 * 0.044715 * square)
+                GELU * (1.0 + 3.0 * 0.044715 * square)
             )
             low = (grad * slope).astype(BF16)
             units2[1, rows, cols] = low
             hidden_sum[:, cols] += jnp.sum(low.astype(F32), axis=0, keepdims=True)
-        for r_at in range(tiles):
-            mine = [e for k, e in enumerate(events) if k * (tiles - 2) // len(events) == r_at]
-            if mine:
-                @pl.when(r == r_at)
-                def _():
-                    for event in mine:
-                        forward_step(*event)
         return carry
 
-    lax.fori_loop(0, tiles, mlp_tile, 0)
     for w in range(4):
         for i in range(n - 1):
             for k in range(pieces[w]):
                 started.extend([z_copy(w, i, k), y_copy(w, i, k)])
 
 
-    def weight_grad(left, right, b, put):
-        wide = max(bw, 128)
-        turned = turned_s.at[pl.ds(0, wide), :]
-        if bw == wide:
-            turned[...] = left[:, at(b, bw)].T
-        else:
-            turned[...] = left[:, at(lax.div(b, wide // bw), wide)].T
-        for j in range(right.shape[1] // CHUNK):
-            cols = pl.ds(j * CHUNK, CHUNK)
-            value = jnp.dot(turned[...], right[:, cols], preferred_element_type=F32)
-            if bw < wide:
-                spot = lax.rem(b, wide // bw)
-                value = sum(
-                    jnp.where(spot == k, value[k * bw : (k + 1) * bw], 0.0) for k in range(wide // bw)
-                )
-            put(cols, value)
-
-    def mlp_grad(w, b, put):
-        weight_grad(rows2.at[w], units2.at[w], b, put)
-
-    def ym_copy(k):
-        w, i = lax.div(k, n), lax.rem(k, n)
-        return remote(y_stage.at[at(k, bw), :], y_mlp.at[w, i], ym_send.at[k], ym_recv.at[k], to_y)
-
-    def ym_step(k, carry):
-        w, i = lax.div(k, n), lax.rem(k, n)
-
-        def put(cols, value):
-            y_stage[at(k, bw), cols] = value.astype(BF16)
-
-        mlp_grad(w, target_block(i) + 1 - y, put)
-        ym_copy(k).start()
-        return carry
-
-    lax.fori_loop(0, 2 * n, ym_step, 0)
-
-    def zm_copy(k):
-        w, i = lax.div(k, n), lax.rem(k, n)
-        return remote(z_stage.at[i], z_mlp.at[w, i], zm_send.at[i], zm_recv.at[k], target(i))
-
-    def zm_local(k):
-        w, i = lax.div(k, n), lax.rem(k, n)
-        return pltpu.make_async_copy(z_stage.at[i], z_mlp.at[w, i], zm_send.at[i])
-
-    def zm_step(k, carry):
-        w, i = lax.div(k, n), lax.rem(k, n)
-        ym_copy(k).wait_recv()
-        load = pltpu.make_async_copy(y_mlp.at[w, i], load_s.at[0, pl.ds(0, bw), :], load_sem.at[0])
-        load.start()
-
-        @pl.when((k >= n) & (i < n - 1))
-        def _():
-            zm_copy(k - n).wait_send()
-
-        @pl.when((k >= n) & (i == n - 1))
-        def _():
-            zm_local(k - n).wait()
-
-        load.wait()
-
-        def put(cols, value):
-            z_stage[i, :, cols] = (value + load_s[0, pl.ds(0, bw), cols].astype(F32)).astype(BF16)
-
-        mlp_grad(w, target_block(i) + y, put)
-
-        @pl.when(i < n - 1)
-        def _():
-            zm_copy(k).start()
-
-        @pl.when(i == n - 1)
-        def _():
-            zm_local(k).start()
-
-        return carry
-
-
-    y_arrived(3)
-    y_arrived(2)
     low_lane = lax.broadcasted_iota(jnp.int32, (1, lanes), 1) % HEAD < ROT // 2
 
     def turn(values, rows, sign):
@@ -368,8 +328,6 @@
                 heads3[rows, pl.ds(t * half_width + g * lanes, lanes)] = part.astype(BF16)
         heads1[rows, :] = jnp.dot(rows2[0, rows, :], dense_w[...], preferred_element_type=F32).astype(BF16)
         return carry
-
-    lax.fori_loop(0, tiles, proj_tile, 0)
 
 
     first = lax.broadcasted_iota(jnp.int32, (1, lanes), 1) < HEAD
@@ -448,29 +406,99 @@
                 low = g.astype(BF16)
                 heads3[at(base + qb, CHUNK), cols(t)] = low
                 head_sum[:, cols(t)] += jnp.sum(low.astype(F32), axis=0, keepdims=True)
-        per = n // 4
-        lax.fori_loop(it * per, (it + 1) * per, zm_step, 0)
         return carry
 
-    head_sum[...] = jnp.zeros_like(head_sum)
-    lax.fori_loop(0, 2 * pairs, attend, 0)
-
-
-    def small(left, right, y_buf, z_buf, stage, ys, yr, zs, zr):
-        cols = stage.shape[2]
+
+    def weight_grad(left, right, b, put):
+        wide = max(bw, 128)
+        turned = turned_s.at[pl.ds(0, wide), :]
+        if bw == wide:
+            turned[...] = left[:, at(b, bw)].T
+        else:
+            turned[...] = left[:, at(lax.div(b, wide // bw), wide)].T
+        for j in range(right.shape[1] // CHUNK):
+            cols = pl.ds(j * CHUNK, CHUNK)
+            value = jnp.dot(turned[...], right[:, cols], preferred_element_type=F32)
+            if bw < wide:
+                spot = lax.rem(b, wide // bw)
+                value = sum(
+                    jnp.where(spot == k, value[k * bw : (k + 1) * bw], 0.0) for k in range(wide // bw)
+                )
+            put(cols, value)
+
+    def mlp_grad(w, b, put):
+        weight_grad(rows2.at[w], units2.at[w], b, put)
+
+    def ym_copy(k):
+        w, i = lax.div(k, n), lax.rem(k, n)
+        return remote(grads_s.at[at(k, bw), :], y_mlp.at[w, i], ym_send.at[k], ym_recv.at[k], to_y)
+
+    def ym_step(k, carry):
+        w, i = lax.div(k, n), lax.rem(k, n)
+
+        def put(cols, value):
+            grads_s[at(k, bw), cols] = value.astype(BF16)
+
+        mlp_grad(w, target_block(i) + 1 - y, put)
+        ym_copy(k).start()
+        return carry
+
+
+    def zm_copy(k):
+        w, i = lax.div(k, n), lax.rem(k, n)
+        return remote(grads_s.at[at(2 * n + i, bw), :], z_mlp.at[w, i], zm_send.at[i], zm_recv.at[k], target(i))
+
+    def zm_local(k):
+        w, i = lax.div(k, n), lax.rem(k, n)
+        return pltpu.make_async_copy(grads_s.at[at(2 * n + i, bw), :], z_mlp.at[w, i], zm_send.at[i])
+
+    def zm_step(k, carry):
+        w, i = lax.div(k, n), lax.rem(k, n)
+        ym_copy(k).wait_recv()
+        load = pltpu.make_async_copy(y_mlp.at[w, i], load_s.at[0, pl.ds(0, bw), :], load_sem.at[0])
+        load.start()
+
+        @pl.when((k >= n) & (i < n - 1))
+        def _():
+            zm_copy(k - n).wait_send()
+
+        @pl.when((k >= n) & (i == n - 1))
+        def _():
+            zm_local(k - n).wait()
+
+        load.wait()
+
+        def put(cols, value):
+            grads_s[at(2 * n + i, bw), cols] = (value + load_s[0, pl.ds(0, bw), cols].astype(F32)).astype(BF16)
+
+        mlp_grad(w, target_block(i) + y, put)
+
+        @pl.when(i < n - 1)
+        def _():
+            zm_copy(k).start()
+
+        @pl.when(i == n - 1)
+        def _():
+            zm_local(k).start()
+
+        return carry
+
+
+    def small(left, right, y_buf, z_buf, held, ys, yr, zs, zr):
+        cols = held.shape[2]
 
         def y_copy_(i):
-            return remote(stage.at[i], y_buf.at[i], ys.at[i], yr.at[i], to_y)
+            return remote(held.at[i], y_buf.at[i], ys.at[i], yr.at[i], to_y)
 
         def z_copy_(i):
-            return remote(stage.at[i], z_buf.at[i], zs.at[i], zr.at[i], target(i))
+            return remote(held.at[i], z_buf.at[i], zs.at[i], zr.at[i], target(i))
 
         def z_local(i):
-            return pltpu.make_async_copy(stage.at[i], z_buf.at[i], zs.at[i])
+            return pltpu.make_async_copy(held.at[i], z_buf.at[i], zs.at[i])
 
         def y_step(i, carry):
             def put(at_cols, value):
-                stage[i, :, at_cols] = value.astype(BF16)
+                held[i, :, at_cols] = value.astype(BF16)
 
             weight_grad(left, right, target_block(i) + 1 - y, put)
             y_copy_(i).start()
@@ -485,7 +513,7 @@
             load.wait()
 
             def put(at_cols, value):
-                stage[i, :, at_cols] = (value + spot[:, at_cols].astype(F32)).astype(BF16)
+                held[i, :, at_cols] = (value + spot[:, at_cols].astype(F32)).astype(BF16)
 
             weight_grad(left, right, target_block(i) + y, put)
 
@@ -521,25 +549,26 @@
     )
 
 
-    def ring_copy(kind, slot, index, to):
+    def tile_copy(kind, slot, sem, index, to):
         return remote(
-            tile_stage.at[slot], rows_in.at[kind, index], tile_send.at[slot],
-            tile_recv.at[kind, index], to,
+            tile_stage.at[slot], rows_in.at[kind, index], sem, tile_recv.at[kind, index], to
         )
 
-    def x_slot(kind, t):
-        return tile_stage.at[RING + t] if kind else y_stage.at[at(t, tok_rows), :]
+    def c_copy(kind, t, index):
+        slot = lax.rem(t, RING)
+        return tile_copy(kind, slot, tile_send.at[slot], index, to_c)
 
     def x_copy(kind, t, index):
-        return remote(
-            x_slot(kind, t), rows_in.at[kind, index], x_send.at[kind, t], tile_recv.at[kind, index], to_x
-        )
-
-    def row_tiles(kind, stage, base, total):
+        return tile_copy(kind, RING + t, x_send.at[t], index, to_x)
+
+    def zt_copy(kind, h, index):
+        return tile_copy(kind, RING + h, zt_send.at[h], index, to_zp)
+
+    def row_tiles(kind, stage):
         left, left_w = units2.at[1 - kind], mlp_w.at[1 - kind]
         right, right_w = ((heads3, qkv_w), (heads1, dense_w))[kind]
 
-        def one(t, carry):
+        def one(t):
             h = lax.rem(t, 2)
             if stage == 0:
                 zq, xq = zp ^ (1 - lax.rem(lax.div(t, 2), 2)), x ^ (1 - lax.div(t, 4))
@@ -556,7 +585,7 @@
                 come = (zp * 4 + x * 2 + h, 8 + zp * 2 + h, 12 + h)
             loads = []
             for slot, (spot, back) in enumerate(zip(come, (to_c, to_x, to_zp))):
-                ring_copy(kind, 0, spot, back).wait_recv()
+                tile_copy(kind, 0, tile_send.at[0], spot, back).wait_recv()
                 loads.append(
                     pltpu.make_async_copy(rows_in.at[kind, spot], load_s.at[slot], load_sem.at[slot])
                 )
@@ -564,16 +593,20 @@
             for load in loads:
                 load.wait()
             rows = at(block, tok_rows)
-            if stage in (0, 2):
-                slot = lax.rem(base + t, RING)
-                spot, copy = tile_stage.at[slot], ring_copy(kind, slot, index, to)
-
-                @pl.when(base + t >= RING)
-                def _():
+            if stage == 0:
+                spot, copy = tile_stage.at[lax.rem(t, RING)], c_copy(kind, t, index)
+                if kind == LATER:
                     copy.wait_send()
-
+                else:
+                    pl.when(t >= RING)(copy.wait_send)
             elif stage == 1:
-                spot, copy = x_slot(kind, t), x_copy(kind, t, index)
+                spot, copy = tile_stage.at[RING + t], x_copy(kind, t, index)
+                if kind == LATER:
+                    pl.when(t < 2)(zt_copy(kind, lax.rem(t, 2), index).wait_send)
+                    pl.when(t >= 2)(copy.wait_send)
+            elif stage == 2:
+                spot, copy = tile_stage.at[RING + h], zt_copy(kind, h, index)
+                x_copy(kind, h, index).wait_send()
             for j in range(half // CHUNK):
                 cols = pl.ds(j * CHUNK, CHUNK)
                 model = at(h * (half // CHUNK) + j, CHUNK)
@@ -604,13 +637,8 @@
                     copy.start()
                 for copy in copies:
                     copy.wait()
-            return carry
-
-        lax.fori_loop(0, total, one, 0)
-
-    def finish_y(k, carry):
-        ym_copy(k).wait_send()
-        return carry
+
+        return one
 
 
     hops = [to_zp, to_y]
@@ -642,31 +670,74 @@
         else:
             sums_ref[0:3, :] = vec_s[0:3, :]
 
-    per = n // 4
-    row_tiles(0, 0, 0, 8)
-    lax.fori_loop(0, n, finish_y, 0)
-    row_tiles(0, 1, 0, 4)
-    lax.fori_loop(n, n + per, zm_step, 0)
-    row_tiles(1, 0, 8, 8)
-    lax.fori_loop(n + per, n + 2 * per, zm_step, 0)
-    row_tiles(1, 1, 0, 4)
-    lax.fori_loop(0, n, dense_steps[0], 0)
-    lax.fori_loop(0, n, qkv_steps[0], 0)
-    row_tiles(0, 2, 16, 2)
-    lax.fori_loop(n + 2 * per, 2 * n, zm_step, 0)
-    lax.fori_loop(0, n, dense_steps[1], 0)
-    lax.fori_loop(0, n // 2, qkv_steps[1], 0)
-    row_tiles(1, 2, 18, 2)
-    row_tiles(0, 3, 0, 2)
-    vec_first()
-    lax.fori_loop(n // 2, n // 2 + per, qkv_steps[1], 0)
-    vec_next(0)
-    vec_next(1)
-    lax.fori_loop(n // 2 + per, n, qkv_steps[1], 0)
-    for k in range(2, len(hops) - 1):
-        vec_next(k)
-    row_tiles(1, 3, 0, 2)
-    vec_next(len(hops) - 1)
+
+    def steps(step_, total, parts):
+        def share(q):
+            if total == parts:
+                step_(q, 0)
+            else:
+                lax.fori_loop(q * total // parts, (q + 1) * total // parts, step_, 0)
+
+        return share
+
+    def pieces_of(w):
+        m = pieces[w]
+        return lambda q: forward_pieces(w, lax.div(q * m, 4), lax.div((q + 1) * m, 4))
+
+    def vector_hop(q):
+        pl.when(q == 0)(vec_first)
+        for k in range(5):
+            @pl.when(q == k + 1)
+            def _():
+                for hop in range(k, len(hops) if k == 4 else k + 1):
+                    vec_next(hop)
+
+    tasks = {
+        "f1": pieces_of(1),
+        "f0": pieces_of(0),
+        "a1": lambda q: y_arrived(1),
+        "a0": lambda q: y_arrived(0),
+        "proj": steps(proj_tile, tiles, 8),
+        "att": steps(attend, 2 * pairs, 4),
+        "act": steps(act_tile, tiles, 8),
+        "slope": steps(slope_tile, tiles, 8),
+        "ysET": steps(dense_steps[0], n, 4),
+        "zsET": steps(dense_steps[1], n, 4),
+        "ysQKV": steps(qkv_steps[0], n, 4),
+        "zsQKV": steps(qkv_steps[1], n, 4),
+        "ysM": steps(ym_step, 2 * n, 8),
+        "zsM": steps(zm_step, 2 * n, 8),
+        "vec": vector_hop,
+    }
+    for kind in (0, 1):
+        for stage, letter in enumerate("cxzf"):
+            tasks[f"r{kind}{letter}"] = row_tiles(kind, stage)
+
+    def dispatch(part, seen):
+        names = list(dict.fromkeys(part))
+
+        def one(now, carry):
+            for name in names:
+                spots = [k for k, other in enumerate(part) if other == name]
+                mine = functools.reduce(jnp.logical_or, [now == k for k in spots])
+                q = seen[name] + sum((now >= k).astype(jnp.int32) for k in spots[1:])
+                pl.when(mine)(functools.partial(tasks[name], q))
+            return carry
+
+        lax.fori_loop(0, len(part), one, 0)
+
+    hidden_sum[...] = jnp.zeros_like(hidden_sum)
+    head_sum[...] = jnp.zeros_like(head_sum)
+    seen = dict.fromkeys(tasks, 0)
+    seen["f1"] = 1
+    for part in ORDER:
+        dispatch(part, dict(seen))
+        for name in part:
+            seen[name] += 1
+
+    def finish_y(k, carry):
+        ym_copy(k).wait_send()
+        return carry
 
 
     for copy in started:
@@ -689,13 +760,13 @@
 
         return carry
 
-    lax.fori_loop(n, 2 * n, finish_y, 0)
+    lax.fori_loop(0, 2 * n, finish_y, 0)
     lax.fori_loop(0, 2 * n, finish_z, 0)
     for slot in range(RING):
-        ring_copy(0, slot, 0, to_c).wait_send()
-    for kind in (0, 1):
-        for t in range(4):
-            x_copy(kind, t, 0).wait_send()
+        c_copy(0, slot, 0).wait_send()
+    for t in (0, 1):
+        zt_copy(0, t, 0).wait_send()
+        x_copy(0, 2 + t, 0).wait_send()
     lax.fori_loop(0, n, dense_steps[2], 0)
     lax.fori_loop(0, n, qkv_steps[2], 0)
 
@@ -745,8 +816,7 @@
         pltpu.VMEM((1, triple), F32),
         pltpu.VMEM((8, width), F32),
         pltpu.VMEM((hops, 8, width), F32),
-        pltpu.VMEM((2 * n * bw, units), BF16),
-        pltpu.VMEM((n, bw, units), BF16),
+        pltpu.VMEM((3 * n * bw, units), BF16),
         pltpu.VMEM((n, bw, triple), BF16),
         pltpu.VMEM((n, bw, half_width), BF16),
         pltpu.VMEM((RING + 4, tok_rows, width // 2), BF16),
@@ -756,7 +826,7 @@
         dma((2 * n,)), dma((2 * n,)), dma((n,)), dma((2 * n,)),
         dma((n,)), dma((n,)), dma((n,)), dma((n,)),
         dma((n,)), dma((n,)), dma((n,)), dma((n,)),
-        dma((RING,)), dma((2, 14)), dma((2, 4)), dma((3,)), dma((width // 2 // CHUNK,)), dma((hops,)), dma((hops,)),
+        dma((RING,)), dma((2, 14)), dma((4,)), dma((2,)), dma((3,)), dma((width // 2 // CHUNK,)), dma((hops,)), dma((hops,)),
     ]
     return pl.pallas_call(
         functools.partial(block_kernel, n_zh),
@@ -820,7 +890,7 @@
             in_specs=[pl.BlockSpec(*parts_spec)] + [spec] * 3,
             out_specs=[spec] * 3,
         ),
-        compiler_params=pltpu.CompilerParams(vmem_limit_bytes=32 * 1024 * 1024),
+        compiler_params=pltpu.CompilerParams(vmem_limit_bytes=VMEM_LIMIT),
     )(zp, parts, *state)
 
 
@@ -846,7 +916,7 @@
         out_shape=[jax.ShapeDtypeStruct((rows, width), BF16), jax.ShapeDtypeStruct((rows, width), F32)],
         in_specs=[spec] * 4 + [pl.BlockSpec(outer_params.shape, lambda i: (0, 0))],
         out_specs=[spec] * 2,
-        compiler_params=pltpu.CompilerParams(vmem_limit_bytes=32 * 1024 * 1024),
+        compiler_params=pltpu.CompilerParams(vmem_limit_bytes=VMEM_LIMIT),
     )(tokens, cotangent, grad_normed, branch, outer_params)
 
 

time: 440 us -> 407 us (0.925)
  Pallas kernels: 408 us -> 390 us
  local copies, waits for them, and re-layouts: 25.7 us -> 10.9 us
    pallas_call x1, Pallas kernels: 391 us -> 359 us  [block(): pl.pallas_call(functools.partial(block_kernel, n_zh), out_shape=outs, in_...]
    unnamed x64 -> x26, local copies, waits for them, and re-layouts: 19.7 us -> 4.92 us
    pallas_call x4, Pallas kernels: 14.5 us -> 25.2 us  [adam(): pl.pallas_call(functools.partial(adam_kernel, rate, turned), out_shape=[s...]
where the time goes in v4:
time: 407 us; the launch traced here: 405 us
  Pallas kernels  390 us (96%)
  local copies, waits for them, and re-layouts  10.9 us (3%)
    pallas_call x1, Pallas kernels, block(): pl.pallas_call(functools.partial(block_kernel, n_zh), out_shape=outs, in_...  359 us
    pallas_call x4, Pallas kernels, adam(): pl.pallas_call(functools.partial(adam_kernel, rate, turned), out_shape=[s...  25.2 us

profile of v4, /device:TPU:0, one launch (start us, length us, event | category | flops | bytes accessed | tf_op | source)
XLA Modules:
  0.0 405.0 jit_solution(5185847324719254028)
XLA Ops:
  0.7 1.3 dynamic-slice_bitcast_fusion.1.hidden_bias
  1.9 0.7 dynamic-slice_bitcast_fusion
  2.6 0.6 copy.64
  3.2 1.1 convert_element_type.36
  4.3 0.8 copy.59
  5.1 1.7 copy.60
  6.8 0.1 copy.61
  6.9 1.2 copy.63.qkv_in
  8.0 0.0 copy-start
  8.0 1.9 copy.57
  9.9 1.3 copy.58
  11.3 0.0 copy-done
  11.3 0.1 convert_element_type.30
  11.4 1.3 copy.56
  12.7 359.1 %shard_map.416 = (bf16[2,4,256,1024]{3,2,1,0:T(8,128)(2,1)}, bf16[4,256,256]{2,1,0:T(8,128)(2,1)}, bf16[4,256,768]{2,1,0:T(8,128)(2,1)}, bf16[2,4,256,1024]{3,2,...) custom-call(bf16[256,2048]{1,0:T(8,128)(2,1)} %tok_ref.1, ...), custom_call_target="tpu_custom_call" | custom-call | tf_op jit(solution)/shard_map/pallas_call | solution.py:831
  371.8 0.0 copy-start.2
  371.8 0.0 copy-start.5
  371.8 0.0 copy-start.7
  371.8 0.0 copy-start.8
  371.9 0.0 copy-start.6
  371.9 0.0 copy-start.9
  371.9 0.0 copy-start.10
  371.9 0.0 copy-start.1
  371.9 0.0 copy-start.3
  371.9 0.0 copy-start.4
  371.9 5.8 %shard_map.417 = (bf16[256,2048]{1,0:T(8,128)(2,1)}, f32[256,2048]{1,0:T(8,128)}) custom-call(bf16[256,2048]{1,0:T(8,128)(2,1)} %tok_ref.1, bf16[256,2048]{1,0:T(8,128)(2,1)} %back_ref.1, f32[256,2048]{1,0:T(8,128)} %get-tuple-element.43.grad_ref, f32[256,2048]{1,0:T(8,128)} %get-tuple-element.44.branch_ref, f32[4,2048]{1,0:T(4,128)} %outer_ref.3), custom_call_target="tpu_custom_call" | custom-call | tf_op jit(solution)/shard_map/pallas_call | solution.py:913
  377.7 0.0 copy-done.2
  377.8 0.0 copy-done.5
  377.8 0.0 copy-done.7
  377.8 0.0 copy-done.8
  377.8 0.6 multiply_subtract_fusion.2
  378.5 0.0 copy-done.6
  378.5 0.0 copy-done.9
  378.5 0.0 copy-done.10
  378.5 0.6 multiply_subtract_fusion.1
  379.1 0.0 copy-done.1
  379.1 0.0 copy-done.3
  379.1 0.0 copy-done.4
  379.1 0.7 multiply_subtract_fusion
  379.8 2.7 shard_map.419
  382.5 6.7 %shard_map.418 = (f32[3,256,512]{2,1,0:T(8,128)}, f32[3,256,512]{2,1,0:T(8,128)}, f32[3,256,512]{2,1,0:T(8,128)}) custom-call(s32[1]{0:T(128)} %bitcast.12.zp_ref, bf16[2,2,256,768]{3,2,1,0:T(8,128)(2,1)} %bitcast.31, f32[3,256,512]{2,1,0:T(8,128)} %w_ref.4, f32[3,256,512]{2,1,0:T(8,128)} %one_ref.4, f32[3,256,512]{2,1,0:T(8,128)} %two_ref.4), custom_call_target="tpu_custom_call" | custom-call | tf_op jit(solution)/shard_map/pallas_call | solution.py:884
  389.2 8.9 %shard_map.421 = (f32[2048,256]{1,0:T(8,128)}, f32[2048,256]{1,0:T(8,128)}, f32[2048,256]{1,0:T(8,128)}) custom-call(s32[1]{0:T(128)} %bitcast.12.zp_ref, bf16[2,2,2,256,1024]{4,3,2,1,0:T(8,128)(2,1)} %bitcast.23, f32[2048,256]{1,0:T(8,128)} %w_ref.7, f32[2048,256]{1,0:T(8,128)} %one_ref.7, f32[2048,256]{1,0:T(8,128)} %two_ref.7), custom_call_target="tpu_custom_call" | custom-call | tf_op jit(solution)/shard_map/pallas_call | solution.py:884
  398.0 7.0 %shard_map.420 = (f32[256,2048]{1,0:T(8,128)}, f32[256,2048]{1,0:T(8,128)}, f32[256,2048]{1,0:T(8,128)}) custom-call(s32[1]{0:T(128)} %bitcast.12.zp_ref, bf16[2,2,2,256,1024]{4,3,2,1,0:T(8,128)(2,1)} %bitcast.24, f32[256,2048]{1,0:T(8,128)} %w_ref.6, f32[256,2048]{1,0:T(8,128)} %one_ref.6, f32[256,2048]{1,0:T(8,128)} %two_ref.6), custom_call_target="tpu_custom_call" | custom-call | tf_op jit(solution)/shard_map/pallas_call | solution.py:884
  (4 shorter events, 0.1 us)
Async XLA Ops:
  8.0 3.2 copy-start
  371.8 5.9 %copy-start.2 = (f32[8,2048]{1,0:T(8,128)S(1)}, f32[8,2048]{1,0:T(8,128)}, u32[]{:S(2)}) copy-start(f32[8,2048]{1,0:T(8,128)} %get-tuple-element.62) | copy-start | bytes 196612
  371.8 6.0 %copy-start.5 = (f32[3,512]{1,0:T(4,128)S(1)}, f32[3,512]{1,0:T(4,128)}, u32[]{:S(2)}) copy-start(f32[3,512]{1,0:T(4,128)} %param.39) | copy-start | bytes 18436
  371.8 6.0 %copy-start.7 = (f32[3,512]{1,0:T(4,128)S(1)}, f32[3,512]{1,0:T(4,128)}, u32[]{:S(2)}) copy-start(f32[3,512]{1,0:T(4,128)} %param.40) | copy-start | bytes 18436
  371.8 6.0 %copy-start.8 = (f32[3,512]{1,0:T(4,128)S(1)}, f32[3,512]{1,0:T(4,128)}, u32[]{:S(2)}) copy-start(f32[3,512]{1,0:T(4,128)} %param.41) | copy-start | bytes 18436
  371.9 6.6 %copy-start.6 = (f32[2048]{0:T(1024)S(1)}, f32[2048]{0:T(1024)}, u32[]{:S(2)}) copy-start(f32[2048]{0:T(1024)} %param.42) | copy-start | bytes 24580
  371.9 6.6 %copy-start.9 = (f32[2048]{0:T(1024)S(1)}, f32[2048]{0:T(1024)}, u32[]{:S(2)}) copy-start(f32[2048]{0:T(1024)} %param.43) | copy-start | bytes 24580
  371.9 6.6 %copy-start.10 = (f32[2048]{0:T(1024)S(1)}, f32[2048]{0:T(1024)}, u32[]{:S(2)}) copy-start(f32[2048]{0:T(1024)} %param.44) | copy-start | bytes 24580
  371.9 7.2 %copy-start.1 = (f32[4,2048]{1,0:T(4,128)S(1)}, f32[4,2048]{1,0:T(4,128)}, u32[]{:S(2)}) copy-start(f32[4,2048]{1,0:T(4,128)} %outer_ref.3) | copy-start | bytes 98308
  371.9 7.2 %copy-start.3 = (f32[4,2048]{1,0:T(4,128)S(1)}, f32[4,2048]{1,0:T(4,128)}, u32[]{:S(2)}) copy-start(f32[4,2048]{1,0:T(4,128)} %param.46) | copy-start | bytes 98308
  371.9 7.2 %copy-start.4 = (f32[4,2048]{1,0:T(4,128)S(1)}, f32[4,2048]{1,0:T(4,128)}, u32[]{:S(2)}) copy-start(f32[4,2048]{1,0:T(4,128)} %param.47) | copy-start | bytes 98308

commit v5 on v4

--- a/solution.py
+++ b/solution.py
@@ -29,22 +29,22 @@
 
 RUNS = (
     (
-        ("proj", 4), ("f1", 1), ("proj", 3), ("f1", 1), ("proj", 1), ("att", 1), ("f1", 1), ("att", 1),
-        ("f0", 2), ("att", 1), ("f0", 1), ("att", 1), ("a1", 1),
+        ("proj", 4), ("n1", 1), ("f1", 1), ("att", 1), ("n2", 1), ("proj", 2), ("f1", 1), ("proj", 2),
+        ("f1", 1), ("att", 1), ("f0", 1), ("att", 1), ("f0", 1), ("att", 1), ("f0", 1), ("a1", 1),
     ),
     (
-        ("act", 1), ("f0", 1), ("act", 4), ("ysET", 1), ("ysQKV", 1), ("act", 1), ("ysQKV", 1), ("a0", 1),
-        ("slope", 1), ("act", 1), ("slope", 2), ("zsQKV", 1), ("ysQKV", 1), ("act", 1), ("slope", 1),
-        ("zsQKV", 1), ("ysM", 1), ("slope", 1), ("ysET", 1), ("slope", 1), ("zsET", 1), ("zsQKV", 1),
-        ("slope", 1), ("ysM", 1), ("slope", 1), ("ysM", 1),
+        ("act", 1), ("f0", 1), ("act", 2), ("ysQKV", 1), ("act", 1), ("ysET", 1), ("ysQKV", 1), ("act", 3),
+        ("a0", 1), ("slope", 2), ("zsQKV", 1), ("act", 1), ("slope", 1), ("ysM", 1), ("slope", 2),
+        ("zsQKV", 1), ("slope", 1), ("zsET", 1), ("ysM", 1), ("slope", 2),
     ),
     (
-        ("zsM", 1), ("r0c", 1), ("zsET", 1), ("r0c", 3), ("zsM", 1), ("r0c", 4), ("r0x", 1), ("zsM", 1),
-        ("r0x", 1), ("ysET", 1), ("ysM", 1), ("r0x", 1), ("zsET", 1), ("r0x", 1), ("r0z", 1), ("r1c", 1),
-        ("ysM", 1), ("r1c", 2), ("r0z", 1), ("r1c", 1), ("ysM", 1), ("r1c", 1), ("zsM", 2), ("r1c", 3),
-        ("r1x", 1), ("zsM", 1), ("r1x", 2), ("ysM", 1), ("r0f", 1), ("r1x", 1), ("r1z", 1), ("ysET", 1),
-        ("ysM", 1), ("r0f", 1), ("r1z", 1), ("zsET", 1), ("vec", 1), ("zsM", 1), ("vec", 3), ("ysQKV", 1),
-        ("vec", 1), ("zsM", 1), ("r1f", 1), ("vec", 1), ("r1f", 1), ("zsQKV", 1),
+        ("zsM", 1), ("ysET", 1), ("ysQKV", 1), ("ysM", 1), ("ysET", 1), ("zsM", 1), ("r0c", 5),
+        ("zsQKV", 1), ("r0c", 2), ("zsET", 1), ("r0c", 1), ("r0x", 1), ("zsET", 1), ("zsM", 1), ("ysM", 1),
+        ("r0x", 3), ("r0z", 1), ("r1c", 1), ("ysM", 2), ("r1c", 1), ("r0z", 1), ("zsM", 1), ("r1c", 3),
+        ("zsM", 1), ("r1c", 3), ("r1x", 1), ("zsM", 1), ("r1x", 1), ("r0f", 1), ("ysM", 1), ("r1x", 2),
+        ("r1z", 1), ("r0f", 1), ("vec", 1), ("ysM", 1), ("vec", 1), ("r1z", 1), ("zsM", 1), ("ysET", 1),
+        ("ysQKV", 1), ("vec", 3), ("zsET", 1), ("r1f", 1), ("zsM", 1), ("zsQKV", 1), ("r1f", 1),
+        ("vec", 1),
     ),
 )
 ORDER = [[name for name, times in part for _ in range(times)] for part in RUNS]
@@ -255,12 +255,12 @@
     forward_pieces(3, 0, pieces[3])
     pass_on(0, 1, 1)
     forward_pieces(2, 0, pieces[2])
-    pass_on(1, 1, 1)
     forward_pieces(1, 0, pieces[1] // 4)
+    started.append(act_copy(1, 2, 3))
     for copy in locals_():
         copy.wait()
     for k in (0, 1):
-        for part in range(4):
+        for part in (0, 2):
             act_copy(k, 2, part).wait_recv()
     y_arrived(3)
     y_arrived(2)
@@ -316,7 +316,7 @@
         return values * cos_ref[rows, :] + jnp.where(low_lane, after, before) * (sign * sin_ref[rows, :])
 
     def proj_tile(r, carry):
-        rows = at(r, CHUNK)
+        rows = at((lax.div(r, count) ^ zp) * count + lax.rem(r, count), CHUNK)
         where = at(lax.rem(r, count), CHUNK)
         for t in range(3):
             cols = pl.ds(t * half_width, half_width)
@@ -334,7 +334,7 @@
     pairs = half_width // lanes
 
     def attend(it, carry):
-        base = lax.div(it, pairs) * count
+        base = (lax.div(it, pairs) ^ zp) * count
         hp = lax.rem(it, pairs)
 
         def cols(t):
@@ -692,7 +692,18 @@
                 for hop in range(k, len(hops) if k == 4 else k + 1):
                     vec_next(hop)
 
+    def pass_last(q):
+        act_copy(1, 1, 1).wait_recv()
+        act_copy(1, 2, 3).start()
+
+    def rows_arrived(q):
+        for k in (0, 1):
+            for part in (1, 3):
+                act_copy(k, 2, part).wait_recv()
+
     tasks = {
+        "n1": pass_last,
+        "n2": rows_arrived,
         "f1": pieces_of(1),
         "f0": pieces_of(0),
         "a1": lambda q: y_arrived(1),
@@ -908,7 +919,7 @@
 
 def finish(tokens, cotangent, grad_normed, branch, outer_params):
     rows, width = tokens.shape
-    tile = 64
+    tile = 32
     spec = pl.BlockSpec((tile, width), lambda i: (i, 0))
     return pl.pallas_call(
         finish_kernel,
@@ -962,7 +973,7 @@
     z_mlp = z_mlp.reshape(2, n_zh, 2, bw, half_units)
     z_dense = z_dense.reshape(n_zh, 2, bw, half_width)
     z_qkv = z_qkv.reshape(n_zh, 2, bw, 3 * half_width)
-    tile = min(bw, 128)
+    tile = min(bw, 32)
     new_up = adam(
         zp_array, z_mlp, (up_weight, up_first, up_second), width ** (-0.5), False,
         (2, bw // tile),

time: 407 us -> 427 us (1.049)
  the two profiles are of different devices: /device:TPU:0 before, /device:TPU:23 now
where the time goes in v5:
time: 427 us; the launch traced here: 425 us
  Pallas kernels  410 us (96%)
  local copies, waits for them, and re-layouts  10.9 us (3%)
    pallas_call x1, Pallas kernels, block(): pl.pallas_call(functools.partial(block_kernel, n_zh), out_shape=outs, in_...  372 us
    pallas_call x4, Pallas kernels, adam(): pl.pallas_call(functools.partial(adam_kernel, rate, turned), out_shape=[s...  30 us

profile of v5, /device:TPU:23, one launch (start us, length us, event | category | flops | bytes accessed | tf_op | source)
XLA Modules:
  0.0 424.5 jit_solution(12914203524764835985)
XLA Ops:
  0.7 1.3 dynamic-slice_bitcast_fusion.1.hidden_bias
  1.9 0.7 dynamic-slice_bitcast_fusion
  2.6 0.6 copy.64
  3.2 1.1 convert_element_type.36
  4.3 0.8 copy.59
  5.1 1.7 copy.60
  6.8 0.1 copy.61
  6.9 1.2 copy.63.qkv_in
  8.0 0.0 copy-start
  8.0 1.9 copy.57
  9.9 1.3 copy.58
  11.3 0.0 copy-done
  11.3 0.1 convert_element_type.30
  11.4 1.3 copy.56
  12.7 371.7 %shard_map.416 = (bf16[2,4,256,1024]{3,2,1,0:T(8,128)(2,1)}, bf16[4,256,256]{2,1,0:T(8,128)(2,1)}, bf16[4,256,768]{2,1,0:T(8,128)(2,1)}, bf16[2,4,256,1024]{3,2,...) custom-call(bf16[256,2048]{1,0:T(8,128)(2,1)} %tok_ref.1, ...), custom_call_target="tpu_custom_call" | custom-call | tf_op jit(solution)/shard_map/pallas_call | solution.py:842
  384.4 0.0 copy-start.2
  384.4 0.0 copy-start.5
  384.4 0.0 copy-start.7
  384.4 0.0 copy-start.8
  384.4 0.0 copy-start.6
  384.4 0.0 copy-start.9
  384.4 0.0 copy-start.10
  384.4 0.0 copy-start.1
  384.5 0.0 copy-start.3
  384.5 0.0 copy-start.4
  384.5 7.9 %shard_map.417 = (bf16[256,2048]{1,0:T(8,128)(2,1)}, f32[256,2048]{1,0:T(8,128)}) custom-call(bf16[256,2048]{1,0:T(8,128)(2,1)} %tok_ref.1, bf16[256,2048]{1,0:T(8,128)(2,1)} %back_ref.1, f32[256,2048]{1,0:T(8,128)} %get-tuple-element.43.grad_ref, f32[256,2048]{1,0:T(8,128)} %get-tuple-element.44.branch_ref, f32[4,2048]{1,0:T(4,128)} %outer_ref.3), custom_call_target="tpu_custom_call" | custom-call | tf_op jit(solution)/shard_map/pallas_call | solution.py:924
  392.4 0.0 copy-done.2
  392.5 0.0 copy-done.5
  392.5 0.0 copy-done.7
  392.5 0.0 copy-done.8
  392.5 0.6 multiply_subtract_fusion.2
  393.1 0.0 copy-done.6
  393.2 0.0 copy-done.9
  393.2 0.0 copy-done.10
  393.2 0.6 multiply_subtract_fusion.1
  393.8 0.0 copy-done.1
  393.8 0.0 copy-done.3
  393.8 0.0 copy-done.4
  393.8 0.7 multiply_subtract_fusion
  394.5 2.7 shard_map.419
  397.2 6.7 %shard_map.418 = (f32[3,256,512]{2,1,0:T(8,128)}, f32[3,256,512]{2,1,0:T(8,128)}, f32[3,256,512]{2,1,0:T(8,128)}) custom-call(s32[1]{0:T(128)} %bitcast.12.zp_ref, bf16[2,2,256,768]{3,2,1,0:T(8,128)(2,1)} %bitcast.31, f32[3,256,512]{2,1,0:T(8,128)} %w_ref.4, f32[3,256,512]{2,1,0:T(8,128)} %one_ref.4, f32[3,256,512]{2,1,0:T(8,128)} %two_ref.4), custom_call_target="tpu_custom_call" | custom-call | tf_op jit(solution)/shard_map/pallas_call | solution.py:895
  403.8 8.9 %shard_map.421 = (f32[2048,256]{1,0:T(8,128)}, f32[2048,256]{1,0:T(8,128)}, f32[2048,256]{1,0:T(8,128)}) custom-call(s32[1]{0:T(128)} %bitcast.12.zp_ref, bf16[2,2,2,256,1024]{4,3,2,1,0:T(8,128)(2,1)} %bitcast.23, f32[2048,256]{1,0:T(8,128)} %w_ref.7, f32[2048,256]{1,0:T(8,128)} %one_ref.7, f32[2048,256]{1,0:T(8,128)} %two_ref.7), custom_call_target="tpu_custom_call" | custom-call | tf_op jit(solution)/shard_map/pallas_call | solution.py:895
  412.7 11.8 %shard_map.420 = (f32[256,2048]{1,0:T(8,128)}, f32[256,2048]{1,0:T(8,128)}, f32[256,2048]{1,0:T(8,128)}) custom-call(s32[1]{0:T(128)} %bitcast.12.zp_ref, bf16[2,2,2,256,1024]{4,3,2,1,0:T(8,128)(2,1)} %bitcast.24, f32[256,2048]{1,0:T(8,128)} %w_ref.6, f32[256,2048]{1,0:T(8,128)} %one_ref.6, f32[256,2048]{1,0:T(8,128)} %two_ref.6), custom_call_target="tpu_custom_call" | custom-call | tf_op jit(solution)/shard_map/pallas_call | solution.py:895
  (4 shorter events, 0.1 us)
Async XLA Ops:
  8.0 3.2 copy-start
  384.4 8.0 %copy-start.2 = (f32[8,2048]{1,0:T(8,128)S(1)}, f32[8,2048]{1,0:T(8,128)}, u32[]{:S(2)}) copy-start(f32[8,2048]{1,0:T(8,128)} %get-tuple-element.62) | copy-start | bytes 196612
  384.4 8.1 %copy-start.5 = (f32[3,512]{1,0:T(4,128)S(1)}, f32[3,512]{1,0:T(4,128)}, u32[]{:S(2)}) copy-start(f32[3,512]{1,0:T(4,128)} %param.39) | copy-start | bytes 18436
  384.4 8.1 %copy-start.7 = (f32[3,512]{1,0:T(4,128)S(1)}, f32[3,512]{1,0:T(4,128)}, u32[]{:S(2)}) copy-start(f32[3,512]{1,0:T(4,128)} %param.40) | copy-start | bytes 18436
  384.4 8.1 %copy-start.8 = (f32[3,512]{1,0:T(4,128)S(1)}, f32[3,512]{1,0:T(4,128)}, u32[]{:S(2)}) copy-start(f32[3,512]{1,0:T(4,128)} %param.41) | copy-start | bytes 18436
  384.4 8.7 %copy-start.6 = (f32[2048]{0:T(1024)S(1)}, f32[2048]{0:T(1024)}, u32[]{:S(2)}) copy-start(f32[2048]{0:T(1024)} %param.42) | copy-start | bytes 24580
  384.4 8.7 %copy-start.9 = (f32[2048]{0:T(1024)S(1)}, f32[2048]{0:T(1024)}, u32[]{:S(2)}) copy-start(f32[2048]{0:T(1024)} %param.43) | copy-start | bytes 24580
  384.4 8.7 %copy-start.10 = (f32[2048]{0:T(1024)S(1)}, f32[2048]{0:T(1024)}, u32[]{:S(2)}) copy-start(f32[2048]{0:T(1024)} %param.44) | copy-start | bytes 24580
  384.4 9.4 %copy-start.1 = (f32[4,2048]{1,0:T(4,128)S(1)}, f32[4,2048]{1,0:T(4,128)}, u32[]{:S(2)}) copy-start(f32[4,2048]{1,0:T(4,128)} %outer_ref.3) | copy-start | bytes 98308
  384.5 9.3 %copy-start.3 = (f32[4,2048]{1,0:T(4,128)S(1)}, f32[4,2048]{1,0:T(4,128)}, u32[]{:S(2)}) copy-start(f32[4,2048]{1,0:T(4,128)} %param.46) | copy-start | bytes 98308
  384.5 9.3 %copy-start.4 = (f32[4,2048]{1,0:T(4,128)S(1)}, f32[4,2048]{1,0:T(4,128)}, u32[]{:S(2)}) copy-start(f32[4,2048]{1,0:T(4,128)} %param.47) | copy-start | bytes 98308

commit v6 on v4

--- a/solution.py
+++ b/solution.py
@@ -908,7 +908,7 @@
 
 def finish(tokens, cotangent, grad_normed, branch, outer_params):
     rows, width = tokens.shape
-    tile = 64
+    tile = rows // 2
     spec = pl.BlockSpec((tile, width), lambda i: (i, 0))
     return pl.pallas_call(
         finish_kernel,
@@ -962,7 +962,7 @@
     z_mlp = z_mlp.reshape(2, n_zh, 2, bw, half_units)
     z_dense = z_dense.reshape(n_zh, 2, bw, half_width)
     z_qkv = z_qkv.reshape(n_zh, 2, bw, 3 * half_width)
-    tile = min(bw, 128)
+    tile = bw
     new_up = adam(
         zp_array, z_mlp, (up_weight, up_first, up_second), width ** (-0.5), False,
         (2, bw // tile),
@@ -971,9 +971,9 @@
     )
     new_down = adam(
         zp_array, z_mlp, (down_weight, down_first, down_second), (4 * width) ** (-0.5), True,
-        (2, half_units // CHUNK),
-        ((1, n_zh, 1, bw, CHUNK), lambda h, r, zp_: (0, 0, 1 - (h ^ zp_[0]), 0, r)),
-        ((CHUNK, bw), lambda h, r, zp_: (h * (half_units // CHUNK) + r, 0)),
+        (2, half_units // (2 * CHUNK)),
+        ((1, n_zh, 1, bw, 2 * CHUNK), lambda h, r, zp_: (0, 0, 1 - (h ^ zp_[0]), 0, r)),
+        ((2 * CHUNK, bw), lambda h, r, zp_: (h * (half_units // (2 * CHUNK)) + r, 0)),
     )
     new_dense = adam(
         zp_array, z_dense, (dense_weight, dense_first, dense_second), (width // 16) ** (-0.5), True,

time: 407 us -> 403 us (level)
  no operation moved by 1% of the time
where the time goes in v6:
time: 403 us; the launch traced here: 402 us
  Pallas kernels  387 us (96%)
  local copies, waits for them, and re-layouts  10.9 us (3%)
    pallas_call x1, Pallas kernels, block(): pl.pallas_call(functools.partial(block_kernel, n_zh), out_shape=outs, in_...  359 us
    pallas_call x4, Pallas kernels, adam(): pl.pallas_call(functools.partial(adam_kernel, rate, turned), out_shape=[s...  22.3 us

profile of v6, /device:TPU:0, one launch (start us, length us, event | category | flops | bytes accessed | tf_op | source)
XLA Modules:
  0.0 401.6 jit_solution(7998080902715955828)
XLA Ops:
  0.7 1.3 dynamic-slice_bitcast_fusion.1.hidden_bias
  1.9 0.7 dynamic-slice_bitcast_fusion
  2.6 0.6 copy.64
  3.2 1.1 convert_element_type.36
  4.3 0.8 copy.59
  5.1 1.7 copy.60
  6.8 0.1 copy.61
  6.9 1.2 copy.63.qkv_in
  8.0 0.0 copy-start
  8.0 1.9 copy.57
  9.9 1.3 copy.58
  11.3 0.0 copy-done
  11.3 0.1 convert_element_type.30
  11.4 1.3 copy.56
  12.7 359.1 %shard_map.416 = (bf16[2,4,256,1024]{3,2,1,0:T(8,128)(2,1)}, bf16[4,256,256]{2,1,0:T(8,128)(2,1)}, bf16[4,256,768]{2,1,0:T(8,128)(2,1)}, bf16[2,4,256,1024]{3,2,...) custom-call(bf16[256,2048]{1,0:T(8,128)(2,1)} %tok_ref.1, ...), custom_call_target="tpu_custom_call" | custom-call | tf_op jit(solution)/shard_map/pallas_call | solution.py:831
  371.8 0.0 copy-start.2
  371.8 0.0 copy-start.5
  371.8 0.0 copy-start.7
  371.8 0.0 copy-start.8
  371.9 0.0 copy-start.6
  371.9 0.0 copy-start.9
  371.9 0.0 copy-start.10
  371.9 0.0 copy-start.1
  371.9 0.0 copy-start.3
  371.9 0.0 copy-start.4
  371.9 5.3 %shard_map.417 = (bf16[256,2048]{1,0:T(8,128)(2,1)}, f32[256,2048]{1,0:T(8,128)}) custom-call(bf16[256,2048]{1,0:T(8,128)(2,1)} %tok_ref.1, bf16[256,2048]{1,0:T(8,128)(2,1)} %back_ref.1, f32[256,2048]{1,0:T(8,128)} %get-tuple-element.43.grad_ref, f32[256,2048]{1,0:T(8,128)} %get-tuple-element.44.branch_ref, f32[4,2048]{1,0:T(4,128)} %outer_ref.3), custom_call_target="tpu_custom_call" | custom-call | tf_op jit(solution)/shard_map/pallas_call | solution.py:913
  377.3 0.0 copy-done.2
  377.3 0.0 copy-done.5
  377.3 0.0 copy-done.7
  377.3 0.0 copy-done.8
  377.3 0.6 multiply_subtract_fusion.2
  378.0 0.0 copy-done.6
  378.0 0.0 copy-done.9
  378.0 0.0 copy-done.10
  378.0 0.6 multiply_subtract_fusion.1
  378.6 0.0 copy-done.1
  378.7 0.0 copy-done.3
  378.7 0.0 copy-done.4
  378.7 0.7 multiply_subtract_fusion
  379.4 2.7 shard_map.419
  382.0 6.7 %shard_map.418 = (f32[3,256,512]{2,1,0:T(8,128)}, f32[3,256,512]{2,1,0:T(8,128)}, f32[3,256,512]{2,1,0:T(8,128)}) custom-call(s32[1]{0:T(128)} %bitcast.12.zp_ref, bf16[2,2,256,768]{3,2,1,0:T(8,128)(2,1)} %bitcast.31, f32[3,256,512]{2,1,0:T(8,128)} %w_ref.4, f32[3,256,512]{2,1,0:T(8,128)} %one_ref.4, f32[3,256,512]{2,1,0:T(8,128)} %two_ref.4), custom_call_target="tpu_custom_call" | custom-call | tf_op jit(solution)/shard_map/pallas_call | solution.py:884
  388.7 7.0 %shard_map.421 = (f32[2048,256]{1,0:T(8,128)}, f32[2048,256]{1,0:T(8,128)}, f32[2048,256]{1,0:T(8,128)}) custom-call(s32[1]{0:T(128)} %bitcast.12.zp_ref, bf16[2,2,2,256,1024]{4,3,2,1,0:T(8,128)(2,1)} %bitcast.23, f32[2048,256]{1,0:T(8,128)} %w_ref.7, f32[2048,256]{1,0:T(8,128)} %one_ref.7, f32[2048,256]{1,0:T(8,128)} %two_ref.7), custom_call_target="tpu_custom_call" | custom-call | tf_op jit(solution)/shard_map/pallas_call | solution.py:884
  395.7 5.9 %shard_map.420 = (f32[256,2048]{1,0:T(8,128)}, f32[256,2048]{1,0:T(8,128)}, f32[256,2048]{1,0:T(8,128)}) custom-call(s32[1]{0:T(128)} %bitcast.12.zp_ref, bf16[2,2,2,256,1024]{4,3,2,1,0:T(8,128)(2,1)} %bitcast.24, f32[256,2048]{1,0:T(8,128)} %w_ref.6, f32[256,2048]{1,0:T(8,128)} %one_ref.6, f32[256,2048]{1,0:T(8,128)} %two_ref.6), custom_call_target="tpu_custom_call" | custom-call | tf_op jit(solution)/shard_map/pallas_call | solution.py:884
  (4 shorter events, 0.1 us)
Async XLA Ops:
  8.0 3.2 copy-start
  371.8 5.5 %copy-start.2 = (f32[8,2048]{1,0:T(8,128)S(1)}, f32[8,2048]{1,0:T(8,128)}, u32[]{:S(2)}) copy-start(f32[8,2048]{1,0:T(8,128)} %get-tuple-element.62) | copy-start | bytes 196612
  371.8 5.5 %copy-start.5 = (f32[3,512]{1,0:T(4,128)S(1)}, f32[3,512]{1,0:T(4,128)}, u32[]{:S(2)}) copy-start(f32[3,512]{1,0:T(4,128)} %param.39) | copy-start | bytes 18436
  371.8 5.5 %copy-start.7 = (f32[3,512]{1,0:T(4,128)S(1)}, f32[3,512]{1,0:T(4,128)}, u32[]{:S(2)}) copy-start(f32[3,512]{1,0:T(4,128)} %param.40) | copy-start | bytes 18436
  371.8 5.5 %copy-start.8 = (f32[3,512]{1,0:T(4,128)S(1)}, f32[3,512]{1,0:T(4,128)}, u32[]{:S(2)}) copy-start(f32[3,512]{1,0:T(4,128)} %param.41) | copy-start | bytes 18436
  371.9 6.1 %copy-start.6 = (f32[2048]{0:T(1024)S(1)}, f32[2048]{0:T(1024)}, u32[]{:S(2)}) copy-start(f32[2048]{0:T(1024)} %param.42) | copy-start | bytes 24580
  371.9 6.1 %copy-start.9 = (f32[2048]{0:T(1024)S(1)}, f32[2048]{0:T(1024)}, u32[]{:S(2)}) copy-start(f32[2048]{0:T(1024)} %param.43) | copy-start | bytes 24580
  371.9 6.1 %copy-start.10 = (f32[2048]{0:T(1024)S(1)}, f32[2048]{0:T(1024)}, u32[]{:S(2)}) copy-start(f32[2048]{0:T(1024)} %param.44) | copy-start | bytes 24580
  371.9 6.8 %copy-start.1 = (f32[4,2048]{1,0:T(4,128)S(1)}, f32[4,2048]{1,0:T(4,128)}, u32[]{:S(2)}) copy-start(f32[4,2048]{1,0:T(4,128)} %outer_ref.3) | copy-start | bytes 98308
  371.9 6.8 %copy-start.3 = (f32[4,2048]{1,0:T(4,128)S(1)}, f32[4,2048]{1,0:T(4,128)}, u32[]{:S(2)}) copy-start(f32[4,2048]{1,0:T(4,128)} %param.46) | copy-start | bytes 98308
  371.9 6.7 %copy-start.4 = (f32[4,2048]{1,0:T(4,128)S(1)}, f32[4,2048]{1,0:T(4,128)}, u32[]{:S(2)}) copy-start(f32[4,2048]{1,0:T(4,128)} %param.47) | copy-start | bytes 98308
